TPU v7x, 32 devices: a whole 2x2x4 slice. The times are simulated.
32 devices in a mesh: row: 4 (over y, x), col: 4 (over z), depth: 2 (over core).
Axes of the slice: x: 2, y: 2, z: 4, core: 2. Of those that a mesh axis runs over, the one named last changes fastest.
Arguments:
- amplitude: float32 [100, 512, 512], P('row', 'depth', 'col'), may hold values from -6 to 6
- integral: float32 [512, 100, 2048], P('depth', None, 'col'), may hold values from -0.02734375 to 0.02734375
Outputs:
- cycle_term: float32 [512, 2048], P(('row', 'depth'), 'col')
All inputs are finite; a program needn't handle non-finite values.
Results may differ from a plain program's by a relative error of at most 0.00011.
Values sent between devices are 32-bit elements; how exact they have to be, the bound alone decides.
No kernel may reach another device: no remote copies, remote signals or barrier semaphores. Data moves between devices by JAX's collectives and lax.ppermute only.
A program may use at most 128 MiB of HBM per device.

v0:
```python
import jax
import jax.numpy as jnp
from jax import lax
from jax.sharding import PartitionSpec as P


def shards(amplitude, integral):
    remapped = lax.all_to_all(
        lax.all_to_all(amplitude, "col", split_axis=1, concat_axis=2, tiled=True),
        "row",
        split_axis=2,
        concat_axis=0,
        tiled=True,
    )
    product = jnp.einsum(
        "kcm,ckn->mn",
        lax.all_gather(remapped, "col", axis=1, tiled=True),
        integral,
        precision=lax.Precision.HIGHEST,
        preferred_element_type=jnp.float32,
    )
    return lax.psum_scatter(product, "depth", scatter_dimension=0, tiled=True)


def solution(mesh):
    return jax.shard_map(
        shards,
        mesh=mesh,
        in_specs=(P("row", "depth", "col"), P("depth", None, "col")),
        out_specs=P(("row", "depth"), "col"),
        check_vma=False,
    )
```

profile of v0, /device:TPU:0, one launch (start us, length us, event | category | flops | bytes accessed | tf_op | source)
XLA Modules:
  0.0 484.6 jit_solution(14871730839207396393)
XLA Ops:
  6.5 0.0 all-gather.2.cloned.1.call-start
  6.5 3.9 copy.5
  10.4 99.3 %all_to_all.36 = f32[25,256,128]{2,0,1:T(8,128)S(1)} all-to-all(f32[25,256,128]{2,0,1:T(8,128)S(1)} %copy.5), channel_id=1, replica_groups=mesh['row'=4,'col'=4,'depth'=2] {'col'}, dimensions={1} | all-to-all | bytes 6553600 | tf_op jit(solution)/shard_map/all_to_all | solution.py:9
  109.7 2.1 copy.13
  111.8 5.4 %copy.10 = f32[25,64,4,128]{1,0,3,2:T(8,128)} copy(f32[25,64,4,128]{3,2,1,0:T(4,128)S(1)} %bitcast.17) | data formatting | bytes 6553600 | tf_op jit(solution)/shard_map/all_to_all | solution.py:9
  117.2 6.4 %reshape.1 = f32[4,1,204800]{2,1,0:T(1,128)S(1)} reshape(f32[512,25,64]{2,1,0:T(8,128)} %bitcast.14) | data formatting | bytes 6553600
  123.6 40.5 %all_to_all.37 = f32[4,1,204800]{2,1,0:T(1,128)} all-to-all(f32[4,1,204800]{2,1,0:T(1,128)S(1)} %reshape.1), channel_id=1, replica_groups=mesh['row'=4,'col'=4,'depth'=2] {'row'}, dimensions={0} | all-to-all | bytes 6553600 | tf_op jit(solution)/shard_map/all_to_all | solution.py:8
  164.1 0.5 broadcast
  164.7 28.7 %reduce = f32[4,204800]{1,0:T(4,128)S(1)} reduce(f32[4,1,204800]{2,1,0:T(1,128)} %all_to_all.37, f32[]{:T(128)} %broadcast), dimensions={1}, to_apply=%all_to_all.30.reduce_sub_computation | reduce | bytes 6553604 | tf_op jit(solution)/shard_map/all_to_all | solution.py:8
  193.3 7.4 %reshape.2 = f32[512,25,64]{2,1,0:T(8,128)} reshape(f32[4,204800]{1,0:T(4,128)S(1)} %reduce) | data formatting | bytes 6553600
  200.7 5.6 %copy.11 = f32[25,64,4,128]{3,2,1,0:T(4,128)S(1)} copy(f32[25,64,4,128]{1,0,3,2:T(8,128)} %bitcast.15) | data formatting | bytes 6553600 | tf_op jit(solution)/shard_map/all_to_all | solution.py:8
  206.3 2.1 copy.9
  208.5 0.0 all-gather.2.cloned.1.call-update
  208.5 0.3 reduce-scatter.2.cloned.1.call-start
  208.8 225.2 %all-gather.2.cloned.1.call-done = f32[100,256,128]{2,1,0:T(8,128)} async-done(((f32[100,64,128]{2,1,0:T(8,128)}), f32[100,256,128]{2,1,0:T(8,128)}) %all-gather.2.cloned.1.call-update) | async-done | bytes 13107216 | tf_op jit(solution)/shard_map/all_gather | solution.py:17
  433.9 37.8 %convolution_bitcast_fusion = f32[128,512]{1,0:T(8,128)} fusion(f32[100,256,128]{2,1,0:T(8,128)} %all-gather.2.cloned.1.call-done, f32[256,100,512]{2,0,1:T(8,128)} %param.3), kind=kOutput, calls=%fused_computation.1 | convolution fusion | flops 20132659200 | bytes 65798144 | tf_op jit(solution)/shard_map/kcm,ckn->mn/dot_general | solution.py:15
  471.8 0.0 reduce-scatter.2.cloned.1.call-update
  471.8 6.0 %reduce-scatter.2.cloned.1.call-done = f32[64,512]{1,0:T(8,128)} async-done(((f32[128,512]{1,0:T(8,128)}), f32[64,512]{1,0:T(8,128)}) %reduce-scatter.2.cloned.1.call-update) | async-done | bytes 131088 | tf_op jit(solution)/shard_map/reduce_scatter | solution.py:22
Async XLA Ops:
  6.5 427.4 %all-gather.2.cloned.1.call-start = ((), (), s32[]{:S(2)}) async-start(), calls=%async_computation.3 | async-start | bytes 16384000 | tf_op jit(solution)/shard_map/all_gather | solution.py:17
  208.5 269.3 %reduce-scatter.2.cloned.1.call-start = ((), (), s32[]{:S(2)}) async-start(), calls=%async_computation.4 | async-start | bytes 393216 | tf_op jit(solution)/shard_map/reduce_scatter | solution.py:22
Sparse Core Ops, SparseCore 0:
  208.6 225.2 all-gather.1
  471.9 5.8 reduce-scatter.1
where the time goes:
time: 485 us
  waiting for transfers between devices  231 us (48%)
  blocking collectives  140 us (29%)
  matrix products  37.8 us (8%)
  local copies, waits for them, and re-layouts  33.5 us (7%)
  other arithmetic  28.7 us (6%)
  between operations  13.4 us (3%)
    all_gather x1, waiting for transfers between devices, shards(): lax.all_gather(remapped, 'col', axis=1, tiled=True)  225 us
    all_to_all x1, blocking collectives, shards(): lax.all_to_all(amplitude, 'col', split_axis=1, concat_axis=2, tiled=True)  99.3 us
    all_to_all x1, blocking collectives, shards(): lax.all_to_all(lax.all_to_all(amplitude, 'col', split_axis=1, concat_axis...  40.5 us
    dot_general x1, matrix products, shards(): jnp.einsum('kcm,ckn->mn', lax.all_gather(remapped, 'col', axis=1, tiled=T...  37.8 us
    all_to_all x1, other arithmetic, shards(): lax.all_to_all(lax.all_to_all(amplitude, 'col', split_axis=1, concat_axis...  28.7 us
    unnamed x3, local copies, waits for them, and re-layouts  17.7 us
  transfers between devices with their start and end apart: 2, of which 2 were waited for; matrix products, arithmetic and copies ran while one was open for 0% of the time, Pallas kernels for 0%

commit v1 on v0

v1 whole, which is shorter than its diff:
```python
import jax
import jax.numpy as jnp
from jax import lax
from jax.sharding import PartitionSpec as P


def shards(amplitude, integral):
    ko = amplitude.shape[0]
    own = lax.dynamic_slice_in_dim(integral, lax.axis_index("row") * ko, ko, axis=1)
    product = jnp.einsum(
        "kcm,ckn->mn",
        lax.all_gather(amplitude, "col", axis=2, tiled=True),
        own,
        precision=lax.Precision.HIGH,
        preferred_element_type=jnp.float32,
    )
    return lax.psum_scatter(product, ("row", "depth"), scatter_dimension=0, tiled=True)


def solution(mesh):
    return jax.shard_map(
        shards,
        mesh=mesh,
        in_specs=(P("row", "depth", "col"), P("depth", None, "col")),
        out_specs=P(("row", "depth"), "col"),
        check_vma=False,
    )
```

time: 485 us -> 296 us (0.61)
  blocking collectives: 140 us -> 0 us
  waiting for transfers between devices: 231 us -> 266 us
  local copies, waits for them, and re-layouts: 33.5 us -> 1.3 us
  other arithmetic: 28.7 us -> 0 us
  matrix products: 37.8 us -> 15.8 us
    all_to_all x2 -> x0, blocking collectives: 140 us -> none  [the longest x1 99.3 us: shards(): lax.all_to_all(amplitude, 'col', split_axis=1, concat_axis=2, tiled=True)]
    all_to_all x1 -> x0, other arithmetic: 28.7 us -> none  [shards(): lax.all_to_all(lax.all_to_all(amplitude, 'col', split_axis=1, concat_axis...]
    reduce_scatter x1, waiting for transfers between devices: 6.02 us -> 34.4 us  [shards(): lax.psum_scatter(product, ('row', 'depth'), scatter_dimension=0, tiled=True)]
    dot_general x1, matrix products: 37.8 us -> 15.8 us  [shards(): jnp.einsum('kcm,ckn->mn', lax.all_gather(amplitude, 'col', axis=2, tiled=...]
    unnamed x3 -> x1, local copies, waits for them, and re-layouts: 17.7 us -> 1.3 us
    all_to_all x5 -> x0, local copies, waits for them, and re-layouts: 15.8 us -> none  [the longest x3 8.27 us: shards(): lax.all_to_all(lax.all_to_all(amplitude, 'col', split_axis=1, concat_axis...]
    all_gather x1, waiting for transfers between devices: 225 us -> 231 us  [shards(): lax.all_gather(amplitude, 'col', axis=2, tiled=True)]
where the time goes in v1:
time: 296 us
  waiting for transfers between devices  266 us (90%)
  matrix products  15.8 us (5%)
  between operations  13.4 us (5%)
    all_gather x1, waiting for transfers between devices, shards(): lax.all_gather(amplitude, 'col', axis=2, tiled=True)  231 us
    reduce_scatter x1, waiting for transfers between devices, shards(): lax.psum_scatter(product, ('row', 'depth'), scatter_dimension=0, tiled=True)  34.4 us
    dot_general x1, matrix products, shards(): jnp.einsum('kcm,ckn->mn', lax.all_gather(amplitude, 'col', axis=2, tiled=...  15.8 us
  transfers between devices with their start and end apart: 2, of which 2 were waited for; matrix products, arithmetic and copies ran while one was open for 0% of the time, Pallas kernels for 0%

profile of v1, /device:TPU:0, one launch (start us, length us, event | category | flops | bytes accessed | tf_op | source)
XLA Modules:
  0.0 296.2 jit_solution(2737144833466362861)
XLA Ops:
  6.5 0.0 all-gather.2.cloned.1.call-start
  6.5 0.7 all-gather.2.cloned.1.call-update
  7.3 0.0 reduce-scatter.4.cloned.1.call-start
  7.3 230.6 %all-gather.2.cloned.1.call-done = f32[25,256,512]{2,1,0:T(8,128)} async-done(((f32[25,256,128]{2,1,0:T(8,128)}), f32[25,256,512]{2,1,0:T(8,128)}) %all-gather.2.cloned.1.call-update) | async-done | bytes 13107216 | tf_op jit(solution)/shard_map/all_gather | solution.py:12
  237.9 15.8 %fusion.2 = f32[512,512]{0,1:T(8,128)S(1)} fusion(f32[25,256,512]{2,1,0:T(8,128)} %all-gather.2.cloned.1.call-done, f32[256,100,512]{2,0,1:T(8,128)} %param.3, s32[]{:T(128)S(6)} %select_n.3), kind=kOutput, calls=%fused_computation.2 | convolution fusion | flops 10066329600 | bytes 27262980 | tf_op jit(solution)/shard_map/kcm,ckn->mn/dot_general | solution.py:10
  253.7 1.3 copy.7
  255.0 0.0 reduce-scatter.4.cloned.1.call-update
  255.0 34.4 %reduce-scatter.4.cloned.1.call-done = f32[64,512]{1,0:T(8,128)} async-done(((f32[512,512]{1,0:T(8,128)}), f32[64,512]{1,0:T(8,128)}) %reduce-scatter.4.cloned.1.call-update) | async-done | bytes 131088 | tf_op jit(solution)/shard_map/reduce_scatter | solution.py:17
Async XLA Ops:
  6.5 231.4 %all-gather.2.cloned.1.call-start = ((), (), s32[]{:S(2)}) async-start(), calls=%async_computation.1 | async-start | bytes 16384000 | tf_op jit(solution)/shard_map/all_gather | solution.py:12
  7.3 282.1 %reduce-scatter.4.cloned.1.call-start = ((), (), s32[]{:S(2)}) async-start(), calls=%async_computation.2 | async-start | bytes 1179648 | tf_op jit(solution)/shard_map/reduce_scatter | solution.py:17
Sparse Core Ops, SparseCore 0:
  8.9 228.9 all-gather.1
  255.1 34.1 reduce-scatter.3

commit v2 on v1

v2 whole, which is shorter than its diff:
```python
import jax
import jax.numpy as jnp
from jax import lax
from jax.sharding import PartitionSpec as P

LINE = 4


def after(value, *earlier):
    return lax.optimization_barrier((value,) + earlier)[0]


def bounds(start, stop, size):
    return [(k, min(k + size, stop)) for k in range(start, stop, size)]


def shards(amplitude, integral, rows, cols, layers):
    ko = amplitude.shape[0]
    group = cols // LINE
    row, col, layer = (lax.axis_index(name) for name in ("row", "col", "depth"))
    if group > 1:
        groups = [[z * group + lane for lane in range(group)] for z in range(LINE)]
        amplitude = lax.all_gather(amplitude, "col", axis=2, axis_index_groups=groups, tiled=True)
    place = col // group
    block, width = amplitude.shape[2], integral.shape[2]

    def hop(pairs):
        lanes = [(a * group + lane, b * group + lane) for a, b in pairs for lane in range(group)]
        return lambda value: lax.ppermute(value, "col", lanes)

    inward, across, outward = hop([(0, 1), (3, 2)]), hop([(1, 2), (2, 1)]), hop([(1, 0), (2, 3)])

    lent = round(ko * 2 * block / (3 * block + width))
    main = bounds(0, ko - lent, 3)
    extra = [(ko - lent, ko)]
    pieces = bounds(ko - lent, ko, 1)

    def weights(k0, k1):
        return lax.dynamic_slice_in_dim(integral, row * ko + k0, k1 - k0, axis=1)

    own = {c: amplitude[c[0] : c[1]] for c in main + extra}
    same_in, far_inner, far_end = {}, {}, {}
    out_same, out_inner, out_end, lent_weights = {}, {}, {}, {}

    sends = {"in": [], "across": [], "out": []}
    split = len(pieces) * 2 // 3
    sends["in"] += [(same_in, c, own, inward) for c in extra]
    sends["in"] += [(lent_weights, c, None, inward) for c in pieces[:split]]
    sends["in"] += [(same_in, c, own, inward) for c in main]
    sends["in"] += [(lent_weights, c, None, inward) for c in pieces[split:]]
    sends["across"] += [(far_inner, c, own, across) for c in main + extra]
    sends["across"] += [(far_end, c, same_in, across) for c in extra + main]
    sends["out"] += [(out_same, c, own, outward) for c in main]
    sends["out"] += [(out_inner, c, far_inner, outward) for c in main]
    sends["out"] += [(out_end, c, far_end, outward) for c in main]

    clock = dict.fromkeys(sends, 0)
    arrived = {name: [] for name in sends}
    while any(sends.values()):
        ready = [n for n in sends if sends[n] and (sends[n][0][2] is None or sends[n][0][1] in sends[n][0][2])]
        name = min(ready, key=lambda n: clock[n])
        into, c, source, move = sends[name].pop(0)
        value = weights(*c) if source is None else source[c]
        if len(arrived[name]) >= 2:
            value = after(value, arrived[name][-2])
        into[c] = move(value)
        arrived[name].append(into[c])
        clock[name] += (c[1] - c[0]) * (width / block if source is None else 1)

    def product(left, right):
        return jnp.einsum(
            "kcm,ckn->mn", left, right, precision=lax.Precision.HIGH, preferred_element_type=jnp.float32
        )

    slots = [0.0] * 4
    for c in main + extra:
        held = [own[c], same_in[c], far_inner[c], far_end[c]]
        if c in out_same:
            held = [held[0], held[1] + out_same[c], held[2] + out_inner[c], held[3] + out_end[c]]
        for s in range(4):
            slots[s] = slots[s] + product(held[s], weights(*c))

    loan = [0.0] * 4
    for k0, k1 in pieces:
        for s, held in ((1, own), (2, far_inner), (3, far_end)):
            base = extra[0][0]
            loan[s] = loan[s] + product(held[extra[0]][k0 - base : k1 - base], lent_weights[(k0, k1)])
    loan[0] = jnp.zeros_like(loan[1])

    table = jnp.array([[0, 1, 2, 3], [1, 0, 2, 3], [3, 2, 0, 1], [3, 2, 1, 0]], jnp.int32)

    def reduce_rows(blocks, where):
        halves = jnp.stack(blocks).reshape(4, layers, block // layers, width)
        if layers == 2:
            away = lax.dynamic_index_in_dim(halves, 1 - layer, 1, keepdims=False)
            mine = lax.dynamic_index_in_dim(halves, layer, 1, keepdims=False)
            mine = mine + lax.ppermute(away, "depth", [(0, 1), (1, 0)])
        else:
            mine = lax.psum_scatter(halves, "depth", scatter_dimension=1, tiled=False)
        total = lax.dynamic_index_in_dim(mine, table[where, row], 0, keepdims=False)
        for t in range(1, 4):
            part = lax.dynamic_index_in_dim(mine, table[where, row ^ t], 0, keepdims=False)
            total = total + lax.ppermute(part, "row", [(r, r ^ t) for r in range(4)])
        return total

    returned = outward(reduce_rows(loan, place ^ 1))
    return reduce_rows(slots, place) + returned


def solution(mesh):
    rows, cols, layers = (mesh.shape[name] for name in ("row", "col", "depth"))
    return jax.shard_map(
        lambda amplitude, integral: shards(amplitude, integral, rows, cols, layers),
        mesh=mesh,
        in_specs=(P("row", "depth", "col"), P("depth", None, "col")),
        out_specs=P(("row", "depth"), "col"),
        check_vma=False,
    )
```

time: 296 us -> 260 us (0.88)
  waiting for transfers between devices: 266 us -> 13.4 us
  starting transfers between devices: 0.04 us -> 126 us
  matrix products: 15.8 us -> 78.2 us
  local copies, waits for them, and re-layouts: 1.3 us -> 22.3 us
  between operations: 13.4 us -> 16.9 us
    all_gather x1 -> x0, waiting for transfers between devices: 231 us -> none  [shards(): lax.all_gather(amplitude, 'col', axis=2, tiled=True)]
    ppermute x0 -> x55, starting transfers between devices: none -> 126 us  [the longest x47 118 us: hop(): return lambda value: lax.ppermute(value, 'col', lanes)]
    dot_general x1 -> x49, matrix products: 15.8 us -> 78.2 us  [product(): jnp.einsum('kcm,ckn->mn', left, right, precision=lax.Precision.HIGH, pref...]
    reduce_scatter x1 -> x0, waiting for transfers between devices: 34.4 us -> none  [shards(): lax.psum_scatter(product, ('row', 'depth'), scatter_dimension=0, tiled=True)]
    ppermute x0 -> x55, waiting for transfers between devices: none -> 13.4 us  [the longest x47 9.11 us: hop(): return lambda value: lax.ppermute(value, 'col', lanes)]
    optimization_barrier x0 -> x7, local copies, waits for them, and re-layouts: none -> 12 us  [after(): return lax.optimization_barrier((value,) + earlier)[0]]
    dynamic_slice x0 -> x2, local copies, waits for them, and re-layouts: none -> 4.73 us  [the longest x1 4.03 us: weights(): return lax.dynamic_slice_in_dim(integral, row * ko + k0, k1 - k0, axis=1)]
    unnamed x1 -> x26, local copies, waits for them, and re-layouts: 1.3 us -> 4.65 us
  transfers between devices with their start and end apart: 2 -> 55, of which waited for: 2 -> 6; matrix products, arithmetic and copies ran while one was open for 0% -> 37% of each run, Pallas kernels for 0% -> 0%
where the time goes in v2:
time: 260 us; the launch traced here: 258 us
  starting transfers between devices  126 us (48%)
  matrix products  78.2 us (30%)
  local copies, waits for them, and re-layouts  22.3 us (9%)
  between operations  16.9 us (6%)
  waiting for transfers between devices  13.4 us (5%)
    ppermute x47, starting transfers between devices, hop(): return lambda value: lax.ppermute(value, 'col', lanes)  118 us
    dot_general x49, matrix products, product(): jnp.einsum('kcm,ckn->mn', left, right, precision=lax.Precision.HIGH, pref...  78.2 us
    optimization_barrier x7, local copies, waits for them, and re-layouts, after(): return lax.optimization_barrier((value,) + earlier)[0]  12 us
    ppermute x47, waiting for transfers between devices, hop(): return lambda value: lax.ppermute(value, 'col', lanes)  9.11 us
    ppermute x6, starting transfers between devices, reduce_rows(): total = total + lax.ppermute(part, 'row', [(r, r ^ t) for r in range(4)])  7.11 us
  transfers between devices with their start and end apart: 55, of which 6 were waited for; matrix products, arithmetic and copies ran while one was open for 37% of the time, Pallas kernels for 0%

profile of v2, /device:TPU:0, one launch (start us, length us, event | category | flops | bytes accessed | tf_op | source)
XLA Modules:
  0.0 257.7 jit_solution(9494084342152507294)
XLA Ops:
  0.0 2.8 %fusion.338 = (f32[3,256,128]{2,1,0:T(8,128)S(1)}, f32[3,256,128]{2,1,0:T(8,128)}, f32[3,256,128]{2,1,0:T(8,128)}, f32[3,256,128]{2,1,0:T(8,128)}, f32[3,256,128]{2,1,0:T(8,128)}, /*index=5*/f32[3,256,128]{2,1,0:T(8,128)S(1)}) fusion(f32[25,256,128]{2,1,0:T(8,128)} %param.3), kind=kLoop, calls=%fused_computation.272 | loop fusion | bytes 4718592
  10.1 4.0 %constant_dynamic-slice_fusion.3 = (f32[256,1,512]{2,0,1:T(8,128)}, f32[256,1,512]{2,0,1:T(8,128)}, f32[256,1,512]{2,0,1:T(8,128)}, f32[256,1,512]{2,0,1:T(8,128...) fusion(f32[256,100,512]{2,0,1:T(8,128)} %param.4, s32[]{:T(128)S(6)} %select_n.135, ...), kind=kLoop, calls=%fused_computation.254 | loop fusion | bytes 7340060 | tf_op jit(solution)/shard_map/dynamic_slice | solution.py:39
  14.2 12.0 %collective-permute-start = (f32[256,1,512]{2,0,1:T(8,128)}, f32[256,1,512]{2,0,1:T(8,128)}, u32[]{:S(2)}, u32[]{:S(2)}) collective-permute-start(f32[256,1,512]{2,0,1:T(8,128)} %get-tuple-element.88), channel_id=1, source_target_pairs={{0,2},{6,4},{1,3},{7,5},{8,10},{14,12},{9,11},{15,13},{16,18},{22,... | collective-permute-start | bytes 1572872 | tf_op jit(solution)/shard_map/ppermute | solution.py:29
  31.2 2.4 copy.17
  37.4 2.3 collective-permute-start.4
  49.1 4.4 %collective-permute-done.10 = f32[3,256,128]{1,2,0:T(8,128)S(1)} collective-permute-done((f32[3,256,128]{1,2,0:T(8,128)}, f32[3,256,128]{1,2,0:T(8,128)S(1)}, u32[]{:S(2)}, u32[]{:S(2)}) %collective-permute-start.10) | collective-permute-done | bytes 393248 | tf_op jit(solution)/shard_map/ppermute | solution.py:29
  54.2 4.8 %collective-permute-start.1 = (f32[256,1,512]{2,0,1:T(8,128)}, f32[256,1,512]{2,0,1:T(8,128)}, u32[]{:S(2)}, u32[]{:S(2)}) collective-permute-start(f32[256,1,512]{2,0,1:T(8,128)} %get-tuple-element.45), channel_id=1, source_target_pairs={{0,2},{6,4},{1,3},{7,5},{8,10},{14,12},{9,11},{15,13},{16,18},{22,... | collective-permute-start | bytes 1572872 | tf_op jit(solution)/shard_map/ppermute | solution.py:29
  71.1 9.3 %collective-permute-start.5 = (f32[256,1,512]{2,0,1:T(8,128)}, f32[256,1,512]{2,0,1:T(8,128)}, u32[]{:S(2)}, u32[]{:S(2)}) collective-permute-start(f32[256,1,512]{2,0,1:T(8,128)} %get-tuple-element.47), channel_id=1, source_target_pairs={{0,2},{6,4},{1,3},{7,5},{8,10},{14,12},{9,11},{15,13},{16,18},{22,... | collective-permute-start | bytes 1572872 | tf_op jit(solution)/shard_map/ppermute | solution.py:29
  80.4 3.2 %fusion.155 = f32[512,128]{0,1:T(8,128)S(1)} fusion(f32[512,128]{0,1:T(8,128)S(1)} %fusion.158, f32[256,100,512]{2,0,1:T(8,128)} %param.4, s32[]{:T(128)S(6)} %select_n.132, f32[25,256,128]{2,1,0:T(8,128)S(1)} %copy-done), kind=kOutput, calls=%fused_computation.102 | convolution fusion | flops 704708608 | bytes 5111812 | tf_op jit(solution)/shard_map/kcm,ckn->mn/dot_general | solution.py:71
  94.2 3.3 %fusion.131 = f32[128,512]{1,0:T(8,128)S(1)} fusion(f32[7,256,128]{1,2,0:T(8,128)} %collective-permute-done.4, f32[256,100,512]{2,0,1:T(8,128)} %param.4, s32[]{:T(128)S(6)} %select_n.132), kind=kOutput, calls=%fused_computation.81 | convolution fusion | flops 704643072 | bytes 4849668 | tf_op jit(solution)/shard_map/kcm,ckn->mn/dot_general | solution.py:71
  101.2 7.8 %collective-permute-start.9 = (f32[3,256,128]{1,2,0:T(8,128)S(1)}, f32[3,256,128]{1,2,0:T(8,128)S(1)}, u32[]{:S(2)}, u32[]{:S(2)}) collective-permute-start(f32[3,256,128]{1,2,0:T(8,128)S(1)} %copy-done.7), channel_id=1, source_target_pairs={{0,2},{6,4},{1,3},{7,5},{8,10},{14,12},{9,11},{15,13},{16,18},{22,... | collective-permute-start | bytes 1179656 | tf_op jit(solution)/shard_map/ppermute | solution.py:29
  114.3 2.1 fusion.74
  116.5 2.1 collective-permute-done.9
  121.3 2.6 collective-permute-done.22
  123.8 3.5 %collective-permute-start.13 = (f32[3,256,128]{1,2,0:T(8,128)S(1)}, f32[3,256,128]{1,2,0:T(8,128)S(1)}, u32[]{:S(2)}, u32[]{:S(2)}) collective-permute-start(f32[3,256,128]{1,2,0:T(8,128)S(1)} %copy-done.8), channel_id=1, source_target_pairs={{0,2},{6,4},{1,3},{7,5},{8,10},{14,12},{9,11},{15,13},{16,18},{22,... | collective-permute-start | bytes 1179656 | tf_op jit(solution)/shard_map/ppermute | solution.py:29
  127.3 2.1 fusion.86
  132.2 2.1 fusion.98
  134.7 4.6 %collective-permute-start.7 = (f32[3,256,128]{1,2,0:T(8,128)}, f32[3,256,128]{1,2,0:T(8,128)S(1)}, u32[]{:S(2)}, u32[]{:S(2)}) collective-permute-start(f32[3,256,128]{1,2,0:T(8,128)} %copy.12), channel_id=1, source_target_pairs={{0,2},{6,4},{1,3},{7,5},{8,10},{14,12},{9,11},{15,13},{16,18},{22,... | collective-permute-start | bytes 1179656 | tf_op jit(solution)/shard_map/ppermute | solution.py:29
  145.9 3.2 %fusion.137 = f32[128,512]{1,0:T(8,128)S(1)} fusion(f32[7,256,128]{1,2,0:T(8,128)S(1)} %collective-permute-done.32, f32[256,100,512]{2,0,1:T(8,128)} %param.4, s32[]{:T(128)S(6)} %select_n.132), kind=kOutput, calls=%fused_computation.83 | convolution fusion | flops 704643072 | bytes 4849668 | tf_op jit(solution)/shard_map/kcm,ckn->mn/dot_general | solution.py:71
  149.1 3.2 %fusion.134 = f32[128,512]{1,0:T(8,128)S(1)} fusion(f32[7,256,128]{1,2,0:T(8,128)S(1)} %collective-permute-done.29, f32[256,100,512]{2,0,1:T(8,128)} %param.4, s32[]{:T(128)S(6)} %select_n.132), kind=kOutput, calls=%fused_computation.82 | convolution fusion | flops 704643072 | bytes 4849668 | tf_op jit(solution)/shard_map/kcm,ckn->mn/dot_general | solution.py:71
  152.4 7.5 %collective-permute-start.47 = (f32[256,1,512]{2,0,1:T(8,128)S(1)}, f32[256,1,512]{2,0,1:T(8,128)S(1)}, u32[]{:S(2)}, u32[]{:S(2)}) collective-permute-start(f32[256,1,512]{2,0,1:T(8,128)S(1)} %copy-done.4), channel_id=1, source_target_pairs={{0,2},{6,4},{1,3},{7,5},{8,10},{14,12},{9,11},{15,13},{16,18},{22,... | collective-permute-start | bytes 1572872 | tf_op jit(solution)/shard_map/ppermute | solution.py:29
  160.0 2.1 fusion.107
  163.4 2.1 fusion.71
  166.3 2.1 fusion.110
  170.5 2.2 fusion.206
  174.8 5.9 %collective-permute-start.15 = (f32[3,256,128]{1,2,0:T(8,128)S(1)}, f32[3,256,128]{1,2,0:T(8,128)S(1)}, u32[]{:S(2)}, u32[]{:S(2)}) collective-permute-start(f32[3,256,128]{1,2,0:T(8,128)S(1)} %copy-done.6), channel_id=1, source_target_pairs={{0,2},{6,4},{1,3},{7,5},{8,10},{14,12},{9,11},{15,13},{16,18},{22,... | collective-permute-start | bytes 1179656 | tf_op jit(solution)/shard_map/ppermute | solution.py:29
  183.4 2.1 fusion.95
  185.9 7.7 %collective-permute-start.49 = (f32[256,1,512]{2,0,1:T(8,128)S(1)}, f32[256,1,512]{2,0,1:T(8,128)S(1)}, u32[]{:S(2)}, u32[]{:S(2)}) collective-permute-start(f32[256,1,512]{2,0,1:T(8,128)S(1)} %copy-done.3), channel_id=1, source_target_pairs={{0,2},{6,4},{1,3},{7,5},{8,10},{14,12},{9,11},{15,13},{16,18},{22,... | collective-permute-start | bytes 1572872 | tf_op jit(solution)/shard_map/ppermute | solution.py:29
  197.6 2.1 fusion.119
  201.8 2.2 fusion.224
  204.1 9.3 %collective-permute-start.48 = (f32[256,1,512]{2,0,1:T(8,128)S(1)}, f32[256,1,512]{2,0,1:T(8,128)S(1)}, u32[]{:S(2)}, u32[]{:S(2)}) collective-permute-start(f32[256,1,512]{2,0,1:T(8,128)S(1)} %copy-done.2), channel_id=1, source_target_pairs={{0,2},{6,4},{1,3},{7,5},{8,10},{14,12},{9,11},{15,13},{16,18},{22,... | collective-permute-start | bytes 1572872 | tf_op jit(solution)/shard_map/ppermute | solution.py:29
  253.3 2.4 collective-permute-done.46
  (173 shorter events, 110.9 us)
Async XLA Ops:
  3.7 33.7 %collective-permute-start.3 = (f32[3,256,128]{1,2,0:T(8,128)}, f32[3,256,128]{1,2,0:T(8,128)}, u32[]{:S(2)}, u32[]{:S(2)}) collective-permute-start(f32[3,256,128]{1,2,0:T(8,128)} %copy.11), channel_id=1, source_target_pairs={{2,0},{4,6},{3,1},{5,7},{10,8},{12,14},{11,9},{13,15},{18,16},{20,... | collective-permute-start | bytes 1179656 | tf_op jit(solution)/shard_map/ppermute | solution.py:29
  5.0 34.7 %collective-permute-start.17 = (f32[3,256,128]{1,2,0:T(8,128)}, f32[3,256,128]{1,2,0:T(8,128)}, u32[]{:S(2)}, u32[]{:S(2)}) collective-permute-start(f32[3,256,128]{1,2,0:T(8,128)} %copy.11), channel_id=1, source_target_pairs={{2,4},{4,2},{3,5},{5,3},{10,12},{12,10},{11,13},{13,11},{18,20},{2... | collective-permute-start | bytes 1179656 | tf_op jit(solution)/shard_map/ppermute | solution.py:29
  7.4 35.6 %collective-permute-start.8 = (f32[3,256,128]{1,2,0:T(8,128)}, f32[3,256,128]{1,2,0:T(8,128)}, u32[]{:S(2)}, u32[]{:S(2)}) collective-permute-start(f32[3,256,128]{1,2,0:T(8,128)} %copy.12), channel_id=1, source_target_pairs={{2,0},{4,6},{3,1},{5,7},{10,8},{12,14},{11,9},{13,15},{18,16},{20,... | collective-permute-start | bytes 1179656 | tf_op jit(solution)/shard_map/ppermute | solution.py:29
  8.7 35.7 %collective-permute-start.19 = (f32[3,256,128]{1,2,0:T(8,128)}, f32[3,256,128]{1,2,0:T(8,128)}, u32[]{:S(2)}, u32[]{:S(2)}) collective-permute-start(f32[3,256,128]{1,2,0:T(8,128)} %copy.12), channel_id=1, source_target_pairs={{2,4},{4,2},{3,5},{5,3},{10,12},{12,10},{11,13},{13,11},{18,20},{2... | collective-permute-start | bytes 1179656 | tf_op jit(solution)/shard_map/ppermute | solution.py:29
  14.2 33.6 %collective-permute-start = (f32[256,1,512]{2,0,1:T(8,128)}, f32[256,1,512]{2,0,1:T(8,128)}, u32[]{:S(2)}, u32[]{:S(2)}) collective-permute-start(f32[256,1,512]{2,0,1:T(8,128)} %get-tuple-element.88), channel_id=1, source_target_pairs={{0,2},{6,4},{1,3},{7,5},{8,10},{14,12},{9,11},{15,13},{16,18},{22,... | collective-permute-start | bytes 1572872 | tf_op jit(solution)/shard_map/ppermute | solution.py:29
  37.4 32.2 %collective-permute-start.4 = (f32[7,256,128]{1,2,0:T(8,128)}, f32[7,256,128]{1,2,0:T(8,128)}, u32[]{:S(2)}, u32[]{:S(2)}) collective-permute-start(f32[7,256,128]{1,2,0:T(8,128)} %copy.17), channel_id=1, source_target_pairs={{0,2},{6,4},{1,3},{7,5},{8,10},{14,12},{9,11},{15,13},{16,18},{22,... | collective-permute-start | bytes 2752520 | tf_op jit(solution)/shard_map/ppermute | solution.py:29
  43.0 23.3 %collective-permute-start.21 = (f32[3,256,128]{1,2,0:T(8,128)}, f32[3,256,128]{1,2,0:T(8,128)}, u32[]{:S(2)}, u32[]{:S(2)}) collective-permute-start(f32[3,256,128]{1,2,0:T(8,128)} %copy.13), channel_id=1, source_target_pairs={{2,4},{4,2},{3,5},{5,3},{10,12},{12,10},{11,13},{13,11},{18,20},{2... | collective-permute-start | bytes 1179656 | tf_op jit(solution)/shard_map/ppermute | solution.py:29
  44.4 20.5 %collective-permute-start.12 = (f32[3,256,128]{1,2,0:T(8,128)}, f32[3,256,128]{1,2,0:T(8,128)}, u32[]{:S(2)}, u32[]{:S(2)}) collective-permute-start(f32[3,256,128]{1,2,0:T(8,128)} %copy.14), channel_id=1, source_target_pairs={{2,0},{4,6},{3,1},{5,7},{10,8},{12,14},{11,9},{13,15},{18,16},{20,... | collective-permute-start | bytes 1179656 | tf_op jit(solution)/shard_map/ppermute | solution.py:29
  47.7 23.4 %collective-permute-start.23 = (f32[3,256,128]{1,2,0:T(8,128)}, f32[3,256,128]{1,2,0:T(8,128)}, u32[]{:S(2)}, u32[]{:S(2)}) collective-permute-start(f32[3,256,128]{1,2,0:T(8,128)} %copy.14), channel_id=1, source_target_pairs={{2,4},{4,2},{3,5},{5,3},{10,12},{12,10},{11,13},{13,11},{18,20},{2... | collective-permute-start | bytes 1179656 | tf_op jit(solution)/shard_map/ppermute | solution.py:29
  54.2 36.0 %collective-permute-start.1 = (f32[256,1,512]{2,0,1:T(8,128)}, f32[256,1,512]{2,0,1:T(8,128)}, u32[]{:S(2)}, u32[]{:S(2)}) collective-permute-start(f32[256,1,512]{2,0,1:T(8,128)} %get-tuple-element.45), channel_id=1, source_target_pairs={{0,2},{6,4},{1,3},{7,5},{8,10},{14,12},{9,11},{15,13},{16,18},{22,... | collective-permute-start | bytes 1572872 | tf_op jit(solution)/shard_map/ppermute | solution.py:29
  64.9 26.2 %collective-permute-start.14 = (f32[3,256,128]{1,2,0:T(8,128)}, f32[3,256,128]{1,2,0:T(8,128)}, u32[]{:S(2)}, u32[]{:S(2)}) collective-permute-start(f32[3,256,128]{1,2,0:T(8,128)} %copy.15), channel_id=1, source_target_pairs={{2,0},{4,6},{3,1},{5,7},{10,8},{12,14},{11,9},{13,15},{18,16},{20,... | collective-permute-start | bytes 1179656 | tf_op jit(solution)/shard_map/ppermute | solution.py:29
  66.3 26.5 %collective-permute-start.16 = (f32[3,256,128]{1,2,0:T(8,128)}, f32[3,256,128]{1,2,0:T(8,128)}, u32[]{:S(2)}, u32[]{:S(2)}) collective-permute-start(f32[3,256,128]{1,2,0:T(8,128)} %copy.16), channel_id=1, source_target_pairs={{2,0},{4,6},{3,1},{5,7},{10,8},{12,14},{11,9},{13,15},{18,16},{20,... | collective-permute-start | bytes 1179656 | tf_op jit(solution)/shard_map/ppermute | solution.py:29
  69.6 27.8 %collective-permute-start.25 = (f32[3,256,128]{1,2,0:T(8,128)}, f32[3,256,128]{1,2,0:T(8,128)}, u32[]{:S(2)}, u32[]{:S(2)}) collective-permute-start(f32[3,256,128]{1,2,0:T(8,128)} %copy.15), channel_id=1, source_target_pairs={{2,4},{4,2},{3,5},{5,3},{10,12},{12,10},{11,13},{13,11},{18,20},{2... | collective-permute-start | bytes 1179656 | tf_op jit(solution)/shard_map/ppermute | solution.py:29
  71.1 37.9 %collective-permute-start.5 = (f32[256,1,512]{2,0,1:T(8,128)}, f32[256,1,512]{2,0,1:T(8,128)}, u32[]{:S(2)}, u32[]{:S(2)}) collective-permute-start(f32[256,1,512]{2,0,1:T(8,128)} %get-tuple-element.47), channel_id=1, source_target_pairs={{0,2},{6,4},{1,3},{7,5},{8,10},{14,12},{9,11},{15,13},{16,18},{22,... | collective-permute-start | bytes 1572872 | tf_op jit(solution)/shard_map/ppermute | solution.py:29
  92.9 17.5 %collective-permute-start.18 = (f32[3,256,128]{1,2,0:T(8,128)}, f32[3,256,128]{1,2,0:T(8,128)S(1)}, u32[]{:S(2)}, u32[]{:S(2)}) collective-permute-start(f32[3,256,128]{1,2,0:T(8,128)} %collective-permute-done.17), channel_id=1, source_target_pairs={{2,0},{4,6},{3,1},{5,7},{10,8},{12,14},{11,9},{13,15},{18,16},{20,... | collective-permute-start | bytes 1179656 | tf_op jit(solution)/shard_map/ppermute | solution.py:29
  100.3 34.4 %collective-permute-start.29 = (f32[7,256,128]{1,2,0:T(8,128)S(1)}, f32[7,256,128]{1,2,0:T(8,128)S(1)}, u32[]{:S(2)}, u32[]{:S(2)}) collective-permute-start(f32[7,256,128]{1,2,0:T(8,128)S(1)} %copy-done.1), channel_id=1, source_target_pairs={{2,4},{4,2},{3,5},{5,3},{10,12},{12,10},{11,13},{13,11},{18,20},{2... | collective-permute-start | bytes 2752520 | tf_op jit(solution)/shard_map/ppermute | solution.py:29
  101.2 17.3 %collective-permute-start.9 = (f32[3,256,128]{1,2,0:T(8,128)S(1)}, f32[3,256,128]{1,2,0:T(8,128)S(1)}, u32[]{:S(2)}, u32[]{:S(2)}) collective-permute-start(f32[3,256,128]{1,2,0:T(8,128)S(1)} %copy-done.7), channel_id=1, source_target_pairs={{0,2},{6,4},{1,3},{7,5},{8,10},{14,12},{9,11},{15,13},{16,18},{22,... | collective-permute-start | bytes 1179656 | tf_op jit(solution)/shard_map/ppermute | solution.py:29
  109.0 21.9 %collective-permute-start.6 = (f32[256,1,512]{2,0,1:T(8,128)S(1)}, f32[256,1,512]{2,0,1:T(8,128)S(1)}, u32[]{:S(2)}, u32[]{:S(2)}) collective-permute-start(f32[256,1,512]{2,0,1:T(8,128)S(1)} %copy-done.5), channel_id=1, source_target_pairs={{0,2},{6,4},{1,3},{7,5},{8,10},{14,12},{9,11},{15,13},{16,18},{22,... | collective-permute-start | bytes 1572872 | tf_op jit(solution)/shard_map/ppermute | solution.py:29
  118.5 22.4 %collective-permute-start.32 = (f32[7,256,128]{1,2,0:T(8,128)}, f32[7,256,128]{1,2,0:T(8,128)S(1)}, u32[]{:S(2)}, u32[]{:S(2)}) collective-permute-start(f32[7,256,128]{1,2,0:T(8,128)} %collective-permute-done.4), channel_id=1, source_target_pairs={{2,4},{4,2},{3,5},{5,3},{10,12},{12,10},{11,13},{13,11},{18,20},{2... | collective-permute-start | bytes 2752520 | tf_op jit(solution)/shard_map/ppermute | solution.py:29
  123.8 28.6 %collective-permute-start.13 = (f32[3,256,128]{1,2,0:T(8,128)S(1)}, f32[3,256,128]{1,2,0:T(8,128)S(1)}, u32[]{:S(2)}, u32[]{:S(2)}) collective-permute-start(f32[3,256,128]{1,2,0:T(8,128)S(1)} %copy-done.8), channel_id=1, source_target_pairs={{0,2},{6,4},{1,3},{7,5},{8,10},{14,12},{9,11},{15,13},{16,18},{22,... | collective-permute-start | bytes 1179656 | tf_op jit(solution)/shard_map/ppermute | solution.py:29
  129.4 36.1 %collective-permute-start.26 = (f32[3,256,128]{1,2,0:T(8,128)}, f32[3,256,128]{1,2,0:T(8,128)S(1)}, u32[]{:S(2)}, u32[]{:S(2)}) collective-permute-start(f32[3,256,128]{1,2,0:T(8,128)} %collective-permute-done.25), channel_id=1, source_target_pairs={{2,0},{4,6},{3,1},{5,7},{10,8},{12,14},{11,9},{13,15},{18,16},{20,... | collective-permute-start | bytes 1179656 | tf_op jit(solution)/shard_map/ppermute | solution.py:29
  130.9 37.5 %collective-permute-start.28 = (f32[3,256,128]{1,2,0:T(8,128)S(1)}, f32[3,256,128]{1,2,0:T(8,128)S(1)}, u32[]{:S(2)}, u32[]{:S(2)}) collective-permute-start(f32[3,256,128]{1,2,0:T(8,128)S(1)} %collective-permute-done.27), channel_id=1, source_target_pairs={{2,0},{4,6},{3,1},{5,7},{10,8},{12,14},{11,9},{13,15},{18,16},{20,... | collective-permute-start | bytes 1179656 | tf_op jit(solution)/shard_map/ppermute | solution.py:29
  134.7 27.4 %collective-permute-start.7 = (f32[3,256,128]{1,2,0:T(8,128)}, f32[3,256,128]{1,2,0:T(8,128)S(1)}, u32[]{:S(2)}, u32[]{:S(2)}) collective-permute-start(f32[3,256,128]{1,2,0:T(8,128)} %copy.12), channel_id=1, source_target_pairs={{0,2},{6,4},{1,3},{7,5},{8,10},{14,12},{9,11},{15,13},{16,18},{22,... | collective-permute-start | bytes 1179656 | tf_op jit(solution)/shard_map/ppermute | solution.py:29
  140.9 31.8 %collective-permute-start.30 = (f32[3,256,128]{1,2,0:T(8,128)S(1)}, f32[3,256,128]{1,2,0:T(8,128)S(1)}, u32[]{:S(2)}, u32[]{:S(2)}) collective-permute-start(f32[3,256,128]{1,2,0:T(8,128)S(1)} %collective-permute-done.2), channel_id=1, source_target_pairs={{2,4},{4,2},{3,5},{5,3},{10,12},{12,10},{11,13},{13,11},{18,20},{2... | collective-permute-start | bytes 1179656 | tf_op jit(solution)/shard_map/ppermute | solution.py:29
  152.4 29.7 %collective-permute-start.47 = (f32[256,1,512]{2,0,1:T(8,128)S(1)}, f32[256,1,512]{2,0,1:T(8,128)S(1)}, u32[]{:S(2)}, u32[]{:S(2)}) collective-permute-start(f32[256,1,512]{2,0,1:T(8,128)S(1)} %copy-done.4), channel_id=1, source_target_pairs={{0,2},{6,4},{1,3},{7,5},{8,10},{14,12},{9,11},{15,13},{16,18},{22,... | collective-permute-start | bytes 1572872 | tf_op jit(solution)/shard_map/ppermute | solution.py:29
  172.7 20.9 %collective-permute-start.31 = (f32[3,256,128]{1,2,0:T(8,128)S(1)}, f32[3,256,128]{1,2,0:T(8,128)S(1)}, u32[]{:S(2)}, u32[]{:S(2)}) collective-permute-start(f32[3,256,128]{1,2,0:T(8,128)S(1)} %collective-permute-done.30), channel_id=1, source_target_pairs={{2,0},{4,6},{3,1},{5,7},{10,8},{12,14},{11,9},{13,15},{18,16},{20,... | collective-permute-start | bytes 1179656 | tf_op jit(solution)/shard_map/ppermute | solution.py:29
  174.8 20.1 %collective-permute-start.15 = (f32[3,256,128]{1,2,0:T(8,128)S(1)}, f32[3,256,128]{1,2,0:T(8,128)S(1)}, u32[]{:S(2)}, u32[]{:S(2)}) collective-permute-start(f32[3,256,128]{1,2,0:T(8,128)S(1)} %copy-done.6), channel_id=1, source_target_pairs={{0,2},{6,4},{1,3},{7,5},{8,10},{14,12},{9,11},{15,13},{16,18},{22,... | collective-permute-start | bytes 1179656 | tf_op jit(solution)/shard_map/ppermute | solution.py:29
  185.9 18.2 %collective-permute-start.49 = (f32[256,1,512]{2,0,1:T(8,128)S(1)}, f32[256,1,512]{2,0,1:T(8,128)S(1)}, u32[]{:S(2)}, u32[]{:S(2)}) collective-permute-start(f32[256,1,512]{2,0,1:T(8,128)S(1)} %copy-done.3), channel_id=1, source_target_pairs={{0,2},{6,4},{1,3},{7,5},{8,10},{14,12},{9,11},{15,13},{16,18},{22,... | collective-permute-start | bytes 1572872 | tf_op jit(solution)/shard_map/ppermute | solution.py:29
  193.6 20.7 %collective-permute-start.36 = (f32[3,256,128]{1,2,0:T(8,128)S(1)}, f32[3,256,128]{1,2,0:T(8,128)S(1)}, u32[]{:S(2)}, u32[]{:S(2)}) collective-permute-start(f32[3,256,128]{1,2,0:T(8,128)S(1)} %collective-permute-done.35), channel_id=1, source_target_pairs={{2,0},{4,6},{3,1},{5,7},{10,8},{12,14},{11,9},{13,15},{18,16},{20,... | collective-permute-start | bytes 1179656 | tf_op jit(solution)/shard_map/ppermute | solution.py:29
  194.9 19.4 %collective-permute-start.39 = (f32[3,256,128]{1,2,0:T(8,128)S(1)}, f32[3,256,128]{1,2,0:T(8,128)S(1)}, u32[]{:S(2)}, u32[]{:S(2)}) collective-permute-start(f32[3,256,128]{1,2,0:T(8,128)S(1)} %collective-permute-done.13), channel_id=1, source_target_pairs={{2,4},{4,2},{3,5},{5,3},{10,12},{12,10},{11,13},{13,11},{18,20},{2... | collective-permute-start | bytes 1179656 | tf_op jit(solution)/shard_map/ppermute | solution.py:29
  195.6 22.0 %collective-permute-start.38 = (f32[3,256,128]{1,2,0:T(8,128)S(1)}, f32[3,256,128]{1,2,0:T(8,128)S(1)}, u32[]{:S(2)}, u32[]{:S(2)}) collective-permute-start(f32[3,256,128]{1,2,0:T(8,128)S(1)} %collective-permute-done.37), channel_id=1, source_target_pairs={{2,0},{4,6},{3,1},{5,7},{10,8},{12,14},{11,9},{13,15},{18,16},{20,... | collective-permute-start | bytes 1179656 | tf_op jit(solution)/shard_map/ppermute | solution.py:29
  196.9 20.7 %collective-permute-start.41 = (f32[3,256,128]{1,2,0:T(8,128)S(1)}, f32[3,256,128]{1,2,0:T(8,128)S(1)}, u32[]{:S(2)}, u32[]{:S(2)}) collective-permute-start(f32[3,256,128]{1,2,0:T(8,128)S(1)} %collective-permute-done.15), channel_id=1, source_target_pairs={{2,4},{4,2},{3,5},{5,3},{10,12},{12,10},{11,13},{13,11},{18,20},{2... | collective-permute-start | bytes 1179656 | tf_op jit(solution)/shard_map/ppermute | solution.py:29
  (35 other events, 412.6 us)

commit v3 on v2

v3 whole, which is shorter than its diff:
```python
import functools

import jax
import jax.numpy as jnp
from jax import lax
from jax.experimental import pallas as pl
from jax.experimental.pallas import tpu as pltpu
from jax.sharding import PartitionSpec as P

LINE = 4


def after(value, *earlier):
    return lax.optimization_barrier((value,) + earlier)[0]


def bounds(start, *sizes):
    ends = [start + sum(sizes[: i + 1]) for i in range(len(sizes))]
    return [(stop - size, stop) for stop, size in zip(ends, sizes) if size > 0]


def thirds(count):
    return count - 2 * (count // 3), count // 3, count // 3


def parts(value):
    high = value.astype(jnp.bfloat16)
    return high, (value - high.astype(jnp.float32)).astype(jnp.bfloat16)


def contract_kernel(terms, first, offset_ref, *refs):
    del offset_ref
    out_ref = refs[-1]
    weight_ref = refs[sum(terms)]

    @pl.when(pl.program_id(0) == 0)
    def _():
        out_ref[...] = jnp.zeros_like(out_ref) if first else refs[sum(terms) + 1][...]

    highs, lows, at = [], [], 0
    for n in terms:
        value = refs[at][0]
        for ref in refs[at + 1 : at + n]:
            value = value + ref[0]
        at += n
        high, low = parts(value)
        highs.append(high)
        lows.append(low)
    high, low = parts(weight_ref[0])
    highs = jnp.concatenate(highs, axis=1)
    lows = jnp.concatenate(lows, axis=1)
    left = jnp.concatenate([highs, highs, lows], axis=0)
    right = jnp.concatenate([high, low, high], axis=0)
    product = lax.dot_general(left, right, (((0,), (0,)), ((), ())), preferred_element_type=jnp.float32)
    out_ref[...] += product.reshape(out_ref.shape)


def contract(slots, weights, offset, total):
    terms = [len(slot) for slot in slots]
    steps, depth, block = slots[0][0].shape
    width = weights.shape[2]
    shape = (len(slots), block, width)
    whole = pl.BlockSpec(shape, lambda i, o: (0, 0, 0))
    in_specs = [pl.BlockSpec((1, depth, block), lambda i, o: (i, 0, 0))] * sum(terms)
    in_specs.append(pl.BlockSpec((1, depth, width), lambda i, o: (o[0] + i, 0, 0)))
    operands = [a for slot in slots for a in slot] + [weights]
    aliases = {}
    if total is not None:
        in_specs.append(whole)
        aliases = {len(operands) + 1: 0}
        operands.append(total)
    return pl.pallas_call(
        functools.partial(contract_kernel, terms, total is None),
        out_shape=jax.ShapeDtypeStruct(shape, jnp.float32),
        grid_spec=pltpu.PrefetchScalarGridSpec(
            num_scalar_prefetch=1, grid=(steps,), in_specs=in_specs, out_specs=whole
        ),
        input_output_aliases=aliases,
        compiler_params=pltpu.CompilerParams(vmem_limit_bytes=40 << 20),
        cost_estimate=pl.CostEstimate(
            flops=6 * steps * depth * len(slots) * block * width,
            bytes_accessed=4 * (steps * depth * (width + sum(terms) * block) + 2 * len(slots) * block * width),
            transcendentals=0,
        ),
    )(jnp.reshape(offset, (1,)).astype(jnp.int32), *operands)


def shards(amplitude, integral, rows, cols, layers):
    ko = amplitude.shape[0]
    group = cols // LINE
    row, col, layer = (lax.axis_index(name) for name in ("row", "col", "depth"))
    if group > 1:
        groups = [[z * group + lane for lane in range(group)] for z in range(LINE)]
        amplitude = lax.all_gather(amplitude, "col", axis=2, axis_index_groups=groups, tiled=True)
    place = col // group
    block, width = amplitude.shape[2], integral.shape[2]
    integral = jnp.transpose(integral, (1, 0, 2))

    def hop(pairs):
        lanes = [(a * group + lane, b * group + lane) for a, b in pairs for lane in range(group)]
        return lambda value: lax.ppermute(value, "col", lanes)

    inward, across, outward = hop([(0, 1), (3, 2)]), hop([(1, 2), (2, 1)]), hop([(1, 0), (2, 3)])

    lent = round(ko * 2 * block / (3 * block + width))
    base = ko - lent
    main = bounds(0, *thirds(base))
    extra = (base, ko)
    sizes = [lent // 4 + (i < lent % 4) for i in range(4)]
    pieces = bounds(base, *sizes)

    own, same_in, far_inner, far_end = {}, {}, {}, {}
    out_same, out_inner, out_end, lent_weights = {}, {}, {}, {}
    last = main[-1]
    tail = bounds(last[0], last[1] - last[0] - (last[1] - last[0]) // 3, (last[1] - last[0]) // 3)

    sends = {"in": [], "across": [], "out": []}
    early = len(pieces) // 2
    sends["in"] += [(lent_weights, c, None, inward) for c in pieces[:early]]
    sends["in"] += [(same_in, c, own, inward) for c in main + [extra]]
    sends["in"] += [(lent_weights, c, None, inward) for c in pieces[early:]]
    sends["across"] += [(far_inner, c, own, across) for c in main + [extra]]
    sends["across"] += [(far_end, c, same_in, across) for c in main + [extra]]
    sends["out"] += [(out_same, c, own, outward) for c in main]
    sends["out"] += [(out_inner, c, far_inner, outward) for c in main]
    sends["out"] += [(out_end, c, far_end, outward) for c in main[:-1] + tail]

    def find(table, c):
        for (k0, k1), value in table.items():
            if k0 <= c[0] and c[1] <= k1:
                return value if (k0, k1) == c else value[c[0] - k0 : c[1] - k0]
        return None

    clock = dict.fromkeys(sends, 0)
    arrived = {name: [] for name in sends}
    newest = None
    while any(sends.values()):
        for c in main + [extra]:
            if c not in own and (newest is not None or c == main[0]):
                own[c] = (amplitude if newest is None else after(amplitude, newest))[c[0] : c[1]]
                break
        ready = [
            n
            for n in sends
            if sends[n] and (sends[n][0][2] is None or find(sends[n][0][2], sends[n][0][1]) is not None)
        ]
        name = min(ready, key=lambda n: (clock[n], n != "out"))
        into, c, source, move = sends[name].pop(0)
        if source is None:
            value = lax.dynamic_slice_in_dim(integral, row * ko + c[0], c[1] - c[0], axis=0)
        else:
            value = find(source, c)
        if len(arrived[name]) >= 2:
            value = after(value, arrived[name][-2])
        into[c] = newest = move(value)
        arrived[name].append(newest)
        clock[name] += (c[1] - c[0]) * (width / block if source is None else 1)

    near, far = None, None
    for c in main:
        near = contract([[own[c]], [same_in[c], out_same[c]], [far_inner[c], out_inner[c]]], integral, row * ko + c[0], near)
    near = contract([[own[extra]], [same_in[extra]], [far_inner[extra]]], integral, row * ko + base, near)
    for c in main[:-1] + tail:
        far = contract([[find(far_end, c), out_end[c]]], integral, row * ko + c[0], far)
    far = contract([[far_end[extra]]], integral, row * ko + base, far)

    loan = None
    for c in pieces:
        loan = contract(
            [[find(held, c)] for held in (own, far_inner, far_end)], lent_weights[c], jnp.int32(0), loan
        )

    table = jnp.array([[0, 1, 2, 3], [1, 0, 2, 3], [3, 2, 0, 1], [3, 2, 1, 0]], jnp.int32)

    def reduce_rows(blocks, where):
        halves = blocks.reshape(4, layers, block // layers, width)
        if layers == 2:
            away = lax.dynamic_index_in_dim(halves, 1 - layer, 1, keepdims=False)
            mine = lax.dynamic_index_in_dim(halves, layer, 1, keepdims=False)
            mine = mine + lax.ppermute(away, "depth", [(0, 1), (1, 0)])
        else:
            mine = lax.psum_scatter(halves, "depth", scatter_dimension=1, tiled=False)
        total = lax.dynamic_index_in_dim(mine, table[where, row], 0, keepdims=False)
        for t in range(1, 4):
            part = lax.dynamic_index_in_dim(mine, table[where, row ^ t], 0, keepdims=False)
            total = total + lax.ppermute(part, "row", [(r, r ^ t) for r in range(4)])
        return total

    returned = outward(reduce_rows(jnp.concatenate([jnp.zeros_like(far), loan]), place ^ 1))
    return reduce_rows(jnp.concatenate([near, far]), place) + returned


def solution(mesh):
    rows, cols, layers = (mesh.shape[name] for name in ("row", "col", "depth"))
    return jax.shard_map(
        lambda amplitude, integral: shards(amplitude, integral, rows, cols, layers),
        mesh=mesh,
        in_specs=(P("row", "depth", "col"), P("depth", None, "col")),
        out_specs=P(("row", "depth"), "col"),
        check_vma=False,
    )
```

time: 260 us -> 243 us (0.935)
  matrix products: 78.2 us -> 0 us
  Pallas kernels: 0 us -> 48.7 us
  waiting for transfers between devices: 13.4 us -> 55.3 us
  starting transfers between devices: 126 us -> 96.6 us
    dot_general x49 -> x0, matrix products: 78.2 us -> none  [product(): jnp.einsum('kcm,ckn->mn', left, right, precision=lax.Precision.HIGH, pref...]
    pallas_call x0 -> x13, Pallas kernels: none -> 48.7 us  [contract(): pl.pallas_call(functools.partial(contract_kernel, terms, total is None),...]
    ppermute x47 -> x27, waiting for transfers between devices: 9.11 us -> 52.4 us  [hop(): return lambda value: lax.ppermute(value, 'col', lanes)]
    ppermute x47 -> x27, starting transfers between devices: 118 us -> 86.9 us  [hop(): return lambda value: lax.ppermute(value, 'col', lanes)]
    optimization_barrier x7 -> x0, local copies, waits for them, and re-layouts: 12 us -> none  [after(): return lax.optimization_barrier((value,) + earlier)[0]]
    slice x0 -> x12, local copies, waits for them, and re-layouts: none -> 8.24 us  [the longest x4 5.98 us: shards(): (amplitude if newest is None else after(amplitude, newest))[c[0]:c[1]]]
    unnamed x26 -> x36, local copies, waits for them, and re-layouts: 4.65 us -> 8.92 us
  transfers between devices with their start and end apart: 55 -> 35, of which waited for: 6 -> 8; matrix products, arithmetic and copies ran while one was open for 37% -> 6% of each run, Pallas kernels for 0% -> 20%
where the time goes in v3:
time: 243 us; the launch traced here: 241 us
  starting transfers between devices  96.6 us (40%)
  waiting for transfers between devices  55.3 us (23%)
  Pallas kernels  48.7 us (20%)
  local copies, waits for them, and re-layouts  24.1 us (10%)
  between operations  15.6 us (6%)
    ppermute x27, starting transfers between devices, hop(): return lambda value: lax.ppermute(value, 'col', lanes)  86.9 us
    ppermute x27, waiting for transfers between devices, hop(): return lambda value: lax.ppermute(value, 'col', lanes)  52.4 us
    pallas_call x13, Pallas kernels, contract(): pl.pallas_call(functools.partial(contract_kernel, terms, total is None),...  48.7 us
    ppermute x6, starting transfers between devices, reduce_rows(): total = total + lax.ppermute(part, 'row', [(r, r ^ t) for r in range(4)])  9.21 us
    unnamed x36, local copies, waits for them, and re-layouts  8.92 us
    slice x4, local copies, waits for them, and re-layouts, shards(): (amplitude if newest is None else after(amplitude, newest))[c[0]:c[1]]  5.98 us
  transfers between devices with their start and end apart: 35, of which 8 were waited for; matrix products, arithmetic and copies ran while one was open for 6% of the time, Pallas kernels for 20%

profile of v3, /device:TPU:0, one launch (start us, length us, event | category | flops | bytes accessed | tf_op | source)
XLA Modules:
  0.0 241.3 jit_solution(3195429282419334194)
XLA Ops:
  2.5 3.1 %dynamic-slice_bitcast_fusion.1 = (f32[2,256,512]{2,1,0:T(8,128)S(1)}, f32[2,256,512]{2,1,0:T(8,128)S(1)}, f32[2,256,512]{2,1,0:T(8,128)}) fusion(f32[256,100,512]{2,0,1:T(8,128)} %param.4, s32[]{:T(128)S(6)} %select_n.78, s32[]{:T(128)S(6)} %select_n.77, s32[]{:T(128)S(6)} %select_n.91), kind=kLoop, calls=%fused_computation.2 | loop fusion | bytes 6291468 | tf_op jit(solution)/shard_map/dynamic_slice | solution.py:150
  5.6 5.0 %collective-permute-start.2 = (f32[2,256,512]{2,1,0:T(8,128)S(1)}, f32[2,256,512]{2,1,0:T(8,128)S(1)}, u32[]{:S(2)}, u32[]{:S(2)}) collective-permute-start(f32[2,256,512]{2,1,0:T(8,128)S(1)} %get-tuple-element.52), channel_id=1, source_target_pairs={{0,2},{6,4},{1,3},{7,5},{8,10},{14,12},{9,11},{15,13},{16,18},{22,... | collective-permute-start | bytes 3145736 | tf_op jit(solution)/shard_map/ppermute | solution.py:101
  11.4 11.6 %collective-permute-done.1.refs_2_ = f32[6,256,128]{2,1,0:T(8,128)S(1)} collective-permute-done((f32[6,256,128]{2,1,0:T(8,128)S(1)}, f32[6,256,128]{2,1,0:T(8,128)S(1)}, u32[]{:S(2)}, u32[]{:S(2)}) %collective-permute-start.1) | collective-permute-done | bytes 786464 | tf_op jit(solution)/shard_map/ppermute | solution.py:101
  25.1 1.6 collective-permute-start.5
  26.7 5.3 %collective-permute-start.7 = (f32[2,256,512]{2,1,0:T(8,128)S(1)}, f32[2,256,512]{2,1,0:T(8,128)S(1)}, u32[]{:S(2)}, u32[]{:S(2)}) collective-permute-start(f32[2,256,512]{2,1,0:T(8,128)S(1)} %get-tuple-element.51), channel_id=1, source_target_pairs={{0,2},{6,4},{1,3},{7,5},{8,10},{14,12},{9,11},{15,13},{16,18},{22,... | collective-permute-start | bytes 3145736 | tf_op jit(solution)/shard_map/ppermute | solution.py:101
  34.3 22.0 %collective-permute-start.3 = (f32[6,256,128]{2,1,0:T(8,128)S(1)}, f32[6,256,128]{2,1,0:T(8,128)}, u32[]{:S(2)}, u32[]{:S(2)}) collective-permute-start(f32[6,256,128]{2,1,0:T(8,128)S(1)} %slice.62.refs_0_), channel_id=1, source_target_pairs={{0,2},{6,4},{1,3},{7,5},{8,10},{14,12},{9,11},{15,13},{16,18},{22,... | collective-permute-start | bytes 2359304 | tf_op jit(solution)/shard_map/ppermute | solution.py:101
  58.6 2.1 slice.63.refs_0_
  62.0 10.3 %collective-permute-done.3.refs_1_ = f32[6,256,128]{2,1,0:T(8,128)} collective-permute-done((f32[6,256,128]{2,1,0:T(8,128)S(1)}, f32[6,256,128]{2,1,0:T(8,128)}, u32[]{:S(2)}, u32[]{:S(2)}) %collective-permute-start.3) | collective-permute-done | bytes 786464 | tf_op jit(solution)/shard_map/ppermute | solution.py:101
  72.3 4.5 %collective-permute-start.4 = (f32[7,256,128]{2,1,0:T(8,128)S(1)}, f32[7,256,128]{2,1,0:T(8,128)S(1)}, u32[]{:S(2)}, u32[]{:S(2)}) collective-permute-start(f32[7,256,128]{2,1,0:T(8,128)S(1)} %slice.61.refs_0_), channel_id=1, source_target_pairs={{0,2},{6,4},{1,3},{7,5},{8,10},{14,12},{9,11},{15,13},{16,18},{22,... | collective-permute-start | bytes 2752520 | tf_op jit(solution)/shard_map/ppermute | solution.py:101
  76.9 2.2 collective-permute-start.8
  80.0 1.6 collective-permute-start.11
  82.9 12.6 %collective-permute-done.10.refs_2_ = f32[6,256,128]{2,1,0:T(8,128)S(1)} collective-permute-done((f32[6,256,128]{2,1,0:T(8,128)}, f32[6,256,128]{2,1,0:T(8,128)S(1)}, u32[]{:S(2)}, u32[]{:S(2)}) %collective-permute-start.10) | collective-permute-done | bytes 786464 | tf_op jit(solution)/shard_map/ppermute | solution.py:101
  96.4 1.6 collective-permute-start.16
  98.0 14.4 %collective-permute-done.8.refs_1_ = f32[6,256,128]{2,1,0:T(8,128)} collective-permute-done((f32[6,256,128]{2,1,0:T(8,128)S(1)}, f32[6,256,128]{2,1,0:T(8,128)}, u32[]{:S(2)}, u32[]{:S(2)}) %collective-permute-start.8) | collective-permute-done | bytes 786464 | tf_op jit(solution)/shard_map/ppermute | solution.py:101
  113.7 1.6 collective-permute-start.18
  116.2 9.8 %collective-permute-start.9 = (f32[6,256,128]{2,1,0:T(8,128)}, f32[6,256,128]{2,1,0:T(8,128)}, u32[]{:S(2)}, u32[]{:S(2)}) collective-permute-start(f32[6,256,128]{2,1,0:T(8,128)} %slice.63.refs_0_), channel_id=1, source_target_pairs={{0,2},{6,4},{1,3},{7,5},{8,10},{14,12},{9,11},{15,13},{16,18},{22,... | collective-permute-start | bytes 2359304 | tf_op jit(solution)/shard_map/ppermute | solution.py:101
  135.7 5.7 %shard_map.37.refs_6_ = f32[3,128,512]{2,1,0:T(8,128)S(1)} custom-call(s32[1]{0:T(128)} %bitcast.6.offset_ref, f32[6,256,128]{2,1,0:T(8,128)S(1)} %slice.60.refs_0_, f32[6,256,128]{2,1,0:T(8,128)} %collective-permute-done.8.refs_1_, f32[6,256,128]{2,1,0:T(8,128)S(1)} %copy-done.7, f32[6,256,128]{2,1,0:T(8,128)S(1)} %copy-done.13, ...), custom_call_target="tpu_custom_call" | custom-call | flops 1811939328 | bytes 8650752 | tf_op jit(solution)/shard_map/pallas_call | solution.py:72
  143.4 10.0 %collective-permute-start.29 = (f32[2,256,512]{2,1,0:T(8,128)S(1)}, f32[2,256,512]{2,1,0:T(8,128)S(1)}, u32[]{:S(2)}, u32[]{:S(2)}) collective-permute-start(f32[2,256,512]{2,1,0:T(8,128)S(1)} %copy-done.16), channel_id=1, source_target_pairs={{0,2},{6,4},{1,3},{7,5},{8,10},{14,12},{9,11},{15,13},{16,18},{22,... | collective-permute-start | bytes 3145736 | tf_op jit(solution)/shard_map/ppermute | solution.py:101
  154.8 6.1 %shard_map.38.refs_6_ = f32[3,128,512]{2,1,0:T(8,128)S(1)} custom-call(s32[1]{0:T(128)} %bitcast.5.offset_ref, f32[6,256,128]{2,1,0:T(8,128)S(1)} %slice.62.refs_0_, f32[6,256,128]{2,1,0:T(8,128)} %collective-permute-done.3.refs_1_, f32[6,256,128]{2,1,0:T(8,128)S(1)} %copy-done.9, ...), custom_call_target="tpu_custom_call", output_to_operand_aliasing={{}: (7, {})} | custom-call | flops 1811939328 | bytes 8650752 | tf_op jit(solution)/shard_map/pallas_call | solution.py:72
  160.9 6.2 %shard_map.39.refs_4_ = f32[3,128,512]{2,1,0:T(8,128)S(1)} custom-call(s32[1]{0:T(128)} %bitcast.3.offset_ref, f32[6,256,128]{2,1,0:T(8,128)} %slice.63.refs_0_, f32[6,256,128]{2,1,0:T(8,128)} %collective-permute-done.9.refs_1_, f32[6,256,128]{2,1,0:T(8,128)S(1)} %copy-done.11, ...), custom_call_target="tpu_custom_call", output_to_operand_aliasing={{}: (7, {})} | custom-call | flops 1811939328 | bytes 8650752 | tf_op jit(solution)/shard_map/pallas_call | solution.py:72
  167.1 6.4 %shard_map.40 = f32[3,128,512]{2,1,0:T(8,128)S(1)} custom-call(s32[1]{0:T(128)} %bitcast.offset_ref, f32[7,256,128]{2,1,0:T(8,128)S(1)} %slice.61.refs_0_, f32[7,256,128]{2,1,0:T(8,128)S(1)} %copy-done.5, f32[7,256,128]{2,1,0:T(8,128)S(1)} %collective-permute-done.6.refs_2_, f32[100,256,512]{2,1,0:T(8,128)} %bitcast.61, ...), custom_call_target="tpu_custom_call", output_to_operand_aliasing={{}: (5, {})} | custom-call | flops 2113929216 | bytes 7995392 | tf_op jit(solution)/shard_map/pallas_call | solution.py:72
  173.5 4.6 %collective-permute-start.28 = (f32[1,256,512]{2,1,0:T(8,128)S(1)}, f32[1,256,512]{2,1,0:T(8,128)S(1)}, u32[]{:S(2)}, u32[]{:S(2)}) collective-permute-start(f32[1,256,512]{2,1,0:T(8,128)S(1)} %dynamic-slice_bitcast_fusion.4), channel_id=1, source_target_pairs={{0,2},{6,4},{1,3},{7,5},{8,10},{14,12},{9,11},{15,13},{16,18},{22,... | collective-permute-start | bytes 1572872 | tf_op jit(solution)/shard_map/ppermute | solution.py:101
  179.6 4.9 %shard_map.41.refs_3_ = f32[1,128,512]{2,1,0:T(8,128)S(1)} custom-call(s32[1]{0:T(128)} %bitcast.6.offset_ref, f32[6,256,128]{2,1,0:T(8,128)} %collective-permute-done.18.refs_0_, f32[6,256,128]{2,1,0:T(8,128)S(1)} %collective-permute-done.22.refs_1_, f32[100,256,512]{2,1,0:T(8,128)} %bitcast.62), custom_call_target="tpu_custom_call" | custom-call | flops 603979776 | bytes 5242880 | tf_op jit(solution)/shard_map/pallas_call | solution.py:72
  186.8 4.8 %shard_map.42.refs_3_ = f32[1,128,512]{2,1,0:T(8,128)S(1)} custom-call(s32[1]{0:T(128)} %bitcast.5.offset_ref, f32[6,256,128]{2,1,0:T(8,128)} %collective-permute-done.16.refs_0_, f32[6,256,128]{2,1,0:T(8,128)S(1)} %collective-permute-done.20.refs_1_, f32[100,256,512]{2,1,0:T(8,128)} %bitcast.63, ...), custom_call_target="tpu_custom_call", output_to_operand_aliasing={{}: (4, {})} | custom-call | flops 603979776 | bytes 5242880 | tf_op jit(solution)/shard_map/pallas_call | solution.py:72
  196.8 3.2 %shard_map.43.refs_3_ = f32[1,128,512]{2,1,0:T(8,128)S(1)} custom-call(s32[1]{0:T(128)} %bitcast.3.offset_ref, f32[4,256,128]{2,1,0:T(8,128)S(1)} %slice.79.refs_0_, f32[4,256,128]{2,1,0:T(8,128)S(1)} %collective-permute-done.23.refs_1_, f32[100,256,512]{2,1,0:T(8,128)} %bitcast.64, f32[1,128,512]{2,1,0:T(8,128)S(1)} %shard_map.42.refs_3_), custom_call_target="tpu_custom_call", output_to_operand_aliasing={{}: (4, {})} | custom-call | flops 402653184 | bytes 3670016 | tf_op jit(solution)/shard_map/pallas_call | solution.py:72
  200.0 1.8 shard_map.44.refs_2_
  201.8 5.6 %shard_map.45 = f32[1,128,512]{2,1,0:T(8,128)S(1)} custom-call(s32[1]{0:T(128)} %bitcast.offset_ref, f32[7,256,128]{2,1,0:T(8,128)S(1)} %collective-permute-done.17.refs_0_, f32[100,256,512]{2,1,0:T(8,128)} %bitcast.66, f32[1,128,512]{2,1,0:T(8,128)S(1)} %shard_map.44.refs_2_), custom_call_target="tpu_custom_call", output_to_operand_aliasing={{}: (3, {})} | custom-call | flops 704643072 | bytes 5111808 | tf_op jit(solution)/shard_map/pallas_call | solution.py:72
  222.6 2.0 collective-permute-start.31
  226.3 2.0 collective-permute-start.25
  229.8 2.1 collective-permute-start.27
  231.9 1.7 collective-permute-done.32
  238.2 2.4 collective-permute-done.34
  (112 shorter events, 46.7 us)
Async XLA Ops:
  1.2 21.8 %collective-permute-start.1 = (f32[6,256,128]{2,1,0:T(8,128)S(1)}, f32[6,256,128]{2,1,0:T(8,128)S(1)}, u32[]{:S(2)}, u32[]{:S(2)}) collective-permute-start(f32[6,256,128]{2,1,0:T(8,128)S(1)} %slice.60.refs_0_), channel_id=1, source_target_pairs={{2,0},{4,6},{3,1},{5,7},{10,8},{12,14},{11,9},{13,15},{18,16},{20,... | collective-permute-start | bytes 2359304 | tf_op jit(solution)/shard_map/ppermute | solution.py:101
  5.6 28.7 %collective-permute-start.2 = (f32[2,256,512]{2,1,0:T(8,128)S(1)}, f32[2,256,512]{2,1,0:T(8,128)S(1)}, u32[]{:S(2)}, u32[]{:S(2)}) collective-permute-start(f32[2,256,512]{2,1,0:T(8,128)S(1)} %get-tuple-element.52), channel_id=1, source_target_pairs={{0,2},{6,4},{1,3},{7,5},{8,10},{14,12},{9,11},{15,13},{16,18},{22,... | collective-permute-start | bytes 3145736 | tf_op jit(solution)/shard_map/ppermute | solution.py:101
  10.7 21.3 %collective-permute-start = (f32[6,256,128]{2,1,0:T(8,128)S(1)}, f32[6,256,128]{2,1,0:T(8,128)S(1)}, u32[]{:S(2)}, u32[]{:S(2)}) collective-permute-start(f32[6,256,128]{2,1,0:T(8,128)S(1)} %slice.60.refs_0_), channel_id=1, source_target_pairs={{2,4},{4,2},{3,5},{5,3},{10,12},{12,10},{11,13},{13,11},{18,20},{2... | collective-permute-start | bytes 2359304 | tf_op jit(solution)/shard_map/ppermute | solution.py:101
  25.1 8.5 %collective-permute-start.5 = (f32[6,256,128]{2,1,0:T(8,128)S(1)}, f32[6,256,128]{2,1,0:T(8,128)}, u32[]{:S(2)}, u32[]{:S(2)}) collective-permute-start(f32[6,256,128]{2,1,0:T(8,128)S(1)} %slice.62.refs_0_), channel_id=1, source_target_pairs={{2,4},{4,2},{3,5},{5,3},{10,12},{12,10},{11,13},{13,11},{18,20},{2... | collective-permute-start | bytes 2359304 | tf_op jit(solution)/shard_map/ppermute | solution.py:101
  26.7 31.0 %collective-permute-start.7 = (f32[2,256,512]{2,1,0:T(8,128)S(1)}, f32[2,256,512]{2,1,0:T(8,128)S(1)}, u32[]{:S(2)}, u32[]{:S(2)}) collective-permute-start(f32[2,256,512]{2,1,0:T(8,128)S(1)} %get-tuple-element.51), channel_id=1, source_target_pairs={{0,2},{6,4},{1,3},{7,5},{8,10},{14,12},{9,11},{15,13},{16,18},{22,... | collective-permute-start | bytes 3145736 | tf_op jit(solution)/shard_map/ppermute | solution.py:101
  33.6 48.1 %collective-permute-start.6 = (f32[7,256,128]{2,1,0:T(8,128)S(1)}, f32[7,256,128]{2,1,0:T(8,128)S(1)}, u32[]{:S(2)}, u32[]{:S(2)}) collective-permute-start(f32[7,256,128]{2,1,0:T(8,128)S(1)} %slice.61.refs_0_), channel_id=1, source_target_pairs={{2,4},{4,2},{3,5},{5,3},{10,12},{12,10},{11,13},{13,11},{18,20},{2... | collective-permute-start | bytes 2752520 | tf_op jit(solution)/shard_map/ppermute | solution.py:101
  34.3 38.0 %collective-permute-start.3 = (f32[6,256,128]{2,1,0:T(8,128)S(1)}, f32[6,256,128]{2,1,0:T(8,128)}, u32[]{:S(2)}, u32[]{:S(2)}) collective-permute-start(f32[6,256,128]{2,1,0:T(8,128)S(1)} %slice.62.refs_0_), channel_id=1, source_target_pairs={{0,2},{6,4},{1,3},{7,5},{8,10},{14,12},{9,11},{15,13},{16,18},{22,... | collective-permute-start | bytes 2359304 | tf_op jit(solution)/shard_map/ppermute | solution.py:101
  56.3 22.7 %collective-permute-start.12 = (f32[6,256,128]{2,1,0:T(8,128)S(1)}, f32[6,256,128]{2,1,0:T(8,128)S(1)}, u32[]{:S(2)}, u32[]{:S(2)}) collective-permute-start(f32[6,256,128]{2,1,0:T(8,128)S(1)} %slice.62.refs_0_), channel_id=1, source_target_pairs={{2,0},{4,6},{3,1},{5,7},{10,8},{12,14},{11,9},{13,15},{18,16},{20,... | collective-permute-start | bytes 2359304 | tf_op jit(solution)/shard_map/ppermute | solution.py:101
  60.7 34.8 %collective-permute-start.10 = (f32[6,256,128]{2,1,0:T(8,128)}, f32[6,256,128]{2,1,0:T(8,128)S(1)}, u32[]{:S(2)}, u32[]{:S(2)}) collective-permute-start(f32[6,256,128]{2,1,0:T(8,128)} %slice.63.refs_0_), channel_id=1, source_target_pairs={{2,0},{4,6},{3,1},{5,7},{10,8},{12,14},{11,9},{13,15},{18,16},{20,... | collective-permute-start | bytes 2359304 | tf_op jit(solution)/shard_map/ppermute | solution.py:101
  72.3 53.7 %collective-permute-start.4 = (f32[7,256,128]{2,1,0:T(8,128)S(1)}, f32[7,256,128]{2,1,0:T(8,128)S(1)}, u32[]{:S(2)}, u32[]{:S(2)}) collective-permute-start(f32[7,256,128]{2,1,0:T(8,128)S(1)} %slice.61.refs_0_), channel_id=1, source_target_pairs={{0,2},{6,4},{1,3},{7,5},{8,10},{14,12},{9,11},{15,13},{16,18},{22,... | collective-permute-start | bytes 2752520 | tf_op jit(solution)/shard_map/ppermute | solution.py:101
  76.9 35.5 %collective-permute-start.8 = (f32[6,256,128]{2,1,0:T(8,128)S(1)}, f32[6,256,128]{2,1,0:T(8,128)}, u32[]{:S(2)}, u32[]{:S(2)}) collective-permute-start(f32[6,256,128]{2,1,0:T(8,128)S(1)} %slice.60.refs_0_), channel_id=1, source_target_pairs={{0,2},{6,4},{1,3},{7,5},{8,10},{14,12},{9,11},{15,13},{16,18},{22,... | collective-permute-start | bytes 2359304 | tf_op jit(solution)/shard_map/ppermute | solution.py:101
  80.0 33.6 %collective-permute-start.11 = (f32[6,256,128]{2,1,0:T(8,128)}, f32[6,256,128]{2,1,0:T(8,128)}, u32[]{:S(2)}, u32[]{:S(2)}) collective-permute-start(f32[6,256,128]{2,1,0:T(8,128)} %slice.63.refs_0_), channel_id=1, source_target_pairs={{2,4},{4,2},{3,5},{5,3},{10,12},{12,10},{11,13},{13,11},{18,20},{2... | collective-permute-start | bytes 2359304 | tf_op jit(solution)/shard_map/ppermute | solution.py:101
  81.7 33.7 %collective-permute-start.13 = (f32[6,256,128]{2,1,0:T(8,128)S(1)}, f32[6,256,128]{2,1,0:T(8,128)S(1)}, u32[]{:S(2)}, u32[]{:S(2)}) collective-permute-start(f32[6,256,128]{2,1,0:T(8,128)S(1)} %collective-permute-done.refs_3_), channel_id=1, source_target_pairs={{2,0},{4,6},{3,1},{5,7},{10,8},{12,14},{11,9},{13,15},{18,16},{20,... | collective-permute-start | bytes 2359304 | tf_op jit(solution)/shard_map/ppermute | solution.py:101
  96.4 35.1 %collective-permute-start.16 = (f32[6,256,128]{2,1,0:T(8,128)}, f32[6,256,128]{2,1,0:T(8,128)}, u32[]{:S(2)}, u32[]{:S(2)}) collective-permute-start(f32[6,256,128]{2,1,0:T(8,128)} %collective-permute-done.3.refs_1_), channel_id=1, source_target_pairs={{2,4},{4,2},{3,5},{5,3},{10,12},{12,10},{11,13},{13,11},{18,20},{2... | collective-permute-start | bytes 2359304 | tf_op jit(solution)/shard_map/ppermute | solution.py:101
  112.4 29.0 %collective-permute-start.15 = (f32[6,256,128]{2,1,0:T(8,128)}, f32[6,256,128]{2,1,0:T(8,128)}, u32[]{:S(2)}, u32[]{:S(2)}) collective-permute-start(f32[6,256,128]{2,1,0:T(8,128)} %collective-permute-done.5.refs_3_), channel_id=1, source_target_pairs={{2,0},{4,6},{3,1},{5,7},{10,8},{12,14},{11,9},{13,15},{18,16},{20,... | collective-permute-start | bytes 2359304 | tf_op jit(solution)/shard_map/ppermute | solution.py:101
  113.7 27.7 %collective-permute-start.18 = (f32[6,256,128]{2,1,0:T(8,128)}, f32[6,256,128]{2,1,0:T(8,128)}, u32[]{:S(2)}, u32[]{:S(2)}) collective-permute-start(f32[6,256,128]{2,1,0:T(8,128)} %collective-permute-done.8.refs_1_), channel_id=1, source_target_pairs={{2,4},{4,2},{3,5},{5,3},{10,12},{12,10},{11,13},{13,11},{18,20},{2... | collective-permute-start | bytes 2359304 | tf_op jit(solution)/shard_map/ppermute | solution.py:101
  116.2 26.5 %collective-permute-start.9 = (f32[6,256,128]{2,1,0:T(8,128)}, f32[6,256,128]{2,1,0:T(8,128)}, u32[]{:S(2)}, u32[]{:S(2)}) collective-permute-start(f32[6,256,128]{2,1,0:T(8,128)} %slice.63.refs_0_), channel_id=1, source_target_pairs={{0,2},{6,4},{1,3},{7,5},{8,10},{14,12},{9,11},{15,13},{16,18},{22,... | collective-permute-start | bytes 2359304 | tf_op jit(solution)/shard_map/ppermute | solution.py:101
  126.9 26.5 %collective-permute-start.14 = (f32[6,256,128]{2,1,0:T(8,128)}, f32[6,256,128]{2,1,0:T(8,128)}, u32[]{:S(2)}, u32[]{:S(2)}) collective-permute-start(f32[6,256,128]{2,1,0:T(8,128)} %collective-permute-done.11.refs_3_), channel_id=1, source_target_pairs={{2,0},{4,6},{3,1},{5,7},{10,8},{12,14},{11,9},{13,15},{18,16},{20,... | collective-permute-start | bytes 2359304 | tf_op jit(solution)/shard_map/ppermute | solution.py:101
  131.6 60.1 %collective-permute-start.17 = (f32[7,256,128]{2,1,0:T(8,128)}, f32[7,256,128]{2,1,0:T(8,128)S(1)}, u32[]{:S(2)}, u32[]{:S(2)}) collective-permute-start(f32[7,256,128]{2,1,0:T(8,128)} %copy-done.4), channel_id=1, source_target_pairs={{2,4},{4,2},{3,5},{5,3},{10,12},{12,10},{11,13},{13,11},{18,20},{2... | collective-permute-start | bytes 2752520 | tf_op jit(solution)/shard_map/ppermute | solution.py:101
  141.4 36.9 %collective-permute-start.22 = (f32[6,256,128]{2,1,0:T(8,128)}, f32[6,256,128]{2,1,0:T(8,128)S(1)}, u32[]{:S(2)}, u32[]{:S(2)}) collective-permute-start(f32[6,256,128]{2,1,0:T(8,128)} %collective-permute-done.18.refs_0_), channel_id=1, source_target_pairs={{2,0},{4,6},{3,1},{5,7},{10,8},{12,14},{11,9},{13,15},{18,16},{20,... | collective-permute-start | bytes 2359304 | tf_op jit(solution)/shard_map/ppermute | solution.py:101
  142.7 30.8 %collective-permute-start.19 = (f32[6,256,128]{2,1,0:T(8,128)}, f32[6,256,128]{2,1,0:T(8,128)S(1)}, u32[]{:S(2)}, u32[]{:S(2)}) collective-permute-start(f32[6,256,128]{2,1,0:T(8,128)} %collective-permute-done.9.refs_1_), channel_id=1, source_target_pairs={{2,4},{4,2},{3,5},{5,3},{10,12},{12,10},{11,13},{13,11},{18,20},{2... | collective-permute-start | bytes 2359304 | tf_op jit(solution)/shard_map/ppermute | solution.py:101
  143.4 50.7 %collective-permute-start.29 = (f32[2,256,512]{2,1,0:T(8,128)S(1)}, f32[2,256,512]{2,1,0:T(8,128)S(1)}, u32[]{:S(2)}, u32[]{:S(2)}) collective-permute-start(f32[2,256,512]{2,1,0:T(8,128)S(1)} %copy-done.16), channel_id=1, source_target_pairs={{0,2},{6,4},{1,3},{7,5},{8,10},{14,12},{9,11},{15,13},{16,18},{22,... | collective-permute-start | bytes 3145736 | tf_op jit(solution)/shard_map/ppermute | solution.py:101
  153.4 32.1 %collective-permute-start.20 = (f32[6,256,128]{2,1,0:T(8,128)}, f32[6,256,128]{2,1,0:T(8,128)S(1)}, u32[]{:S(2)}, u32[]{:S(2)}) collective-permute-start(f32[6,256,128]{2,1,0:T(8,128)} %collective-permute-done.16.refs_0_), channel_id=1, source_target_pairs={{2,0},{4,6},{3,1},{5,7},{10,8},{12,14},{11,9},{13,15},{18,16},{20,... | collective-permute-start | bytes 2359304 | tf_op jit(solution)/shard_map/ppermute | solution.py:101
  173.5 21.7 %collective-permute-start.28 = (f32[1,256,512]{2,1,0:T(8,128)S(1)}, f32[1,256,512]{2,1,0:T(8,128)S(1)}, u32[]{:S(2)}, u32[]{:S(2)}) collective-permute-start(f32[1,256,512]{2,1,0:T(8,128)S(1)} %dynamic-slice_bitcast_fusion.4), channel_id=1, source_target_pairs={{0,2},{6,4},{1,3},{7,5},{8,10},{14,12},{9,11},{15,13},{16,18},{22,... | collective-permute-start | bytes 1572872 | tf_op jit(solution)/shard_map/ppermute | solution.py:101
  178.2 18.5 %collective-permute-start.23 = (f32[4,256,128]{2,1,0:T(8,128)S(1)}, f32[4,256,128]{2,1,0:T(8,128)S(1)}, u32[]{:S(2)}, u32[]{:S(2)}) collective-permute-start(f32[4,256,128]{2,1,0:T(8,128)S(1)} %slice.79.refs_0_), channel_id=1, source_target_pairs={{2,0},{4,6},{3,1},{5,7},{10,8},{12,14},{11,9},{13,15},{18,16},{20,... | collective-permute-start | bytes 1572872 | tf_op jit(solution)/shard_map/ppermute | solution.py:101
  185.5 14.5 %collective-permute-start.21 = (f32[2,256,128]{2,1,0:T(8,128)S(1)}, f32[2,256,128]{2,1,0:T(8,128)S(1)}, u32[]{:S(2)}, u32[]{:S(2)}) collective-permute-start(f32[2,256,128]{2,1,0:T(8,128)S(1)} %slice.78.refs_0_), channel_id=1, source_target_pairs={{2,0},{4,6},{3,1},{5,7},{10,8},{12,14},{11,9},{13,15},{18,16},{20,... | collective-permute-start | bytes 786440 | tf_op jit(solution)/shard_map/ppermute | solution.py:101
  196.8 25.7 %collective-permute-start.30 = (f32[4,64,512]{2,1,0:T(8,128)}, f32[4,64,512]{2,1,0:T(8,128)S(1)}, u32[]{:S(2)}, u32[]{:S(2)}) collective-permute-start(f32[4,64,512]{2,1,0:T(8,128)} %dynamic-slice_bitcast_fusion.3), channel_id=1, source_target_pairs={{0,1},{1,0},{2,3},{3,2},{4,5},{5,4},{6,7},{7,6},{8,9},{9,8},{10,11... | collective-permute-start | bytes 1572872 | tf_op jit(solution)/shard_map/ppermute | solution.py:180
  208.3 17.8 %collective-permute-start.24 = (f32[4,64,512]{2,1,0:T(8,128)}, f32[4,64,512]{2,1,0:T(8,128)S(1)}, u32[]{:S(2)}, u32[]{:S(2)}) collective-permute-start(f32[4,64,512]{2,1,0:T(8,128)} %dynamic-slice_bitcast_fusion.5), channel_id=1, source_target_pairs={{0,1},{1,0},{2,3},{3,2},{4,5},{5,4},{6,7},{7,6},{8,9},{9,8},{10,11... | collective-permute-start | bytes 1572872 | tf_op jit(solution)/shard_map/ppermute | solution.py:180
  224.6 9.0 %collective-permute-start.32 = (f32[64,512]{1,0:T(8,128)S(1)}, f32[64,512]{1,0:T(8,128)S(1)}, u32[]{:S(2)}, u32[]{:S(2)}) collective-permute-start(f32[64,512]{1,0:T(8,128)S(1)} %get-tuple-element.68), channel_id=1, source_target_pairs={{0,16},{8,24},{16,0},{24,8},{1,17},{9,25},{17,1},{25,9},{2,18},{10... | collective-permute-start | bytes 393224 | tf_op jit(solution)/shard_map/ppermute | solution.py:186
  226.3 10.6 %collective-permute-start.25 = (f32[64,512]{1,0:T(8,128)S(1)}, f32[64,512]{1,0:T(8,128)S(1)}, u32[]{:S(2)}, u32[]{:S(2)}) collective-permute-start(f32[64,512]{1,0:T(8,128)S(1)} %get-tuple-element.63), channel_id=1, source_target_pairs={{0,8},{8,0},{16,24},{24,16},{1,9},{9,1},{17,25},{25,17},{2,10},{10... | collective-permute-start | bytes 393224 | tf_op jit(solution)/shard_map/ppermute | solution.py:186
  228.3 9.9 %collective-permute-start.26 = (f32[64,512]{1,0:T(8,128)S(1)}, f32[64,512]{1,0:T(8,128)S(1)}, u32[]{:S(2)}, u32[]{:S(2)}) collective-permute-start(f32[64,512]{1,0:T(8,128)S(1)} %get-tuple-element.65), channel_id=1, source_target_pairs={{0,16},{8,24},{16,0},{24,8},{1,17},{9,25},{17,1},{25,9},{2,18},{10... | collective-permute-start | bytes 393224 | tf_op jit(solution)/shard_map/ppermute | solution.py:186
  229.8 8.3 %collective-permute-start.27 = (f32[64,512]{1,0:T(8,128)S(1)}, f32[64,512]{1,0:T(8,128)S(1)}, u32[]{:S(2)}, u32[]{:S(2)}) collective-permute-start(f32[64,512]{1,0:T(8,128)S(1)} %get-tuple-element.64), channel_id=1, source_target_pairs={{0,24},{8,16},{16,8},{24,0},{1,25},{9,17},{17,9},{25,1},{2,26},{10... | collective-permute-start | bytes 393224 | tf_op jit(solution)/shard_map/ppermute | solution.py:186
  (21 other events, 329.8 us)

commit v4 on v3

v4 whole, which is shorter than its diff:
```python
import functools

import jax
import jax.numpy as jnp
from jax import lax
from jax.experimental import pallas as pl
from jax.experimental.pallas import tpu as pltpu
from jax.sharding import PartitionSpec as P

LINE = 4


def after(value, *earlier):
    return lax.optimization_barrier((value,) + earlier)[0]


def bounds(start, *sizes):
    ends = [start + sum(sizes[: i + 1]) for i in range(len(sizes))]
    return [(stop - size, stop) for stop, size in zip(ends, sizes) if size > 0]


def parts(value):
    high = value.astype(jnp.bfloat16)
    return high, (value - high.astype(jnp.float32)).astype(jnp.bfloat16)


def contract_kernel(terms, per, first, offset_ref, *refs):
    del offset_ref
    out_ref = refs[-1]
    weight_refs = refs[sum(terms) : sum(terms) + per]

    @pl.when(pl.program_id(0) == 0)
    def _():
        out_ref[...] = jnp.zeros_like(out_ref) if first else refs[sum(terms) + per][...]

    left, right = [], []
    for j in range(per):
        highs, lows, at = [], [], 0
        for n in terms:
            value = refs[at][j]
            for ref in refs[at + 1 : at + n]:
                value = value + ref[j]
            at += n
            high, low = parts(value)
            highs.append(high)
            lows.append(low)
        highs = jnp.concatenate(highs, axis=1)
        left += [highs, highs, jnp.concatenate(lows, axis=1)]
        high, low = parts(weight_refs[j][0])
        right += [high, low, high]
    product = lax.dot_general(
        jnp.concatenate(left, axis=0),
        jnp.concatenate(right, axis=0),
        (((0,), (0,)), ((), ())),
        preferred_element_type=jnp.float32,
    )
    out_ref[...] += product.reshape(out_ref.shape)


def contract(slots, weights, offset, total):
    terms = [len(slot) for slot in slots]
    steps, depth, block = slots[0][0].shape
    width = weights.shape[2]
    per = max(n for n in (1, 2, 3) if steps % n == 0)
    shape = (len(slots), block, width)
    whole = pl.BlockSpec(shape, lambda i, o: (0, 0, 0))
    in_specs = [pl.BlockSpec((per, depth, block), lambda i, o: (i, 0, 0))] * sum(terms)
    for j in range(per):
        in_specs.append(pl.BlockSpec((1, depth, width), lambda i, o, j=j: (o[0] + per * i + j, 0, 0)))
    operands = [a for slot in slots for a in slot] + [weights] * per
    aliases = {}
    if total is not None:
        in_specs.append(whole)
        aliases = {len(operands) + 1: 0}
        operands.append(total)
    return pl.pallas_call(
        functools.partial(contract_kernel, terms, per, total is None),
        out_shape=jax.ShapeDtypeStruct(shape, jnp.float32),
        grid_spec=pltpu.PrefetchScalarGridSpec(
            num_scalar_prefetch=1, grid=(steps // per,), in_specs=in_specs, out_specs=whole
        ),
        input_output_aliases=aliases,
        compiler_params=pltpu.CompilerParams(vmem_limit_bytes=40 << 20),
        cost_estimate=pl.CostEstimate(
            flops=6 * steps * depth * len(slots) * block * width,
            bytes_accessed=4 * (steps * depth * (width + sum(terms) * block) + 2 * len(slots) * block * width),
            transcendentals=0,
        ),
    )(jnp.reshape(offset, (1,)).astype(jnp.int32), *operands)


def shards(amplitude, integral, rows, cols, layers):
    ko = amplitude.shape[0]
    group = cols // LINE
    row, col, layer = (lax.axis_index(name) for name in ("row", "col", "depth"))
    if group > 1:
        groups = [[z * group + lane for lane in range(group)] for z in range(LINE)]
        amplitude = lax.all_gather(amplitude, "col", axis=2, axis_index_groups=groups, tiled=True)
    place = col // group
    block, width = amplitude.shape[2], integral.shape[2]
    integral = jnp.transpose(integral, (1, 0, 2))

    def hop(pairs):
        lanes = [(a * group + lane, b * group + lane) for a, b in pairs for lane in range(group)]
        return lambda value: lax.ppermute(value, "col", lanes)

    inward, across, outward = hop([(0, 1), (3, 2)]), hop([(1, 2), (2, 1)]), hop([(1, 0), (2, 3)])

    lent = round(ko * 2 * block / (3 * block + width))
    base = ko - lent
    main = bounds(0, base - base // 2, base // 2)
    extra = (base, ko)
    sizes = [lent // 4 + (i + lent % 4 >= 4) for i in range(4)]
    pieces = bounds(base, sizes[1], sizes[0], *sizes[2:])
    last = main[-1]
    size = last[1] - last[0]
    tail = bounds(last[0], size - size // 3, size // 3)

    own = {main[0]: amplitude[: main[0][1]]}
    later = after(amplitude, own[main[0]])
    for c in main[1:] + [extra]:
        own[c] = later[c[0] : c[1]]
    same_in, far_inner, far_end = {}, {}, {}
    out_same, out_inner, out_end, lent_weights = {}, {}, {}, {}

    sends = {"out": [], "across": [], "in": []}
    early = len(pieces) // 2
    sends["in"] += [(lent_weights, c, None, inward) for c in pieces[:early]]
    sends["in"] += [(same_in, c, own, inward) for c in main + [extra]]
    sends["in"] += [(lent_weights, c, None, inward) for c in pieces[early:]]
    sends["across"] += [(far_inner, c, own, across) for c in main + [extra]]
    sends["across"] += [(far_end, c, same_in, across) for c in main + [extra]]
    sends["out"] += [(out_same, c, own, outward) for c in main]
    sends["out"] += [(out_inner, c, far_inner, outward) for c in main]
    sends["out"] += [(out_end, c, far_end, outward) for c in main[:-1] + tail]

    def find(table, c):
        for (k0, k1), value in table.items():
            if k0 <= c[0] and c[1] <= k1:
                return value if (k0, k1) == c else value[c[0] - k0 : c[1] - k0]
        return None

    clock = dict.fromkeys(sends, 0)
    arrived = {name: [] for name in sends}
    while any(sends.values()):
        ready = [n for n in sends if sends[n]]
        ready = [n for n in ready if sends[n][0][2] is None or find(sends[n][0][2], sends[n][0][1]) is not None]
        name = min(ready, key=lambda n: clock[n])
        into, c, source, move = sends[name].pop(0)
        if source is None:
            value = lax.dynamic_slice_in_dim(integral, row * ko + c[0], c[1] - c[0], axis=0)
        else:
            value = find(source, c)
        if len(arrived[name]) >= 2:
            value = after(value, arrived[name][-2])
        into[c] = move(value)
        arrived[name].append(into[c])
        clock[name] += (c[1] - c[0]) * (width / block if source is None else 1)

    near, far, loan = None, None, None
    for c in main:
        slots = [[own[c]], [same_in[c], out_same[c]], [far_inner[c], out_inner[c]]]
        near = contract(slots, integral, row * ko + c[0], near)
    near = contract([[own[extra]], [same_in[extra]], [far_inner[extra]]], integral, row * ko + base, near)
    for c in main[:-1] + [extra] + tail:
        slots = [[find(far_end, c)] + ([out_end[c]] if c in out_end else [])]
        far = contract(slots, integral, row * ko + c[0], far)
    for c in pieces:
        slots = [[find(held, c)] for held in (own, far_inner, far_end)]
        loan = contract(slots, lent_weights[c], jnp.int32(0), loan)

    def layer_sum(blocks):
        halves = blocks.reshape(blocks.shape[0], layers, block // layers, width)
        if layers != 2:
            return lax.psum_scatter(halves, "depth", scatter_dimension=1, tiled=False)
        away = lax.dynamic_index_in_dim(halves, 1 - layer, 1, keepdims=False)
        mine = lax.dynamic_index_in_dim(halves, layer, 1, keepdims=False)
        return mine + lax.ppermute(away, "depth", [(0, 1), (1, 0)])

    inner = jnp.logical_or(place == 1, place == 2).astype(jnp.int32)

    def row_sum(halves, swapped):
        def part(target):
            mirrored = jnp.where(place < 2, target, 3 - target)
            slot = mirrored ^ (swapped * (mirrored < 2).astype(jnp.int32))
            return lax.dynamic_index_in_dim(halves, slot, 0, keepdims=False)

        total = part(row)
        for t in range(1, 4):
            total = total + lax.ppermute(part(row ^ t), "row", [(r, r ^ t) for r in range(4)])
        return total

    near = layer_sum(near)
    loan = layer_sum(loan)
    returned = outward(row_sum(jnp.concatenate([jnp.zeros_like(loan[:1]), loan]), 0))
    return row_sum(jnp.concatenate([near, layer_sum(far)]), inner) + returned


def solution(mesh):
    rows, cols, layers = (mesh.shape[name] for name in ("row", "col", "depth"))
    return jax.shard_map(
        lambda amplitude, integral: shards(amplitude, integral, rows, cols, layers),
        mesh=mesh,
        in_specs=(P("row", "depth", "col"), P("depth", None, "col")),
        out_specs=P(("row", "depth"), "col"),
        check_vma=False,
    )
```

time: 243 us -> 212 us (0.87)
  waiting for transfers between devices: 55.3 us -> 89.3 us
  starting transfers between devices: 96.6 us -> 65.9 us
  between operations: 15.6 us -> 0.56 us
  Pallas kernels: 48.7 us -> 36.2 us
  local copies, waits for them, and re-layouts: 24.1 us -> 18.3 us
    ppermute x27 -> x21, waiting for transfers between devices: 52.4 us -> 84.7 us  [hop(): return lambda value: lax.ppermute(value, 'col', lanes)]
    ppermute x27 -> x21, starting transfers between devices: 86.9 us -> 58.6 us  [hop(): return lambda value: lax.ppermute(value, 'col', lanes)]
    pallas_call x13 -> x11, Pallas kernels: 48.7 us -> 36.2 us  [contract(): pl.pallas_call(functools.partial(contract_kernel, terms, per, total is No...]
    unnamed x36 -> x20, local copies, waits for them, and re-layouts: 8.92 us -> 3.58 us
    slice x8, local copies, waits for them, and re-layouts: 2.26 us -> 7.34 us  [find(): return value if (k0, k1) == c else value[c[0] - k0:c[1] - k0]]
    slice x4 -> x3, local copies, waits for them, and re-layouts: 5.98 us -> 2.33 us  [the longest x2 2.25 us: shards(): own[c] = later[c[0]:c[1]]]
    ppermute x8 -> x9, starting transfers between devices: 9.71 us -> 7.32 us  [the longest x6 7.11 us: row_sum(): lax.ppermute(part(row ^ t), 'row', [(r, r ^ t) for r in range(4)])]
  transfers between devices with their start and end apart: 35 -> 30, of which waited for: 8 -> 15; matrix products, arithmetic and copies ran while one was open for 6% -> 5% of each run, Pallas kernels for 20% -> 17%
where the time goes in v4:
time: 212 us; the launch traced here: 211 us
  waiting for transfers between devices  89.3 us (42%)
  starting transfers between devices  65.9 us (31%)
  Pallas kernels  36.2 us (17%)
  local copies, waits for them, and re-layouts  18.3 us (9%)
    ppermute x21, waiting for transfers between devices, hop(): return lambda value: lax.ppermute(value, 'col', lanes)  84.7 us
    ppermute x21, starting transfers between devices, hop(): return lambda value: lax.ppermute(value, 'col', lanes)  58.6 us
    pallas_call x11, Pallas kernels, contract(): pl.pallas_call(functools.partial(contract_kernel, terms, per, total is No...  36.2 us
    slice x8, local copies, waits for them, and re-layouts, find(): return value if (k0, k1) == c else value[c[0] - k0:c[1] - k0]  7.34 us
    ppermute x6, starting transfers between devices, row_sum(): lax.ppermute(part(row ^ t), 'row', [(r, r ^ t) for r in range(4)])  7.11 us
    dynamic_slice x2, local copies, waits for them, and re-layouts, shards(): lax.dynamic_slice_in_dim(integral, row * ko + c[0], c[1] - c[0], axis=0)  4.87 us
    ppermute x6, waiting for transfers between devices, row_sum(): lax.ppermute(part(row ^ t), 'row', [(r, r ^ t) for r in range(4)])  4.54 us
  transfers between devices with their start and end apart: 30, of which 15 were waited for; matrix products, arithmetic and copies ran while one was open for 5% of the time, Pallas kernels for 17%

profile of v4, /device:TPU:0, one launch (start us, length us, event | category | flops | bytes accessed | tf_op | source)
XLA Modules:
  0.0 211.3 jit_solution(7270873135365093058)
XLA Ops:
  0.0 3.8 %dynamic-slice_bitcast_fusion = (f32[2,256,512]{2,1,0:T(8,128)}, f32[2,256,512]{2,1,0:T(8,128)}, f32[2,256,512]{2,1,0:T(8,128)}) fusion(f32[256,100,512]{2,0,1:T(8,128)} %param.3, s32[]{:T(128)S(6)} %select_n.81, s32[]{:T(128)S(6)} %select_n.68, s32[]{:T(128)S(6)} %select_n.80), kind=kLoop, calls=%fused_computation | loop fusion | bytes 6291468 | tf_op jit(solution)/shard_map/dynamic_slice | solution.py:151
  3.8 5.0 %collective-permute-start = (f32[2,256,512]{2,1,0:T(8,128)}, f32[2,256,512]{2,1,0:T(8,128)S(1)}, u32[]{:S(2)}, u32[]{:S(2)}) collective-permute-start(f32[2,256,512]{2,1,0:T(8,128)} %get-tuple-element.36), channel_id=1, source_target_pairs={{0,2},{6,4},{1,3},{7,5},{8,10},{14,12},{9,11},{15,13},{16,18},{22,... | collective-permute-start | bytes 3145736 | tf_op jit(solution)/shard_map/ppermute | solution.py:105
  9.0 1.7 collective-permute-start.8
  11.8 3.1 %collective-permute-start.5 = (f32[1,256,512]{2,1,0:T(8,128)S(1)}, f32[1,256,512]{2,1,0:T(8,128)S(1)}, u32[]{:S(2)}, u32[]{:S(2)}) collective-permute-start(f32[1,256,512]{2,1,0:T(8,128)S(1)} %dynamic-slice_bitcast_fusion.3), channel_id=1, source_target_pairs={{0,2},{6,4},{1,3},{7,5},{8,10},{14,12},{9,11},{15,13},{16,18},{22,... | collective-permute-start | bytes 1572872 | tf_op jit(solution)/shard_map/ppermute | solution.py:105
  14.8 17.8 %collective-permute-done.refs_3_.refs_4_ = f32[2,256,512]{2,1,0:T(8,128)S(1)} collective-permute-done((f32[2,256,512]{2,1,0:T(8,128)}, f32[2,256,512]{2,1,0:T(8,128)S(1)}, u32[]{:S(2)}, u32[]{:S(2)}) %collective-permute-start) | collective-permute-done | bytes 1048608 | tf_op jit(solution)/shard_map/ppermute | solution.py:105
  32.6 5.3 %collective-permute-start.1 = (f32[9,256,128]{2,1,0:T(8,128)S(1)}, f32[9,256,128]{2,1,0:T(8,128)}, u32[]{:S(2)}, u32[]{:S(2)}) collective-permute-start(f32[9,256,128]{2,1,0:T(8,128)S(1)} %slice.57.refs_0_), channel_id=1, source_target_pairs={{0,2},{6,4},{1,3},{7,5},{8,10},{14,12},{9,11},{15,13},{16,18},{22,... | collective-permute-start | bytes 3538952 | tf_op jit(solution)/shard_map/ppermute | solution.py:105
  37.9 1.7 collective-permute-start.3
  40.9 2.8 %collective-permute-done.5.refs_3_ = f32[1,256,512]{2,1,0:T(8,128)S(1)} collective-permute-done((f32[1,256,512]{2,1,0:T(8,128)S(1)}, f32[1,256,512]{2,1,0:T(8,128)S(1)}, u32[]{:S(2)}, u32[]{:S(2)}) %collective-permute-start.5) | collective-permute-done | bytes 524320 | tf_op jit(solution)/shard_map/ppermute | solution.py:105
  45.8 5.6 %collective-permute-start.6 = (f32[9,256,128]{2,1,0:T(8,128)S(1)}, f32[9,256,128]{2,1,0:T(8,128)}, u32[]{:S(2)}, u32[]{:S(2)}) collective-permute-start(f32[9,256,128]{2,1,0:T(8,128)S(1)} %slice.59.refs_0_), channel_id=1, source_target_pairs={{0,2},{6,4},{1,3},{7,5},{8,10},{14,12},{9,11},{15,13},{16,18},{22,... | collective-permute-start | bytes 3538952 | tf_op jit(solution)/shard_map/ppermute | solution.py:105
  51.4 17.5 %collective-permute-done.1.refs_1_ = f32[9,256,128]{2,1,0:T(8,128)} collective-permute-done((f32[9,256,128]{2,1,0:T(8,128)S(1)}, f32[9,256,128]{2,1,0:T(8,128)}, u32[]{:S(2)}, u32[]{:S(2)}) %collective-permute-start.1) | collective-permute-done | bytes 1179680 | tf_op jit(solution)/shard_map/ppermute | solution.py:105
  69.0 1.7 collective-permute-start.14
  70.7 2.2 %slice.58.refs_0_ = f32[7,256,128]{2,1,0:T(8,128)} slice(f32[25,256,128]{2,1,0:T(8,128)} %param.2), slice={[18:25], [0:256], [0:128]} | slice | bytes 1835008 | tf_op jit(solution)/shard_map/slice | solution.py:122
  76.8 18.8 %collective-permute-done.7.refs_2_ = f32[9,256,128]{2,1,0:T(8,128)S(1)} collective-permute-done((f32[9,256,128]{2,1,0:T(8,128)S(1)}, f32[9,256,128]{2,1,0:T(8,128)S(1)}, u32[]{:S(2)}, u32[]{:S(2)}) %collective-permute-start.7) | collective-permute-done | bytes 1179680 | tf_op jit(solution)/shard_map/ppermute | solution.py:105
  96.8 2.4 %collective-permute-start.2 = (f32[7,256,128]{2,1,0:T(8,128)}, f32[7,256,128]{2,1,0:T(8,128)}, u32[]{:S(2)}, u32[]{:S(2)}) collective-permute-start(f32[7,256,128]{2,1,0:T(8,128)} %slice.58.refs_0_), channel_id=1, source_target_pairs={{0,2},{6,4},{1,3},{7,5},{8,10},{14,12},{9,11},{15,13},{16,18},{22,... | collective-permute-start | bytes 2752520 | tf_op jit(solution)/shard_map/ppermute | solution.py:105
  100.5 1.7 collective-permute-start.13
  102.1 2.0 fusion.19
  105.2 7.7 %collective-permute-done.2.refs_1_ = f32[7,256,128]{2,1,0:T(8,128)} collective-permute-done((f32[7,256,128]{2,1,0:T(8,128)}, f32[7,256,128]{2,1,0:T(8,128)}, u32[]{:S(2)}, u32[]{:S(2)}) %collective-permute-start.2) | collective-permute-done | bytes 917536 | tf_op jit(solution)/shard_map/ppermute | solution.py:105
  112.9 14.9 %collective-permute-start.24 = (f32[2,256,512]{2,1,0:T(8,128)}, f32[2,256,512]{2,1,0:T(8,128)S(1)}, u32[]{:S(2)}, u32[]{:S(2)}) collective-permute-start(f32[2,256,512]{2,1,0:T(8,128)} %get-tuple-element.34), channel_id=1, source_target_pairs={{0,2},{6,4},{1,3},{7,5},{8,10},{14,12},{9,11},{15,13},{16,18},{22,... | collective-permute-start | bytes 3145736 | tf_op jit(solution)/shard_map/ppermute | solution.py:105
  130.6 2.9 %collective-permute-start.23 = (f32[2,256,512]{2,1,0:T(8,128)}, f32[2,256,512]{2,1,0:T(8,128)S(1)}, u32[]{:S(2)}, u32[]{:S(2)}) collective-permute-start(f32[2,256,512]{2,1,0:T(8,128)} %get-tuple-element.33), channel_id=1, source_target_pairs={{0,2},{6,4},{1,3},{7,5},{8,10},{14,12},{9,11},{15,13},{16,18},{22,... | collective-permute-start | bytes 3145736 | tf_op jit(solution)/shard_map/ppermute | solution.py:105
  133.6 5.9 %shard_map.28.refs_8_ = f32[3,128,512]{2,1,0:T(8,128)S(1)} custom-call(s32[1]{0:T(128)} %bitcast.5.offset_ref, f32[9,256,128]{2,1,0:T(8,128)S(1)} %slice.57.refs_0_, f32[9,256,128]{2,1,0:T(8,128)} %collective-permute-done.1.refs_1_, f32[9,256,128]{2,1,0:T(8,128)S(1)} %copy-done.3, f32[9,256,128]{2,1,0:T(8,128)} %collective-permute-done.3.refs_3_, ...), custom_call_target="tpu_custom_call" | custom-call | flops 2717908992 | bytes 12189696 | tf_op jit(solution)/shard_map/pallas_call | solution.py:76
  139.5 3.4 %collective-permute-done.9.refs_4_ = f32[9,256,128]{2,1,0:T(8,128)} collective-permute-done((f32[9,256,128]{2,1,0:T(8,128)}, f32[9,256,128]{2,1,0:T(8,128)}, u32[]{:S(2)}, u32[]{:S(2)}) %collective-permute-start.9) | collective-permute-done | bytes 1179680 | tf_op jit(solution)/shard_map/ppermute | solution.py:105
  144.2 5.9 %shard_map.29.refs_4_ = f32[3,128,512]{2,1,0:T(8,128)S(1)} custom-call(s32[1]{0:T(128)} %bitcast.3.offset_ref, f32[9,256,128]{2,1,0:T(8,128)S(1)} %slice.59.refs_0_, f32[9,256,128]{2,1,0:T(8,128)} %collective-permute-done.6.refs_1_, f32[9,256,128]{2,1,0:T(8,128)S(1)} %copy-done.1, ...), custom_call_target="tpu_custom_call", output_to_operand_aliasing={{}: (9, {})} | custom-call | flops 2717908992 | bytes 12189696 | tf_op jit(solution)/shard_map/pallas_call | solution.py:76
  150.1 7.1 %shard_map.30 = f32[3,128,512]{2,1,0:T(8,128)S(1)} custom-call(s32[1]{0:T(128)} %bitcast.offset_ref, f32[7,256,128]{2,1,0:T(8,128)} %slice.58.refs_0_, f32[7,256,128]{2,1,0:T(8,128)} %collective-permute-done.2.refs_1_, f32[7,256,128]{2,1,0:T(8,128)} %collective-permute-done.4.refs_2_, f32[100,256,512]{2,1,0:T(8,128)} %bitcast.70, ...), custom_call_target="tpu_custom_call", output_to_operand_aliasing={{}: (5, {})} | custom-call | flops 2113929216 | bytes 7995392 | tf_op jit(solution)/shard_map/pallas_call | solution.py:76
  163.8 5.9 %collective-permute-done.23.refs_3_.refs_4_ = f32[2,256,512]{2,1,0:T(8,128)S(1)} collective-permute-done((f32[2,256,512]{2,1,0:T(8,128)}, f32[2,256,512]{2,1,0:T(8,128)S(1)}, u32[]{:S(2)}, u32[]{:S(2)}) %collective-permute-start.23) | collective-permute-done | bytes 1048608 | tf_op jit(solution)/shard_map/ppermute | solution.py:105
  170.7 3.2 %collective-permute-done.15.refs_1_ = f32[9,256,128]{2,1,0:T(8,128)S(1)} collective-permute-done((f32[9,256,128]{2,1,0:T(8,128)}, f32[9,256,128]{2,1,0:T(8,128)S(1)}, u32[]{:S(2)}, u32[]{:S(2)}) %collective-permute-start.15) | collective-permute-done | bytes 1179680 | tf_op jit(solution)/shard_map/ppermute | solution.py:105
  175.2 4.2 %shard_map.31.refs_2_ = f32[1,128,512]{2,1,0:T(8,128)S(1)} custom-call(s32[1]{0:T(128)} %bitcast.5.offset_ref, f32[9,256,128]{2,1,0:T(8,128)} %collective-permute-done.14.refs_0_, f32[9,256,128]{2,1,0:T(8,128)S(1)} %collective-permute-done.15.refs_1_, f32[100,256,512]{2,1,0:T(8,128)} %bitcast.71, f32[100,256,512]{2,1,0:T(8,128)} %bitcast.72, ...), custom_call_target="tpu_custom_call" | custom-call | flops 905969664 | bytes 7602176 | tf_op jit(solution)/shard_map/pallas_call | solution.py:76
  179.4 5.6 %shard_map.32.refs_5_ = f32[1,128,512]{2,1,0:T(8,128)S(1)} custom-call(s32[1]{0:T(128)} %bitcast.offset_ref, f32[7,256,128]{2,1,0:T(8,128)S(1)} %collective-permute-done.18.refs_0_, f32[100,256,512]{2,1,0:T(8,128)} %bitcast.74, f32[1,128,512]{2,1,0:T(8,128)S(1)} %shard_map.31.refs_2_), custom_call_target="tpu_custom_call", output_to_operand_aliasing={{}: (3, {})} | custom-call | flops 704643072 | bytes 5111808 | tf_op jit(solution)/shard_map/pallas_call | solution.py:76
  185.0 5.6 %collective-permute-done.17.refs_1_ = f32[6,256,128]{2,1,0:T(8,128)S(1)} collective-permute-done((f32[6,256,128]{2,1,0:T(8,128)S(1)}, f32[6,256,128]{2,1,0:T(8,128)S(1)}, u32[]{:S(2)}, u32[]{:S(2)}) %collective-permute-start.17) | collective-permute-done | bytes 786464 | tf_op jit(solution)/shard_map/ppermute | solution.py:105
  190.7 2.6 %shard_map.33.refs_5_ = f32[1,128,512]{2,1,0:T(8,128)S(1)} custom-call(s32[1]{0:T(128)} %bitcast.3.offset_ref, f32[6,256,128]{2,1,0:T(8,128)S(1)} %slice.75.refs_0_, f32[6,256,128]{2,1,0:T(8,128)S(1)} %collective-permute-done.17.refs_1_, f32[100,256,512]{2,1,0:T(8,128)} %bitcast.75, f32[100,256,512]{2,1,0:T(8,128)} %bitcast.76, ...), custom_call_target="tpu_custom_call", output_to_operand_aliasing={{}: (6, {})} | custom-call | flops 603979776 | bytes 5242880 | tf_op jit(solution)/shard_map/pallas_call | solution.py:76
  193.5 2.5 %collective-permute-start.28 = (f32[64,512]{1,0:T(8,128)S(1)}, f32[64,512]{1,0:T(8,128)S(1)}, u32[]{:S(2)}, u32[]{:S(2)}) collective-permute-start(f32[64,512]{1,0:T(8,128)S(1)} %get-tuple-element.52), channel_id=1, source_target_pairs={{0,24},{8,16},{16,8},{24,0},{1,25},{9,17},{17,9},{25,1},{2,26},{10... | collective-permute-start | bytes 393224 | tf_op jit(solution)/shard_map/ppermute | solution.py:190
  197.0 1.9 shard_map.34
  206.5 1.9 collective-permute-done.29
  (82 shorter events, 36.3 us)
Async XLA Ops:
  3.8 28.8 %collective-permute-start = (f32[2,256,512]{2,1,0:T(8,128)}, f32[2,256,512]{2,1,0:T(8,128)S(1)}, u32[]{:S(2)}, u32[]{:S(2)}) collective-permute-start(f32[2,256,512]{2,1,0:T(8,128)} %get-tuple-element.36), channel_id=1, source_target_pairs={{0,2},{6,4},{1,3},{7,5},{8,10},{14,12},{9,11},{15,13},{16,18},{22,... | collective-permute-start | bytes 3145736 | tf_op jit(solution)/shard_map/ppermute | solution.py:105
  9.0 36.8 %collective-permute-start.8 = (f32[9,256,128]{2,1,0:T(8,128)S(1)}, f32[9,256,128]{2,1,0:T(8,128)}, u32[]{:S(2)}, u32[]{:S(2)}) collective-permute-start(f32[9,256,128]{2,1,0:T(8,128)S(1)} %slice.59.refs_0_), channel_id=1, source_target_pairs={{2,4},{4,2},{3,5},{5,3},{10,12},{12,10},{11,13},{13,11},{18,20},{2... | collective-permute-start | bytes 3538952 | tf_op jit(solution)/shard_map/ppermute | solution.py:105
  11.8 32.0 %collective-permute-start.5 = (f32[1,256,512]{2,1,0:T(8,128)S(1)}, f32[1,256,512]{2,1,0:T(8,128)S(1)}, u32[]{:S(2)}, u32[]{:S(2)}) collective-permute-start(f32[1,256,512]{2,1,0:T(8,128)S(1)} %dynamic-slice_bitcast_fusion.3), channel_id=1, source_target_pairs={{0,2},{6,4},{1,3},{7,5},{8,10},{14,12},{9,11},{15,13},{16,18},{22,... | collective-permute-start | bytes 1572872 | tf_op jit(solution)/shard_map/ppermute | solution.py:105
  32.6 36.4 %collective-permute-start.1 = (f32[9,256,128]{2,1,0:T(8,128)S(1)}, f32[9,256,128]{2,1,0:T(8,128)}, u32[]{:S(2)}, u32[]{:S(2)}) collective-permute-start(f32[9,256,128]{2,1,0:T(8,128)S(1)} %slice.57.refs_0_), channel_id=1, source_target_pairs={{0,2},{6,4},{1,3},{7,5},{8,10},{14,12},{9,11},{15,13},{16,18},{22,... | collective-permute-start | bytes 3538952 | tf_op jit(solution)/shard_map/ppermute | solution.py:105
  37.9 35.0 %collective-permute-start.3 = (f32[9,256,128]{2,1,0:T(8,128)S(1)}, f32[9,256,128]{2,1,0:T(8,128)}, u32[]{:S(2)}, u32[]{:S(2)}) collective-permute-start(f32[9,256,128]{2,1,0:T(8,128)S(1)} %slice.57.refs_0_), channel_id=1, source_target_pairs={{2,4},{4,2},{3,5},{5,3},{10,12},{12,10},{11,13},{13,11},{18,20},{2... | collective-permute-start | bytes 3538952 | tf_op jit(solution)/shard_map/ppermute | solution.py:105
  39.6 34.9 %collective-permute-start.10 = (f32[9,256,128]{2,1,0:T(8,128)S(1)}, f32[9,256,128]{2,1,0:T(8,128)S(1)}, u32[]{:S(2)}, u32[]{:S(2)}) collective-permute-start(f32[9,256,128]{2,1,0:T(8,128)S(1)} %slice.57.refs_0_), channel_id=1, source_target_pairs={{2,0},{4,6},{3,1},{5,7},{10,8},{12,14},{11,9},{13,15},{18,16},{20,... | collective-permute-start | bytes 3538952 | tf_op jit(solution)/shard_map/ppermute | solution.py:105
  44.5 51.1 %collective-permute-start.7 = (f32[9,256,128]{2,1,0:T(8,128)S(1)}, f32[9,256,128]{2,1,0:T(8,128)S(1)}, u32[]{:S(2)}, u32[]{:S(2)}) collective-permute-start(f32[9,256,128]{2,1,0:T(8,128)S(1)} %slice.59.refs_0_), channel_id=1, source_target_pairs={{2,0},{4,6},{3,1},{5,7},{10,8},{12,14},{11,9},{13,15},{18,16},{20,... | collective-permute-start | bytes 3538952 | tf_op jit(solution)/shard_map/ppermute | solution.py:105
  45.8 53.4 %collective-permute-start.6 = (f32[9,256,128]{2,1,0:T(8,128)S(1)}, f32[9,256,128]{2,1,0:T(8,128)}, u32[]{:S(2)}, u32[]{:S(2)}) collective-permute-start(f32[9,256,128]{2,1,0:T(8,128)S(1)} %slice.59.refs_0_), channel_id=1, source_target_pairs={{0,2},{6,4},{1,3},{7,5},{8,10},{14,12},{9,11},{15,13},{16,18},{22,... | collective-permute-start | bytes 3538952 | tf_op jit(solution)/shard_map/ppermute | solution.py:105
  69.0 58.8 %collective-permute-start.14 = (f32[9,256,128]{2,1,0:T(8,128)}, f32[9,256,128]{2,1,0:T(8,128)}, u32[]{:S(2)}, u32[]{:S(2)}) collective-permute-start(f32[9,256,128]{2,1,0:T(8,128)} %collective-permute-done.1.refs_1_), channel_id=1, source_target_pairs={{2,4},{4,2},{3,5},{5,3},{10,12},{12,10},{11,13},{13,11},{18,20},{2... | collective-permute-start | bytes 3538952 | tf_op jit(solution)/shard_map/ppermute | solution.py:105
  72.9 27.6 %collective-permute-start.4 = (f32[7,256,128]{2,1,0:T(8,128)}, f32[7,256,128]{2,1,0:T(8,128)}, u32[]{:S(2)}, u32[]{:S(2)}) collective-permute-start(f32[7,256,128]{2,1,0:T(8,128)} %slice.58.refs_0_), channel_id=1, source_target_pairs={{2,4},{4,2},{3,5},{5,3},{10,12},{12,10},{11,13},{13,11},{18,20},{2... | collective-permute-start | bytes 2752520 | tf_op jit(solution)/shard_map/ppermute | solution.py:105
  75.5 55.1 %collective-permute-start.11 = (f32[9,256,128]{2,1,0:T(8,128)}, f32[9,256,128]{2,1,0:T(8,128)}, u32[]{:S(2)}, u32[]{:S(2)}) collective-permute-start(f32[9,256,128]{2,1,0:T(8,128)} %collective-permute-done.3.refs_3_), channel_id=1, source_target_pairs={{2,0},{4,6},{3,1},{5,7},{10,8},{12,14},{11,9},{13,15},{18,16},{20,... | collective-permute-start | bytes 3538952 | tf_op jit(solution)/shard_map/ppermute | solution.py:105
  96.8 16.1 %collective-permute-start.2 = (f32[7,256,128]{2,1,0:T(8,128)}, f32[7,256,128]{2,1,0:T(8,128)}, u32[]{:S(2)}, u32[]{:S(2)}) collective-permute-start(f32[7,256,128]{2,1,0:T(8,128)} %slice.58.refs_0_), channel_id=1, source_target_pairs={{0,2},{6,4},{1,3},{7,5},{8,10},{14,12},{9,11},{15,13},{16,18},{22,... | collective-permute-start | bytes 2752520 | tf_op jit(solution)/shard_map/ppermute | solution.py:105
  99.2 43.8 %collective-permute-start.9 = (f32[9,256,128]{2,1,0:T(8,128)}, f32[9,256,128]{2,1,0:T(8,128)}, u32[]{:S(2)}, u32[]{:S(2)}) collective-permute-start(f32[9,256,128]{2,1,0:T(8,128)} %collective-permute-done.8.refs_3_), channel_id=1, source_target_pairs={{2,0},{4,6},{3,1},{5,7},{10,8},{12,14},{11,9},{13,15},{18,16},{20,... | collective-permute-start | bytes 3538952 | tf_op jit(solution)/shard_map/ppermute | solution.py:105
  100.5 56.8 %collective-permute-start.13 = (f32[9,256,128]{2,1,0:T(8,128)}, f32[9,256,128]{2,1,0:T(8,128)}, u32[]{:S(2)}, u32[]{:S(2)}) collective-permute-start(f32[9,256,128]{2,1,0:T(8,128)} %collective-permute-done.6.refs_1_), channel_id=1, source_target_pairs={{2,4},{4,2},{3,5},{5,3},{10,12},{12,10},{11,13},{13,11},{18,20},{2... | collective-permute-start | bytes 3538952 | tf_op jit(solution)/shard_map/ppermute | solution.py:105
  105.2 28.4 %copy-start.3 = (f32[9,256,128]{2,1,0:T(8,128)S(1)}, f32[9,256,128]{2,1,0:T(8,128)}, u32[]{:S(2)}) copy-start(f32[9,256,128]{2,1,0:T(8,128)} %copy-done.2) | copy-start | bytes 3538948
  112.9 49.7 %collective-permute-start.24 = (f32[2,256,512]{2,1,0:T(8,128)}, f32[2,256,512]{2,1,0:T(8,128)S(1)}, u32[]{:S(2)}, u32[]{:S(2)}) collective-permute-start(f32[2,256,512]{2,1,0:T(8,128)} %get-tuple-element.34), channel_id=1, source_target_pairs={{0,2},{6,4},{1,3},{7,5},{8,10},{14,12},{9,11},{15,13},{16,18},{22,... | collective-permute-start | bytes 3145736 | tf_op jit(solution)/shard_map/ppermute | solution.py:105
  127.8 31.8 %collective-permute-start.18 = (f32[7,256,128]{2,1,0:T(8,128)}, f32[7,256,128]{2,1,0:T(8,128)S(1)}, u32[]{:S(2)}, u32[]{:S(2)}) collective-permute-start(f32[7,256,128]{2,1,0:T(8,128)} %collective-permute-done.2.refs_1_), channel_id=1, source_target_pairs={{2,4},{4,2},{3,5},{5,3},{10,12},{12,10},{11,13},{13,11},{18,20},{2... | collective-permute-start | bytes 2752520 | tf_op jit(solution)/shard_map/ppermute | solution.py:105
  130.6 39.1 %collective-permute-start.23 = (f32[2,256,512]{2,1,0:T(8,128)}, f32[2,256,512]{2,1,0:T(8,128)S(1)}, u32[]{:S(2)}, u32[]{:S(2)}) collective-permute-start(f32[2,256,512]{2,1,0:T(8,128)} %get-tuple-element.33), channel_id=1, source_target_pairs={{0,2},{6,4},{1,3},{7,5},{8,10},{14,12},{9,11},{15,13},{16,18},{22,... | collective-permute-start | bytes 3145736 | tf_op jit(solution)/shard_map/ppermute | solution.py:105
  133.6 10.7 %copy-start.1 = (f32[9,256,128]{2,1,0:T(8,128)S(1)}, f32[9,256,128]{2,1,0:T(8,128)}, u32[]{:S(2)}) copy-start(f32[9,256,128]{2,1,0:T(8,128)} %copy-done) | copy-start | bytes 3538948
  142.9 31.0 %collective-permute-start.15 = (f32[9,256,128]{2,1,0:T(8,128)}, f32[9,256,128]{2,1,0:T(8,128)S(1)}, u32[]{:S(2)}, u32[]{:S(2)}) collective-permute-start(f32[9,256,128]{2,1,0:T(8,128)} %collective-permute-done.14.refs_0_), channel_id=1, source_target_pairs={{2,0},{4,6},{3,1},{5,7},{10,8},{12,14},{11,9},{13,15},{18,16},{20,... | collective-permute-start | bytes 3538952 | tf_op jit(solution)/shard_map/ppermute | solution.py:105
  157.2 13.4 %collective-permute-start.12 = (f32[3,64,512]{2,1,0:T(8,128)S(1)}, f32[3,64,512]{2,1,0:T(8,128)S(1)}, u32[]{:S(2)}, u32[]{:S(2)}) collective-permute-start(f32[3,64,512]{2,1,0:T(8,128)S(1)} %dynamic-slice_bitcast_fusion.5), channel_id=1, source_target_pairs={{0,1},{1,0},{2,3},{3,2},{4,5},{5,4},{6,7},{7,6},{8,9},{9,8},{10,11... | collective-permute-start | bytes 1179656 | tf_op jit(solution)/shard_map/ppermute | solution.py:178
  159.6 31.1 %collective-permute-start.17 = (f32[6,256,128]{2,1,0:T(8,128)S(1)}, f32[6,256,128]{2,1,0:T(8,128)S(1)}, u32[]{:S(2)}, u32[]{:S(2)}) collective-permute-start(f32[6,256,128]{2,1,0:T(8,128)S(1)} %slice.75.refs_0_), channel_id=1, source_target_pairs={{2,0},{4,6},{3,1},{5,7},{10,8},{12,14},{11,9},{13,15},{18,16},{20,... | collective-permute-start | bytes 2359304 | tf_op jit(solution)/shard_map/ppermute | solution.py:105
  170.5 22.8 %collective-permute-start.25 = (f32[3,64,512]{2,1,0:T(8,128)S(1)}, f32[3,64,512]{2,1,0:T(8,128)S(1)}, u32[]{:S(2)}, u32[]{:S(2)}) collective-permute-start(f32[3,64,512]{2,1,0:T(8,128)S(1)} %dynamic-slice_bitcast_fusion.4), channel_id=1, source_target_pairs={{0,1},{1,0},{2,3},{3,2},{4,5},{5,4},{6,7},{7,6},{8,9},{9,8},{10,11... | collective-permute-start | bytes 1179656 | tf_op jit(solution)/shard_map/ppermute | solution.py:178
  173.9 23.1 %collective-permute-start.16 = (f32[3,256,128]{2,1,0:T(8,128)S(1)}, f32[3,256,128]{2,1,0:T(8,128)S(1)}, u32[]{:S(2)}, u32[]{:S(2)}) collective-permute-start(f32[3,256,128]{2,1,0:T(8,128)S(1)} %slice.74.refs_0_), channel_id=1, source_target_pairs={{2,0},{4,6},{3,1},{5,7},{10,8},{12,14},{11,9},{13,15},{18,16},{20,... | collective-permute-start | bytes 1179656 | tf_op jit(solution)/shard_map/ppermute | solution.py:105
  193.5 5.9 %collective-permute-start.28 = (f32[64,512]{1,0:T(8,128)S(1)}, f32[64,512]{1,0:T(8,128)S(1)}, u32[]{:S(2)}, u32[]{:S(2)}) collective-permute-start(f32[64,512]{1,0:T(8,128)S(1)} %get-tuple-element.52), channel_id=1, source_target_pairs={{0,24},{8,16},{16,8},{24,0},{1,25},{9,17},{17,9},{25,1},{2,26},{10... | collective-permute-start | bytes 393224 | tf_op jit(solution)/shard_map/ppermute | solution.py:190
  196.0 5.0 %collective-permute-start.27 = (f32[64,512]{1,0:T(8,128)S(1)}, f32[64,512]{1,0:T(8,128)S(1)}, u32[]{:S(2)}, u32[]{:S(2)}) collective-permute-start(f32[64,512]{1,0:T(8,128)S(1)} %get-tuple-element.51), channel_id=1, source_target_pairs={{0,16},{8,24},{16,0},{24,8},{1,17},{9,25},{17,1},{25,9},{2,18},{10... | collective-permute-start | bytes 393224 | tf_op jit(solution)/shard_map/ppermute | solution.py:190
  196.5 5.0 %collective-permute-start.26 = (f32[64,512]{1,0:T(8,128)S(1)}, f32[64,512]{1,0:T(8,128)S(1)}, u32[]{:S(2)}, u32[]{:S(2)}) collective-permute-start(f32[64,512]{1,0:T(8,128)S(1)} %get-tuple-element.50), channel_id=1, source_target_pairs={{0,8},{8,0},{16,24},{24,16},{1,9},{9,1},{17,25},{25,17},{2,10},{10... | collective-permute-start | bytes 393224 | tf_op jit(solution)/shard_map/ppermute | solution.py:190
  199.0 3.8 %collective-permute-start.19 = (f32[1,64,512]{2,1,0:T(8,128)S(1)}, f32[1,64,512]{2,1,0:T(8,128)S(1)}, u32[]{:S(2)}, u32[]{:S(2)}) collective-permute-start(f32[1,64,512]{2,1,0:T(8,128)S(1)} %dynamic-slice_bitcast_fusion.6), channel_id=1, source_target_pairs={{0,1},{1,0},{2,3},{3,2},{4,5},{5,4},{6,7},{7,6},{8,9},{9,8},{10,11... | collective-permute-start | bytes 393224 | tf_op jit(solution)/shard_map/ppermute | solution.py:178
  201.5 6.9 %collective-permute-start.29 = (f32[64,512]{1,0:T(8,128)S(1)}, f32[64,512]{1,0:T(8,128)S(1)}, u32[]{:S(2)}, u32[]{:S(2)}) collective-permute-start(f32[64,512]{1,0:T(8,128)S(1)} %fusion.3), channel_id=1, source_target_pairs={{2,0},{4,6},{3,1},{5,7},{10,8},{12,14},{11,9},{13,15},{18,16},{20,... | collective-permute-start | bytes 393224 | tf_op jit(solution)/shard_map/ppermute | solution.py:105
  202.9 7.1 %collective-permute-start.22 = (f32[64,512]{1,0:T(8,128)S(1)}, f32[64,512]{1,0:T(8,128)S(1)}, u32[]{:S(2)}, u32[]{:S(2)}) collective-permute-start(f32[64,512]{1,0:T(8,128)S(1)} %get-tuple-element.49), channel_id=1, source_target_pairs={{0,24},{8,16},{16,8},{24,0},{1,25},{9,17},{17,9},{25,1},{2,26},{10... | collective-permute-start | bytes 393224 | tf_op jit(solution)/shard_map/ppermute | solution.py:190
  204.5 6.0 %collective-permute-start.21 = (f32[64,512]{1,0:T(8,128)S(1)}, f32[64,512]{1,0:T(8,128)S(1)}, u32[]{:S(2)}, u32[]{:S(2)}) collective-permute-start(f32[64,512]{1,0:T(8,128)S(1)} %get-tuple-element.48), channel_id=1, source_target_pairs={{0,16},{8,24},{16,0},{24,8},{1,17},{9,25},{17,1},{25,9},{2,18},{10... | collective-permute-start | bytes 393224 | tf_op jit(solution)/shard_map/ppermute | solution.py:190
  205.4 5.1 %collective-permute-start.20 = (f32[64,512]{1,0:T(8,128)S(1)}, f32[64,512]{1,0:T(8,128)S(1)}, u32[]{:S(2)}, u32[]{:S(2)}) collective-permute-start(f32[64,512]{1,0:T(8,128)S(1)} %get-tuple-element.47), channel_id=1, source_target_pairs={{0,8},{8,0},{16,24},{24,16},{1,9},{9,1},{17,25},{25,17},{2,10},{10... | collective-permute-start | bytes 393224 | tf_op jit(solution)/shard_map/ppermute | solution.py:190
  (8 other events, 22.9 us)

commit v5 on v4

--- a/solution.py
+++ b/solution.py
@@ -8,6 +8,7 @@
 from jax.sharding import PartitionSpec as P
 
 LINE = 4
+HALVES = 2
 
 
 def after(value, *earlier):
@@ -57,40 +58,49 @@
     out_ref[...] += product.reshape(out_ref.shape)
 
 
-def contract(slots, weights, offset, total):
+def contract_run(slots, weights, offset, total, start, per, steps):
     terms = [len(slot) for slot in slots]
-    steps, depth, block = slots[0][0].shape
+    _, depth, block = slots[0][0].shape
     width = weights.shape[2]
-    per = max(n for n in (1, 2, 3) if steps % n == 0)
     shape = (len(slots), block, width)
     whole = pl.BlockSpec(shape, lambda i, o: (0, 0, 0))
-    in_specs = [pl.BlockSpec((per, depth, block), lambda i, o: (i, 0, 0))] * sum(terms)
+    in_specs = [pl.BlockSpec((per, depth, block), lambda i, o: (start // per + i, 0, 0))] * sum(terms)
     for j in range(per):
-        in_specs.append(pl.BlockSpec((1, depth, width), lambda i, o, j=j: (o[0] + per * i + j, 0, 0)))
+        in_specs.append(pl.BlockSpec((1, depth, width), lambda i, o, j=j: (o[0] + start + per * i + j, 0, 0)))
     operands = [a for slot in slots for a in slot] + [weights] * per
     aliases = {}
     if total is not None:
         in_specs.append(whole)
         aliases = {len(operands) + 1: 0}
         operands.append(total)
+    units = steps * per * depth
     return pl.pallas_call(
         functools.partial(contract_kernel, terms, per, total is None),
         out_shape=jax.ShapeDtypeStruct(shape, jnp.float32),
         grid_spec=pltpu.PrefetchScalarGridSpec(
-            num_scalar_prefetch=1, grid=(steps // per,), in_specs=in_specs, out_specs=whole
+            num_scalar_prefetch=1, grid=(steps,), in_specs=in_specs, out_specs=whole
         ),
         input_output_aliases=aliases,
         compiler_params=pltpu.CompilerParams(vmem_limit_bytes=40 << 20),
         cost_estimate=pl.CostEstimate(
-            flops=6 * steps * depth * len(slots) * block * width,
-            bytes_accessed=4 * (steps * depth * (width + sum(terms) * block) + 2 * len(slots) * block * width),
+            flops=6 * units * len(slots) * block * width,
+            bytes_accessed=4 * (units * (width + sum(terms) * block) + 2 * len(slots) * block * width),
             transcendentals=0,
         ),
     )(jnp.reshape(offset, (1,)).astype(jnp.int32), *operands)
 
 
+def contract(slots, weights, offset, total):
+    count = slots[0][0].shape[0]
+    per = min(6, count)
+    total = contract_run(slots, weights, offset, total, 0, per, count // per)
+    left = count % per
+    if left:
+        total = contract_run(slots, weights, offset, total, count - left, 1, left)
+    return total
+
+
 def shards(amplitude, integral, rows, cols, layers):
-    ko = amplitude.shape[0]
     group = cols // LINE
     row, col, layer = (lax.axis_index(name) for name in ("row", "col", "depth"))
     if group > 1:
@@ -98,41 +108,33 @@
         amplitude = lax.all_gather(amplitude, "col", axis=2, axis_index_groups=groups, tiled=True)
     place = col // group
     block, width = amplitude.shape[2], integral.shape[2]
-    integral = jnp.transpose(integral, (1, 0, 2))
+    integral = jnp.transpose(integral, (1, 0, 2)).reshape(-1, integral.shape[0] // HALVES, width)
+    amplitude = amplitude.reshape(-1, amplitude.shape[1] // HALVES, block)
+    ko = amplitude.shape[0]
 
     def hop(pairs):
         lanes = [(a * group + lane, b * group + lane) for a, b in pairs for lane in range(group)]
         return lambda value: lax.ppermute(value, "col", lanes)
 
     inward, across, outward = hop([(0, 1), (3, 2)]), hop([(1, 2), (2, 1)]), hop([(1, 0), (2, 3)])
-
-    lent = round(ko * 2 * block / (3 * block + width))
+    swap = hop([(0, 1), (1, 0), (2, 3), (3, 2)])
+
+    lent = round(ko * 2 * block / (3 * block + width)) - 1
     base = ko - lent
     main = bounds(0, base - base // 2, base // 2)
     extra = (base, ko)
-    sizes = [lent // 4 + (i + lent % 4 >= 4) for i in range(4)]
-    pieces = bounds(base, sizes[1], sizes[0], *sizes[2:])
-    last = main[-1]
-    size = last[1] - last[0]
-    tail = bounds(last[0], size - size // 3, size // 3)
+    pieces = bounds(base, *[lent // 5 + (i < lent % 5) for i in range(5)])
+    ends = []
+    for start, stop in main:
+        cut = (stop - start) // 2 if not ends else (stop - start) // 3
+        ends += bounds(start, stop - start - cut, cut)
 
     own = {main[0]: amplitude[: main[0][1]]}
     later = after(amplitude, own[main[0]])
+    shift = after(row, own[main[0]]) * ko
     for c in main[1:] + [extra]:
         own[c] = later[c[0] : c[1]]
-    same_in, far_inner, far_end = {}, {}, {}
-    out_same, out_inner, out_end, lent_weights = {}, {}, {}, {}
-
-    sends = {"out": [], "across": [], "in": []}
-    early = len(pieces) // 2
-    sends["in"] += [(lent_weights, c, None, inward) for c in pieces[:early]]
-    sends["in"] += [(same_in, c, own, inward) for c in main + [extra]]
-    sends["in"] += [(lent_weights, c, None, inward) for c in pieces[early:]]
-    sends["across"] += [(far_inner, c, own, across) for c in main + [extra]]
-    sends["across"] += [(far_end, c, same_in, across) for c in main + [extra]]
-    sends["out"] += [(out_same, c, own, outward) for c in main]
-    sends["out"] += [(out_inner, c, far_inner, outward) for c in main]
-    sends["out"] += [(out_end, c, far_end, outward) for c in main[:-1] + tail]
+    same, far_inner, far_end, out_inner, out_end, lent_weights = {}, {}, {}, {}, {}, {}
 
     def find(table, c):
         for (k0, k1), value in table.items():
@@ -140,29 +142,39 @@
                 return value if (k0, k1) == c else value[c[0] - k0 : c[1] - k0]
         return None
 
-    clock = dict.fromkeys(sends, 0)
-    arrived = {name: [] for name in sends}
-    while any(sends.values()):
-        ready = [n for n in sends if sends[n]]
-        ready = [n for n in ready if sends[n][0][2] is None or find(sends[n][0][2], sends[n][0][1]) is not None]
-        name = min(ready, key=lambda n: clock[n])
-        into, c, source, move = sends[name].pop(0)
+    done = {"out": [], "across": [], "in": []}
+
+    def send(name, into, c, source, move):
         if source is None:
-            value = lax.dynamic_slice_in_dim(integral, row * ko + c[0], c[1] - c[0], axis=0)
+            value = lax.dynamic_slice_in_dim(integral, shift + c[0], c[1] - c[0], axis=0)
         else:
             value = find(source, c)
-        if len(arrived[name]) >= 2:
-            value = after(value, arrived[name][-2])
+        if len(done[name]) >= 2:
+            value = after(value, done[name][-2])
         into[c] = move(value)
-        arrived[name].append(into[c])
-        clock[name] += (c[1] - c[0]) * (width / block if source is None else 1)
+        done[name].append(into[c])
+
+    for c in main:
+        send("out", same, c, own, swap)
+        done["in"].append(same[c])
+    for c in main + [extra]:
+        send("across", far_inner, c, own, across)
+    for c in main:
+        send("out", out_inner, c, far_inner, outward)
+    send("in", same, extra, own, inward)
+    for c in main + [extra]:
+        send("across", far_end, c, same, across)
+    for c in ends:
+        send("out", out_end, c, far_end, outward)
+    for c in pieces:
+        send("in", lent_weights, c, None, inward)
 
     near, far, loan = None, None, None
     for c in main:
-        slots = [[own[c]], [same_in[c], out_same[c]], [far_inner[c], out_inner[c]]]
+        slots = [[own[c]], [same[c]], [far_inner[c], out_inner[c]]]
         near = contract(slots, integral, row * ko + c[0], near)
-    near = contract([[own[extra]], [same_in[extra]], [far_inner[extra]]], integral, row * ko + base, near)
-    for c in main[:-1] + [extra] + tail:
+    near = contract([[own[extra]], [same[extra]], [far_inner[extra]]], integral, row * ko + base, near)
+    for c in ends[:2] + [extra] + ends[2:]:
         slots = [[find(far_end, c)] + ([out_end[c]] if c in out_end else [])]
         far = contract(slots, integral, row * ko + c[0], far)
     for c in pieces:

time: 212 us -> 219 us (1.033)
  waiting for transfers between devices: 89.3 us -> 79.5 us
  Pallas kernels: 36.2 us -> 43.8 us
  local copies, waits for them, and re-layouts: 18.3 us -> 23.2 us
  other arithmetic: 1.01 us -> 3.79 us
    ppermute x21, waiting for transfers between devices: 84.7 us -> 74.7 us  [hop(): return lambda value: lax.ppermute(value, 'col', lanes)]
    pallas_call x11 -> x18, Pallas kernels: 36.2 us -> 43.8 us  [contract_run(): pl.pallas_call(functools.partial(contract_kernel, terms, per, total is No...]
    slice x8 -> x10, local copies, waits for them, and re-layouts: 7.34 us -> 12.2 us  [find(): return value if (k0, k1) == c else value[c[0] - k0:c[1] - k0]]
    unnamed x20, local copies, waits for them, and re-layouts: 3.58 us -> 0.04 us
  transfers between devices with their start and end apart: 30 -> 30, of which waited for: 15 -> 9; matrix products, arithmetic and copies ran while one was open for 5% -> 11% of each run, Pallas kernels for 17% -> 20%
where the time goes in v5:
time: 219 us; the launch traced here: 217 us
  waiting for transfers between devices  79.5 us (36%)
  starting transfers between devices  66.3 us (30%)
  Pallas kernels  43.8 us (20%)
  local copies, waits for them, and re-layouts  23.2 us (11%)
  other arithmetic  3.79 us (2%)
    ppermute x21, waiting for transfers between devices, hop(): return lambda value: lax.ppermute(value, 'col', lanes)  74.7 us
    ppermute x21, starting transfers between devices, hop(): return lambda value: lax.ppermute(value, 'col', lanes)  59.2 us
    pallas_call x18, Pallas kernels, contract_run(): pl.pallas_call(functools.partial(contract_kernel, terms, per, total is No...  43.8 us
    slice x10, local copies, waits for them, and re-layouts, find(): return value if (k0, k1) == c else value[c[0] - k0:c[1] - k0]  12.2 us
    ppermute x6, starting transfers between devices, row_sum(): lax.ppermute(part(row ^ t), 'row', [(r, r ^ t) for r in range(4)])  7.04 us
    dynamic_slice x2, local copies, waits for them, and re-layouts, send(): lax.dynamic_slice_in_dim(integral, shift + c[0], c[1] - c[0], axis=0)  5.29 us
    ppermute x6, waiting for transfers between devices, row_sum(): lax.ppermute(part(row ^ t), 'row', [(r, r ^ t) for r in range(4)])  4.8 us
  transfers between devices with their start and end apart: 30, of which 9 were waited for; matrix products, arithmetic and copies ran while one was open for 11% of the time, Pallas kernels for 20%

profile of v5, /device:TPU:0, one launch (start us, length us, event | category | flops | bytes accessed | tf_op | source)
XLA Modules:
  0.0 217.2 jit_solution(11889268927290360358)
XLA Ops:
  2.8 3.1 %collective-permute-start.4 = (f32[18,128,128]{2,1,0:T(8,128)S(1)}, f32[18,128,128]{2,1,0:T(8,128)}, u32[]{:S(2)}, u32[]{:S(2)}) collective-permute-start(f32[18,128,128]{2,1,0:T(8,128)S(1)} %slice.77.refs_0_), channel_id=1, source_target_pairs={{0,2},{2,0},{4,6},{6,4},{1,3},{3,1},{5,7},{7,5},{8,10},{10,8},{12,... | collective-permute-start | bytes 3538952 | tf_op jit(solution)/shard_map/ppermute | solution.py:117
  9.3 3.0 %constant_dynamic-slice_fusion = (f32[3,128,512]{2,1,0:T(8,128)}, f32[3,128,512]{2,1,0:T(8,128)}, f32[3,128,512]{2,1,0:T(8,128)}) fusion(f32[200,128,512]{2,1,0:T(8,128)} %bitcast.60, s32[]{:T(128)S(6)} %select_n.85, s32[]{:T(128)S(6)} %select_n.83, s32[]{:T(128)S(6)} %select_n.82), kind=kLoop, calls=%fused_computation.37 | loop fusion | bytes 4718604 | tf_op jit(solution)/shard_map/dynamic_slice | solution.py:149
  12.4 20.4 %collective-permute-done.4.refs_1_ = f32[18,128,128]{2,1,0:T(8,128)} collective-permute-done((f32[18,128,128]{2,1,0:T(8,128)S(1)}, f32[18,128,128]{2,1,0:T(8,128)}, u32[]{:S(2)}, u32[]{:S(2)}) %collective-permute-start.4) | collective-permute-done | bytes 1179680 | tf_op jit(solution)/shard_map/ppermute | solution.py:117
  32.8 4.8 %collective-permute-start.20 = (f32[3,128,512]{2,1,0:T(8,128)}, f32[3,128,512]{2,1,0:T(8,128)}, u32[]{:S(2)}, u32[]{:S(2)}) collective-permute-start(f32[3,128,512]{2,1,0:T(8,128)} %get-tuple-element.36), channel_id=1, source_target_pairs={{0,2},{6,4},{1,3},{7,5},{8,10},{14,12},{9,11},{15,13},{16,18},{22,... | collective-permute-start | bytes 2359304 | tf_op jit(solution)/shard_map/ppermute | solution.py:117
  37.6 21.3 %collective-permute-done.refs_1_ = f32[19,128,128]{2,1,0:T(8,128)} collective-permute-done((f32[19,128,128]{2,1,0:T(8,128)S(1)}, f32[19,128,128]{2,1,0:T(8,128)}, u32[]{:S(2)}, u32[]{:S(2)}) %collective-permute-start) | collective-permute-done | bytes 1245216 | tf_op jit(solution)/shard_map/ppermute | solution.py:117
  65.3 9.4 %collective-permute-done.20.refs_3_.refs_4_.refs_5_ = f32[3,128,512]{2,1,0:T(8,128)} collective-permute-done((f32[3,128,512]{2,1,0:T(8,128)}, f32[3,128,512]{2,1,0:T(8,128)}, u32[]{:S(2)}, u32[]{:S(2)}) %collective-permute-start.20) | collective-permute-done | bytes 786464 | tf_op jit(solution)/shard_map/ppermute | solution.py:117
  74.7 5.3 %collective-permute-start.1 = (f32[13,128,128]{2,1,0:T(8,128)S(1)}, f32[13,128,128]{2,1,0:T(8,128)}, u32[]{:S(2)}, u32[]{:S(2)}) collective-permute-start(f32[13,128,128]{2,1,0:T(8,128)S(1)} %slice.76.refs_0_), channel_id=1, source_target_pairs={{0,2},{6,4},{1,3},{7,5},{8,10},{14,12},{9,11},{15,13},{16,18},{22,... | collective-permute-start | bytes 2555912 | tf_op jit(solution)/shard_map/ppermute | solution.py:117
  80.1 2.2 %constant_dynamic-slice_fusion.1 = (f32[2,128,512]{2,1,0:T(8,128)}, f32[2,128,512]{2,1,0:T(8,128)}) fusion(f32[200,128,512]{2,1,0:T(8,128)} %bitcast.61, s32[]{:T(128)S(6)} %select_n.84, s32[]{:T(128)S(6)} %select_n.81), kind=kLoop, calls=%fused_computation.38 | loop fusion | bytes 2097160 | tf_op jit(solution)/shard_map/dynamic_slice | solution.py:149
  86.2 10.2 %collective-permute-done.1.refs_1_ = f32[13,128,128]{2,1,0:T(8,128)} collective-permute-done((f32[13,128,128]{2,1,0:T(8,128)S(1)}, f32[13,128,128]{2,1,0:T(8,128)}, u32[]{:S(2)}, u32[]{:S(2)}) %collective-permute-start.1) | collective-permute-done | bytes 852000 | tf_op jit(solution)/shard_map/ppermute | solution.py:117
  96.4 18.9 %collective-permute-start.21 = (f32[3,128,512]{2,1,0:T(8,128)}, f32[3,128,512]{2,1,0:T(8,128)}, u32[]{:S(2)}, u32[]{:S(2)}) collective-permute-start(f32[3,128,512]{2,1,0:T(8,128)} %get-tuple-element.37), channel_id=1, source_target_pairs={{0,2},{6,4},{1,3},{7,5},{8,10},{14,12},{9,11},{15,13},{16,18},{22,... | collective-permute-start | bytes 2359304 | tf_op jit(solution)/shard_map/ppermute | solution.py:117
  116.9 2.0 slice.101.refs_0_
  118.9 2.2 %collective-permute-start.23 = (f32[3,128,512]{2,1,0:T(8,128)}, f32[3,128,512]{2,1,0:T(8,128)}, u32[]{:S(2)}, u32[]{:S(2)}) collective-permute-start(f32[3,128,512]{2,1,0:T(8,128)} %get-tuple-element.39), channel_id=1, source_target_pairs={{0,2},{6,4},{1,3},{7,5},{8,10},{14,12},{9,11},{15,13},{16,18},{22,... | collective-permute-start | bytes 2359304 | tf_op jit(solution)/shard_map/ppermute | solution.py:117
  122.4 5.9 %shard_map.28.refs_5_ = f32[3,128,512]{2,1,0:T(8,128)S(1)} custom-call(s32[1]{0:T(128)} %bitcast.6.offset_ref, f32[19,128,128]{2,1,0:T(8,128)S(1)} %slice.97.refs_0_, f32[19,128,128]{2,1,0:T(8,128)} %collective-permute-done.refs_1_, f32[19,128,128]{2,1,0:T(8,128)} %collective-permute-done.2.refs_2_, f32[19,128,128]{2,1,0:T(8,128)} %collective-permute-done.7.refs_3_, ...), custom_call_target="tpu_custom_call" | custom-call | flops 2717908992 | bytes 11010048 | tf_op jit(solution)/shard_map/pallas_call | solution.py:77
  128.2 1.9 slice.99.refs_0_
  131.7 5.9 %shard_map.30.refs_9_ = f32[3,128,512]{2,1,0:T(8,128)S(1)} custom-call(s32[1]{0:T(128)} %bitcast.5.offset_ref, f32[18,128,128]{2,1,0:T(8,128)S(1)} %copy-done.4, f32[18,128,128]{2,1,0:T(8,128)} %collective-permute-done.4.refs_1_, f32[18,128,128]{2,1,0:T(8,128)} %collective-permute-done.5.refs_2_, ...), custom_call_target="tpu_custom_call", output_to_operand_aliasing={{}: (11, {})} | custom-call | flops 2717908992 | bytes 11010048 | tf_op jit(solution)/shard_map/pallas_call | solution.py:77
  137.6 4.0 %shard_map.31.refs_4_ = f32[3,128,512]{2,1,0:T(8,128)S(1)} custom-call(s32[1]{0:T(128)} %bitcast.offset_ref, f32[13,128,128]{2,1,0:T(8,128)S(1)} %slice.76.refs_0_, f32[13,128,128]{2,1,0:T(8,128)} %collective-permute-done.1.refs_1_, f32[13,128,128]{2,1,0:T(8,128)S(1)} %collective-permute-done.3.refs_2_, ...), custom_call_target="tpu_custom_call", output_to_operand_aliasing={{}: (10, {})} | custom-call | flops 1811939328 | bytes 7077888 | tf_op jit(solution)/shard_map/pallas_call | solution.py:77
  145.1 5.0 %collective-permute-start.22 = (f32[2,128,512]{2,1,0:T(8,128)S(1)}, f32[2,128,512]{2,1,0:T(8,128)S(1)}, u32[]{:S(2)}, u32[]{:S(2)}) collective-permute-start(f32[2,128,512]{2,1,0:T(8,128)S(1)} %copy-done.8), channel_id=1, source_target_pairs={{0,2},{6,4},{1,3},{7,5},{8,10},{14,12},{9,11},{15,13},{16,18},{22,... | collective-permute-start | bytes 1572872 | tf_op jit(solution)/shard_map/ppermute | solution.py:117
  150.2 2.1 slice.100.refs_0_
  157.1 1.8 shard_map.41.refs_6_
  158.9 1.8 shard_map.42.refs_6_
  160.7 1.8 shard_map.43.refs_5_
  162.6 10.6 %collective-permute-done.24.refs_3_.refs_4_ = f32[2,128,512]{2,1,0:T(8,128)S(1)} collective-permute-done((f32[2,128,512]{2,1,0:T(8,128)S(1)}, f32[2,128,512]{2,1,0:T(8,128)S(1)}, u32[]{:S(2)}, u32[]{:S(2)}) %collective-permute-start.24) | collective-permute-done | bytes 524320 | tf_op jit(solution)/shard_map/ppermute | solution.py:117
  175.9 2.1 shard_map.33.refs_3_
  178.0 3.0 %shard_map.34.refs_8_ = f32[1,128,512]{2,1,0:T(8,128)S(1)} custom-call(s32[1]{0:T(128)} %bitcast.6.offset_ref, f32[10,128,128]{2,1,0:T(8,128)} %slice.101.refs_0_, f32[10,128,128]{2,1,0:T(8,128)} %collective-permute-done.13.refs_1_, f32[200,128,512]{2,1,0:T(8,128)} %bitcast.88, f32[1,128,512]{2,1,0:T(8,128)S(1)} %shard_map.33.refs_3_), custom_call_target="tpu_custom_call", output_to_operand_aliasing={{}: (4, {})} | custom-call | flops 201326592 | bytes 2097152 | tf_op jit(solution)/shard_map/pallas_call | solution.py:77
  181.0 1.9 shard_map.35.refs_3_
  182.9 2.5 %shard_map.36.refs_7_ = f32[1,128,512]{2,1,0:T(8,128)S(1)} custom-call(s32[1]{0:T(128)} %bitcast.11.offset_ref, f32[9,128,128]{2,1,0:T(8,128)S(1)} %copy-done.2, f32[9,128,128]{2,1,0:T(8,128)S(1)} %collective-permute-done.11.refs_1_, f32[200,128,512]{2,1,0:T(8,128)} %bitcast.95, f32[1,128,512]{2,1,0:T(8,128)S(1)} %shard_map.35.refs_3_), custom_call_target="tpu_custom_call", output_to_operand_aliasing={{}: (4, {})} | custom-call | flops 150994944 | bytes 1703936 | tf_op jit(solution)/shard_map/pallas_call | solution.py:77
  185.4 1.8 slice.98.refs_0_
  188.6 2.7 %shard_map.37.refs_2_ = f32[1,128,512]{2,1,0:T(8,128)S(1)} custom-call(s32[1]{0:T(128)} %bitcast.offset_ref, f32[13,128,128]{2,1,0:T(8,128)} %collective-permute-done.15.refs_0_, f32[200,128,512]{2,1,0:T(8,128)} %bitcast.99, f32[200,128,512]{2,1,0:T(8,128)} %bitcast.97, f32[200,128,512]{2,1,0:T(8,128)} %bitcast.98, ...), custom_call_target="tpu_custom_call", output_to_operand_aliasing={{}: (8, {})} | custom-call | flops 603979776 | bytes 4456448 | tf_op jit(solution)/shard_map/pallas_call | solution.py:77
  198.1 2.9 %shard_map.39.refs_8_ = f32[1,128,512]{2,1,0:T(8,128)S(1)} custom-call(s32[1]{0:T(128)} %bitcast.5.offset_ref, f32[12,128,128]{2,1,0:T(8,128)} %slice.100.refs_0_, f32[12,128,128]{2,1,0:T(8,128)} %collective-permute-done.14.refs_1_, f32[200,128,512]{2,1,0:T(8,128)} %bitcast.103, f32[200,128,512]{2,1,0:T(8,128)} %bitcast.104, ...), custom_call_target="tpu_custom_call", output_to_operand_aliasing={{}: (9, {})} | custom-call | flops 603979776 | bytes 5242880 | tf_op jit(solution)/shard_map/pallas_call | solution.py:77
  201.0 2.2 %shard_map.40 = f32[1,128,512]{2,1,0:T(8,128)S(1)} custom-call(s32[1]{0:T(128)} %bitcast.10.offset_ref, f32[6,128,128]{2,1,0:T(8,128)} %slice.98.refs_0_, f32[6,128,128]{2,1,0:T(8,128)} %collective-permute-done.12.refs_1_, f32[200,128,512]{2,1,0:T(8,128)} %bitcast.109, f32[200,128,512]{2,1,0:T(8,128)} %bitcast.110, ...), custom_call_target="tpu_custom_call", output_to_operand_aliasing={{}: (9, {})} | custom-call | flops 301989888 | bytes 2883584 | tf_op jit(solution)/shard_map/pallas_call | solution.py:77
  210.9 2.2 %collective-permute-done.29 = f32[64,512]{1,0:T(8,128)S(1)} collective-permute-done((f32[64,512]{1,0:T(8,128)S(1)}, f32[64,512]{1,0:T(8,128)S(1)}, u32[]{:S(2)}, u32[]{:S(2)}) %collective-permute-start.29) | collective-permute-done | bytes 131104 | tf_op jit(solution)/shard_map/ppermute | solution.py:117
  213.2 3.3 %collective-permute-done.18 = f32[64,512]{1,0:T(8,128)S(1)} collective-permute-done((f32[64,512]{1,0:T(8,128)S(1)}, f32[64,512]{1,0:T(8,128)S(1)}, u32[]{:S(2)}, u32[]{:S(2)}) %collective-permute-start.18) | collective-permute-done | bytes 131104 | tf_op jit(solution)/shard_map/ppermute | solution.py:202
  (91 shorter events, 48.2 us)
Async XLA Ops:
  2.8 9.6 %copy-start.3 = (f32[18,128,128]{2,1,0:T(8,128)}, f32[18,128,128]{2,1,0:T(8,128)S(1)}, u32[]{:S(2)}) copy-start(f32[18,128,128]{2,1,0:T(8,128)S(1)} %slice.77.refs_0_) | copy-start | bytes 3538948
  2.8 30.0 %collective-permute-start.4 = (f32[18,128,128]{2,1,0:T(8,128)S(1)}, f32[18,128,128]{2,1,0:T(8,128)}, u32[]{:S(2)}, u32[]{:S(2)}) collective-permute-start(f32[18,128,128]{2,1,0:T(8,128)S(1)} %slice.77.refs_0_), channel_id=1, source_target_pairs={{0,2},{2,0},{4,6},{6,4},{1,3},{3,1},{5,7},{7,5},{8,10},{10,8},{12,... | collective-permute-start | bytes 3538952 | tf_op jit(solution)/shard_map/ppermute | solution.py:117
  5.9 53.1 %collective-permute-start = (f32[19,128,128]{2,1,0:T(8,128)S(1)}, f32[19,128,128]{2,1,0:T(8,128)}, u32[]{:S(2)}, u32[]{:S(2)}) collective-permute-start(f32[19,128,128]{2,1,0:T(8,128)S(1)} %slice.97.refs_0_), channel_id=1, source_target_pairs={{0,2},{2,0},{4,6},{6,4},{1,3},{3,1},{5,7},{7,5},{8,10},{10,8},{12,... | collective-permute-start | bytes 3735560 | tf_op jit(solution)/shard_map/ppermute | solution.py:117
  5.9 31.7 %collective-permute-start.5 = (f32[18,128,128]{2,1,0:T(8,128)S(1)}, f32[18,128,128]{2,1,0:T(8,128)}, u32[]{:S(2)}, u32[]{:S(2)}) collective-permute-start(f32[18,128,128]{2,1,0:T(8,128)S(1)} %slice.77.refs_0_), channel_id=1, source_target_pairs={{2,4},{4,2},{3,5},{5,3},{10,12},{12,10},{11,13},{13,11},{18,20},{2... | collective-permute-start | bytes 3538952 | tf_op jit(solution)/shard_map/ppermute | solution.py:117
  7.6 54.3 %collective-permute-start.2 = (f32[19,128,128]{2,1,0:T(8,128)S(1)}, f32[19,128,128]{2,1,0:T(8,128)}, u32[]{:S(2)}, u32[]{:S(2)}) collective-permute-start(f32[19,128,128]{2,1,0:T(8,128)S(1)} %slice.97.refs_0_), channel_id=1, source_target_pairs={{2,4},{4,2},{3,5},{5,3},{10,12},{12,10},{11,13},{13,11},{18,20},{2... | collective-permute-start | bytes 3735560 | tf_op jit(solution)/shard_map/ppermute | solution.py:117
  32.8 42.0 %collective-permute-start.20 = (f32[3,128,512]{2,1,0:T(8,128)}, f32[3,128,512]{2,1,0:T(8,128)}, u32[]{:S(2)}, u32[]{:S(2)}) collective-permute-start(f32[3,128,512]{2,1,0:T(8,128)} %get-tuple-element.36), channel_id=1, source_target_pairs={{0,2},{6,4},{1,3},{7,5},{8,10},{14,12},{9,11},{15,13},{16,18},{22,... | collective-permute-start | bytes 2359304 | tf_op jit(solution)/shard_map/ppermute | solution.py:117
  58.9 56.4 %collective-permute-start.10 = (f32[19,128,128]{2,1,0:T(8,128)}, f32[19,128,128]{2,1,0:T(8,128)}, u32[]{:S(2)}, u32[]{:S(2)}) collective-permute-start(f32[19,128,128]{2,1,0:T(8,128)} %collective-permute-done.refs_1_), channel_id=1, source_target_pairs={{2,4},{4,2},{3,5},{5,3},{10,12},{12,10},{11,13},{13,11},{18,20},{2... | collective-permute-start | bytes 3735560 | tf_op jit(solution)/shard_map/ppermute | solution.py:117
  61.9 22.6 %collective-permute-start.3 = (f32[13,128,128]{2,1,0:T(8,128)S(1)}, f32[13,128,128]{2,1,0:T(8,128)S(1)}, u32[]{:S(2)}, u32[]{:S(2)}) collective-permute-start(f32[13,128,128]{2,1,0:T(8,128)S(1)} %slice.76.refs_0_), channel_id=1, source_target_pairs={{2,4},{4,2},{3,5},{5,3},{10,12},{12,10},{11,13},{13,11},{18,20},{2... | collective-permute-start | bytes 2555912 | tf_op jit(solution)/shard_map/ppermute | solution.py:117
  62.6 56.3 %collective-permute-start.7 = (f32[19,128,128]{2,1,0:T(8,128)}, f32[19,128,128]{2,1,0:T(8,128)}, u32[]{:S(2)}, u32[]{:S(2)}) collective-permute-start(f32[19,128,128]{2,1,0:T(8,128)} %collective-permute-done.2.refs_2_), channel_id=1, source_target_pairs={{2,0},{4,6},{3,1},{5,7},{10,8},{12,14},{11,9},{13,15},{18,16},{20,... | collective-permute-start | bytes 3735560 | tf_op jit(solution)/shard_map/ppermute | solution.py:117
  63.9 57.2 %collective-permute-start.6 = (f32[18,128,128]{2,1,0:T(8,128)}, f32[18,128,128]{2,1,0:T(8,128)}, u32[]{:S(2)}, u32[]{:S(2)}) collective-permute-start(f32[18,128,128]{2,1,0:T(8,128)} %collective-permute-done.5.refs_2_), channel_id=1, source_target_pairs={{2,0},{4,6},{3,1},{5,7},{10,8},{12,14},{11,9},{13,15},{18,16},{20,... | collective-permute-start | bytes 3538952 | tf_op jit(solution)/shard_map/ppermute | solution.py:117
  74.7 21.7 %collective-permute-start.1 = (f32[13,128,128]{2,1,0:T(8,128)S(1)}, f32[13,128,128]{2,1,0:T(8,128)}, u32[]{:S(2)}, u32[]{:S(2)}) collective-permute-start(f32[13,128,128]{2,1,0:T(8,128)S(1)} %slice.76.refs_0_), channel_id=1, source_target_pairs={{0,2},{6,4},{1,3},{7,5},{8,10},{14,12},{9,11},{15,13},{16,18},{22,... | collective-permute-start | bytes 2555912 | tf_op jit(solution)/shard_map/ppermute | solution.py:117
  84.5 60.7 %collective-permute-start.9 = (f32[18,128,128]{2,1,0:T(8,128)}, f32[18,128,128]{2,1,0:T(8,128)}, u32[]{:S(2)}, u32[]{:S(2)}) collective-permute-start(f32[18,128,128]{2,1,0:T(8,128)} %collective-permute-done.4.refs_1_), channel_id=1, source_target_pairs={{2,4},{4,2},{3,5},{5,3},{10,12},{12,10},{11,13},{13,11},{18,20},{2... | collective-permute-start | bytes 3538952 | tf_op jit(solution)/shard_map/ppermute | solution.py:117
  96.4 46.7 %collective-permute-start.21 = (f32[3,128,512]{2,1,0:T(8,128)}, f32[3,128,512]{2,1,0:T(8,128)}, u32[]{:S(2)}, u32[]{:S(2)}) collective-permute-start(f32[3,128,512]{2,1,0:T(8,128)} %get-tuple-element.37), channel_id=1, source_target_pairs={{0,2},{6,4},{1,3},{7,5},{8,10},{14,12},{9,11},{15,13},{16,18},{22,... | collective-permute-start | bytes 2359304 | tf_op jit(solution)/shard_map/ppermute | solution.py:117
  115.3 38.3 %collective-permute-start.15 = (f32[13,128,128]{2,1,0:T(8,128)}, f32[13,128,128]{2,1,0:T(8,128)}, u32[]{:S(2)}, u32[]{:S(2)}) collective-permute-start(f32[13,128,128]{2,1,0:T(8,128)} %collective-permute-done.1.refs_1_), channel_id=1, source_target_pairs={{2,4},{4,2},{3,5},{5,3},{10,12},{12,10},{11,13},{13,11},{18,20},{2... | collective-permute-start | bytes 2555912 | tf_op jit(solution)/shard_map/ppermute | solution.py:117
  118.9 26.2 %collective-permute-start.23 = (f32[3,128,512]{2,1,0:T(8,128)}, f32[3,128,512]{2,1,0:T(8,128)}, u32[]{:S(2)}, u32[]{:S(2)}) collective-permute-start(f32[3,128,512]{2,1,0:T(8,128)} %get-tuple-element.39), channel_id=1, source_target_pairs={{0,2},{6,4},{1,3},{7,5},{8,10},{14,12},{9,11},{15,13},{16,18},{22,... | collective-permute-start | bytes 2359304 | tf_op jit(solution)/shard_map/ppermute | solution.py:117
  121.1 31.2 %collective-permute-start.13 = (f32[10,128,128]{2,1,0:T(8,128)}, f32[10,128,128]{2,1,0:T(8,128)}, u32[]{:S(2)}, u32[]{:S(2)}) collective-permute-start(f32[10,128,128]{2,1,0:T(8,128)} %slice.101.refs_0_), channel_id=1, source_target_pairs={{2,0},{4,6},{3,1},{5,7},{10,8},{12,14},{11,9},{13,15},{18,16},{20,... | collective-permute-start | bytes 1966088 | tf_op jit(solution)/shard_map/ppermute | solution.py:117
  143.1 9.2 %copy-start.9 = (f32[2,128,512]{2,1,0:T(8,128)S(1)}, f32[2,128,512]{2,1,0:T(8,128)}, u32[]{:S(2)}) copy-start(f32[2,128,512]{2,1,0:T(8,128)} %get-tuple-element.40) | copy-start | bytes 1572868
  143.2 37.8 %collective-permute-start.11 = (f32[9,128,128]{2,1,0:T(8,128)S(1)}, f32[9,128,128]{2,1,0:T(8,128)S(1)}, u32[]{:S(2)}, u32[]{:S(2)}) collective-permute-start(f32[9,128,128]{2,1,0:T(8,128)S(1)} %copy-done.2), channel_id=1, source_target_pairs={{2,0},{4,6},{3,1},{5,7},{10,8},{12,14},{11,9},{13,15},{18,16},{20,... | collective-permute-start | bytes 1769480 | tf_op jit(solution)/shard_map/ppermute | solution.py:117
  145.1 29.9 %collective-permute-start.8 = (f32[3,64,512]{2,1,0:T(8,128)S(1)}, f32[3,64,512]{2,1,0:T(8,128)S(1)}, u32[]{:S(2)}, u32[]{:S(2)}) collective-permute-start(f32[3,64,512]{2,1,0:T(8,128)S(1)} %dynamic-slice_bitcast_fusion.1), channel_id=1, source_target_pairs={{0,1},{1,0},{2,3},{3,2},{4,5},{5,4},{6,7},{7,6},{8,9},{9,8},{10,11... | collective-permute-start | bytes 1179656 | tf_op jit(solution)/shard_map/ppermute | solution.py:190
  145.1 28.5 %collective-permute-start.22 = (f32[2,128,512]{2,1,0:T(8,128)S(1)}, f32[2,128,512]{2,1,0:T(8,128)S(1)}, u32[]{:S(2)}, u32[]{:S(2)}) collective-permute-start(f32[2,128,512]{2,1,0:T(8,128)S(1)} %copy-done.8), channel_id=1, source_target_pairs={{0,2},{6,4},{1,3},{7,5},{8,10},{14,12},{9,11},{15,13},{16,18},{22,... | collective-permute-start | bytes 1572872 | tf_op jit(solution)/shard_map/ppermute | solution.py:117
  152.3 20.9 %collective-permute-start.24 = (f32[2,128,512]{2,1,0:T(8,128)S(1)}, f32[2,128,512]{2,1,0:T(8,128)S(1)}, u32[]{:S(2)}, u32[]{:S(2)}) collective-permute-start(f32[2,128,512]{2,1,0:T(8,128)S(1)} %copy-done.9), channel_id=1, source_target_pairs={{0,2},{6,4},{1,3},{7,5},{8,10},{14,12},{9,11},{15,13},{16,18},{22,... | collective-permute-start | bytes 1572872 | tf_op jit(solution)/shard_map/ppermute | solution.py:117
  153.6 44.5 %collective-permute-start.14 = (f32[12,128,128]{2,1,0:T(8,128)}, f32[12,128,128]{2,1,0:T(8,128)}, u32[]{:S(2)}, u32[]{:S(2)}) collective-permute-start(f32[12,128,128]{2,1,0:T(8,128)} %slice.100.refs_0_), channel_id=1, source_target_pairs={{2,0},{4,6},{3,1},{5,7},{10,8},{12,14},{11,9},{13,15},{18,16},{20,... | collective-permute-start | bytes 2359304 | tf_op jit(solution)/shard_map/ppermute | solution.py:117
  175.1 17.6 %collective-permute-start.25 = (f32[3,64,512]{2,1,0:T(8,128)}, f32[3,64,512]{2,1,0:T(8,128)}, u32[]{:S(2)}, u32[]{:S(2)}) collective-permute-start(f32[3,64,512]{2,1,0:T(8,128)} %dynamic-slice_bitcast_fusion), channel_id=1, source_target_pairs={{0,1},{1,0},{2,3},{3,2},{4,5},{5,4},{6,7},{7,6},{8,9},{9,8},{10,11... | collective-permute-start | bytes 1179656 | tf_op jit(solution)/shard_map/ppermute | solution.py:190
  187.1 13.9 %collective-permute-start.12 = (f32[6,128,128]{2,1,0:T(8,128)}, f32[6,128,128]{2,1,0:T(8,128)}, u32[]{:S(2)}, u32[]{:S(2)}) collective-permute-start(f32[6,128,128]{2,1,0:T(8,128)} %slice.98.refs_0_), channel_id=1, source_target_pairs={{2,0},{4,6},{3,1},{5,7},{10,8},{12,14},{11,9},{13,15},{18,16},{20,... | collective-permute-start | bytes 1179656 | tf_op jit(solution)/shard_map/ppermute | solution.py:117
  194.6 8.8 %collective-permute-start.26 = (f32[64,512]{1,0:T(8,128)}, f32[64,512]{1,0:T(8,128)}, u32[]{:S(2)}, u32[]{:S(2)}) collective-permute-start(f32[64,512]{1,0:T(8,128)} %get-tuple-element.64), channel_id=1, source_target_pairs={{0,8},{8,0},{16,24},{24,16},{1,9},{9,1},{17,25},{25,17},{2,10},{10... | collective-permute-start | bytes 393224 | tf_op jit(solution)/shard_map/ppermute | solution.py:202
  196.1 8.7 %collective-permute-start.27 = (f32[64,512]{1,0:T(8,128)}, f32[64,512]{1,0:T(8,128)}, u32[]{:S(2)}, u32[]{:S(2)}) collective-permute-start(f32[64,512]{1,0:T(8,128)} %get-tuple-element.65), channel_id=1, source_target_pairs={{0,16},{8,24},{16,0},{24,8},{1,17},{9,25},{17,1},{25,9},{2,18},{10... | collective-permute-start | bytes 393224 | tf_op jit(solution)/shard_map/ppermute | solution.py:202
  197.6 7.2 %collective-permute-start.28 = (f32[64,512]{1,0:T(8,128)}, f32[64,512]{1,0:T(8,128)}, u32[]{:S(2)}, u32[]{:S(2)}) collective-permute-start(f32[64,512]{1,0:T(8,128)} %get-tuple-element.66), channel_id=1, source_target_pairs={{0,24},{8,16},{16,8},{24,0},{1,25},{9,17},{17,9},{25,1},{2,26},{10... | collective-permute-start | bytes 393224 | tf_op jit(solution)/shard_map/ppermute | solution.py:202
  203.3 4.0 %collective-permute-start.16 = (f32[1,64,512]{2,1,0:T(8,128)S(1)}, f32[1,64,512]{2,1,0:T(8,128)S(1)}, u32[]{:S(2)}, u32[]{:S(2)}) collective-permute-start(f32[1,64,512]{2,1,0:T(8,128)S(1)} %dynamic-slice_bitcast_fusion.2), channel_id=1, source_target_pairs={{0,1},{1,0},{2,3},{3,2},{4,5},{5,4},{6,7},{7,6},{8,9},{9,8},{10,11... | collective-permute-start | bytes 393224 | tf_op jit(solution)/shard_map/ppermute | solution.py:190
  205.9 7.2 %collective-permute-start.29 = (f32[64,512]{1,0:T(8,128)S(1)}, f32[64,512]{1,0:T(8,128)S(1)}, u32[]{:S(2)}, u32[]{:S(2)}) collective-permute-start(f32[64,512]{1,0:T(8,128)S(1)} %fusion.3), channel_id=1, source_target_pairs={{2,0},{4,6},{3,1},{5,7},{10,8},{12,14},{11,9},{13,15},{18,16},{20,... | collective-permute-start | bytes 393224 | tf_op jit(solution)/shard_map/ppermute | solution.py:117
  207.4 5.8 %collective-permute-start.17 = (f32[64,512]{1,0:T(8,128)S(1)}, f32[64,512]{1,0:T(8,128)S(1)}, u32[]{:S(2)}, u32[]{:S(2)}) collective-permute-start(f32[64,512]{1,0:T(8,128)S(1)} %get-tuple-element.61), channel_id=1, source_target_pairs={{0,8},{8,0},{16,24},{24,16},{1,9},{9,1},{17,25},{25,17},{2,10},{10... | collective-permute-start | bytes 393224 | tf_op jit(solution)/shard_map/ppermute | solution.py:202
  208.7 7.8 %collective-permute-start.18 = (f32[64,512]{1,0:T(8,128)S(1)}, f32[64,512]{1,0:T(8,128)S(1)}, u32[]{:S(2)}, u32[]{:S(2)}) collective-permute-start(f32[64,512]{1,0:T(8,128)S(1)} %get-tuple-element.62), channel_id=1, source_target_pairs={{0,16},{8,24},{16,0},{24,8},{1,17},{9,25},{17,1},{25,9},{2,18},{10... | collective-permute-start | bytes 393224 | tf_op jit(solution)/shard_map/ppermute | solution.py:202
  209.5 7.0 %collective-permute-start.19 = (f32[64,512]{1,0:T(8,128)S(1)}, f32[64,512]{1,0:T(8,128)S(1)}, u32[]{:S(2)}, u32[]{:S(2)}) collective-permute-start(f32[64,512]{1,0:T(8,128)S(1)} %get-tuple-element.63), channel_id=1, source_target_pairs={{0,24},{8,16},{16,8},{24,0},{1,25},{9,17},{17,9},{25,1},{2,26},{10... | collective-permute-start | bytes 393224 | tf_op jit(solution)/shard_map/ppermute | solution.py:202
  (8 other events, 23.9 us)

commit v6 on v5

--- a/solution.py
+++ b/solution.py
@@ -73,7 +73,6 @@
         in_specs.append(whole)
         aliases = {len(operands) + 1: 0}
         operands.append(total)
-    units = steps * per * depth
     return pl.pallas_call(
         functools.partial(contract_kernel, terms, per, total is None),
         out_shape=jax.ShapeDtypeStruct(shape, jnp.float32),
@@ -82,11 +81,6 @@
         ),
         input_output_aliases=aliases,
         compiler_params=pltpu.CompilerParams(vmem_limit_bytes=40 << 20),
-        cost_estimate=pl.CostEstimate(
-            flops=6 * units * len(slots) * block * width,
-            bytes_accessed=4 * (units * (width + sum(terms) * block) + 2 * len(slots) * block * width),
-            transcendentals=0,
-        ),
     )(jnp.reshape(offset, (1,)).astype(jnp.int32), *operands)
 
 
@@ -121,7 +115,7 @@
 
     lent = round(ko * 2 * block / (3 * block + width)) - 1
     base = ko - lent
-    main = bounds(0, base - base // 2, base // 2)
+    main = bounds(0, base // 2, base - base // 2)
     extra = (base, ko)
     pieces = bounds(base, *[lent // 5 + (i < lent % 5) for i in range(5)])
     ends = []

time: 219 us -> 231 us (1.055)
  waiting for transfers between devices: 79.5 us -> 108 us
  starting transfers between devices: 66.3 us -> 50.9 us
    ppermute x21, waiting for transfers between devices: 74.7 us -> 106 us  [hop(): return lambda value: lax.ppermute(value, 'col', lanes)]
    ppermute x21, starting transfers between devices: 59.2 us -> 43.3 us  [hop(): return lambda value: lax.ppermute(value, 'col', lanes)]
    slice x10 -> x9, local copies, waits for them, and re-layouts: 12.2 us -> 7.27 us  [find(): return value if (k0, k1) == c else value[c[0] - k0:c[1] - k0]]
    ppermute x6, waiting for transfers between devices: 4.8 us -> 2.11 us  [row_sum(): lax.ppermute(part(row ^ t), 'row', [(r, r ^ t) for r in range(4)])]
    pallas_call x18 -> x19, Pallas kernels: 43.8 us -> 42.2 us  [contract_run(): pl.pallas_call(functools.partial(contract_kernel, terms, per, total is No...]
  transfers between devices with their start and end apart: 30 -> 30, of which waited for: 9 -> 8; matrix products, arithmetic and copies ran while one was open for 11% -> 9% of each run, Pallas kernels for 20% -> 18%
where the time goes in v6:
time: 231 us; the launch traced here: 229 us
  waiting for transfers between devices  108 us (47%)
  starting transfers between devices  50.9 us (22%)
  Pallas kernels  42.2 us (18%)
  local copies, waits for them, and re-layouts  22.2 us (10%)
  other arithmetic  4.79 us (2%)
    ppermute x21, waiting for transfers between devices, hop(): return lambda value: lax.ppermute(value, 'col', lanes)  106 us
    ppermute x21, starting transfers between devices, hop(): return lambda value: lax.ppermute(value, 'col', lanes)  43.3 us
    pallas_call x19, Pallas kernels, contract_run(): pl.pallas_call(functools.partial(contract_kernel, terms, per, total is No...  42.2 us
    slice x9, local copies, waits for them, and re-layouts, find(): return value if (k0, k1) == c else value[c[0] - k0:c[1] - k0]  7.27 us
    ppermute x6, starting transfers between devices, row_sum(): lax.ppermute(part(row ^ t), 'row', [(r, r ^ t) for r in range(4)])  7.04 us
  transfers between devices with their start and end apart: 30, of which 8 were waited for; matrix products, arithmetic and copies ran while one was open for 9% of the time, Pallas kernels for 18%

profile of v6, /device:TPU:0, one launch (start us, length us, event | category | flops | bytes accessed | tf_op | source)
XLA Modules:
  0.0 229.1 jit_solution(2709108462981064128)
XLA Ops:
  0.0 2.4 %slice.78 = f32[9,256,128]{2,1,0:T(8,128)} slice(f32[25,256,128]{2,1,0:T(8,128)} %param.2), slice={[0:9], [0:256], [0:128]} | slice | bytes 2359296 | tf_op jit(solution)/shard_map/slice | solution.py:126
  4.5 5.8 %collective-permute-start = (f32[18,128,128]{2,1,0:T(8,128)}, f32[18,128,128]{2,1,0:T(8,128)}, u32[]{:S(2)}, u32[]{:S(2)}) collective-permute-start(f32[18,128,128]{2,1,0:T(8,128)} %bitcast.2.refs_0_), channel_id=1, source_target_pairs={{0,2},{2,0},{4,6},{6,4},{1,3},{3,1},{5,7},{7,5},{8,10},{10,8},{12,... | collective-permute-start | bytes 3538952 | tf_op jit(solution)/shard_map/ppermute | solution.py:111
  10.5 1.7 collective-permute-start.2
  12.1 2.1 slice.80.refs_0_
  14.3 23.3 %collective-permute-done.refs_1_ = f32[18,128,128]{2,1,0:T(8,128)} collective-permute-done((f32[18,128,128]{2,1,0:T(8,128)}, f32[18,128,128]{2,1,0:T(8,128)}, u32[]{:S(2)}, u32[]{:S(2)}) %collective-permute-start) | collective-permute-done | bytes 1179680 | tf_op jit(solution)/shard_map/ppermute | solution.py:111
  37.5 4.9 %collective-permute-start.1 = (f32[13,128,128]{2,1,0:T(8,128)}, f32[13,128,128]{2,1,0:T(8,128)}, u32[]{:S(2)}, u32[]{:S(2)}) collective-permute-start(f32[13,128,128]{2,1,0:T(8,128)} %slice.80.refs_0_), channel_id=1, source_target_pairs={{0,2},{6,4},{1,3},{7,5},{8,10},{14,12},{9,11},{15,13},{16,18},{22,... | collective-permute-start | bytes 2555912 | tf_op jit(solution)/shard_map/ppermute | solution.py:111
  42.5 1.7 collective-permute-start.10
  44.2 3.1 %constant_dynamic-slice_fusion = (f32[3,128,512]{2,1,0:T(8,128)}, f32[3,128,512]{2,1,0:T(8,128)}, f32[3,128,512]{2,1,0:T(8,128)}) fusion(f32[200,128,512]{2,1,0:T(8,128)} %bitcast.61, s32[]{:T(128)S(6)} %select_n.85, s32[]{:T(128)S(6)} %select_n.83, s32[]{:T(128)S(6)} %select_n.82), kind=kLoop, calls=%fused_computation.37 | loop fusion | bytes 4718604 | tf_op jit(solution)/shard_map/dynamic_slice | solution.py:143
  47.2 16.5 %collective-permute-done.4.refs_1_ = f32[19,128,128]{2,1,0:T(8,128)} collective-permute-done((f32[19,128,128]{2,1,0:T(8,128)S(1)}, f32[19,128,128]{2,1,0:T(8,128)}, u32[]{:S(2)}, u32[]{:S(2)}) %collective-permute-start.4) | collective-permute-done | bytes 1245216 | tf_op jit(solution)/shard_map/ppermute | solution.py:111
  63.7 5.4 %collective-permute-start.20 = (f32[3,128,512]{2,1,0:T(8,128)}, f32[3,128,512]{2,1,0:T(8,128)}, u32[]{:S(2)}, u32[]{:S(2)}) collective-permute-start(f32[3,128,512]{2,1,0:T(8,128)} %get-tuple-element.36), channel_id=1, source_target_pairs={{0,2},{6,4},{1,3},{7,5},{8,10},{14,12},{9,11},{15,13},{16,18},{22,... | collective-permute-start | bytes 2359304 | tf_op jit(solution)/shard_map/ppermute | solution.py:111
  71.1 26.3 %collective-permute-done.20.refs_3_.refs_4_.refs_5_ = f32[3,128,512]{2,1,0:T(8,128)} collective-permute-done((f32[3,128,512]{2,1,0:T(8,128)}, f32[3,128,512]{2,1,0:T(8,128)}, u32[]{:S(2)}, u32[]{:S(2)}) %collective-permute-start.20) | collective-permute-done | bytes 786464 | tf_op jit(solution)/shard_map/ppermute | solution.py:111
  98.7 4.7 %collective-permute-start.21 = (f32[3,128,512]{2,1,0:T(8,128)}, f32[3,128,512]{2,1,0:T(8,128)S(1)}, u32[]{:S(2)}, u32[]{:S(2)}) collective-permute-start(f32[3,128,512]{2,1,0:T(8,128)} %get-tuple-element.37), channel_id=1, source_target_pairs={{0,2},{6,4},{1,3},{7,5},{8,10},{14,12},{9,11},{15,13},{16,18},{22,... | collective-permute-start | bytes 2359304 | tf_op jit(solution)/shard_map/ppermute | solution.py:111
  109.0 12.7 %collective-permute-done.21.refs_3_.refs_4_.refs_5_ = f32[3,128,512]{2,1,0:T(8,128)S(1)} collective-permute-done((f32[3,128,512]{2,1,0:T(8,128)}, f32[3,128,512]{2,1,0:T(8,128)S(1)}, u32[]{:S(2)}, u32[]{:S(2)}) %collective-permute-start.21) | collective-permute-done | bytes 786464 | tf_op jit(solution)/shard_map/ppermute | solution.py:111
  122.4 13.5 %collective-permute-done.23.refs_3_.refs_4_.refs_5_ = f32[3,128,512]{2,1,0:T(8,128)S(1)} collective-permute-done((f32[3,128,512]{2,1,0:T(8,128)}, f32[3,128,512]{2,1,0:T(8,128)S(1)}, u32[]{:S(2)}, u32[]{:S(2)}) %collective-permute-start.23) | collective-permute-done | bytes 786464 | tf_op jit(solution)/shard_map/ppermute | solution.py:111
  136.0 4.3 %collective-permute-start.22 = (f32[2,128,512]{2,1,0:T(8,128)S(1)}, f32[2,128,512]{2,1,0:T(8,128)S(1)}, u32[]{:S(2)}, u32[]{:S(2)}) collective-permute-start(f32[2,128,512]{2,1,0:T(8,128)S(1)} %get-tuple-element.38), channel_id=1, source_target_pairs={{0,2},{6,4},{1,3},{7,5},{8,10},{14,12},{9,11},{15,13},{16,18},{22,... | collective-permute-start | bytes 1572872 | tf_op jit(solution)/shard_map/ppermute | solution.py:111
  141.6 2.2 fusion.21
  147.6 1.8 shard_map.42.refs_6_
  150.9 9.5 %collective-permute-done.24.refs_3_.refs_4_ = f32[2,128,512]{2,1,0:T(8,128)S(1)} collective-permute-done((f32[2,128,512]{2,1,0:T(8,128)S(1)}, f32[2,128,512]{2,1,0:T(8,128)S(1)}, u32[]{:S(2)}, u32[]{:S(2)}) %collective-permute-start.24) | collective-permute-done | bytes 524320 | tf_op jit(solution)/shard_map/ppermute | solution.py:111
  165.8 6.1 %shard_map.28.refs_10_ = f32[3,128,512]{2,1,0:T(8,128)S(1)} custom-call(s32[1]{0:T(128)} %bitcast.7.offset_ref, f32[18,128,128]{2,1,0:T(8,128)} %bitcast.2.refs_0_, f32[18,128,128]{2,1,0:T(8,128)} %collective-permute-done.refs_1_, f32[18,128,128]{2,1,0:T(8,128)} %collective-permute-done.2.refs_2_, f32[18,128,128]{2,1,0:T(8,128)} %collective-permute-done.7.refs_3_, ...), custom_call_target="tpu_custom_call" | custom-call | tf_op jit(solution)/shard_map/pallas_call | solution.py:76
  171.9 5.4 %shard_map.29.refs_5_ = f32[3,128,512]{2,1,0:T(8,128)S(1)} custom-call(s32[1]{0:T(128)} %bitcast.6.offset_ref, f32[19,128,128]{2,1,0:T(8,128)S(1)} %slice.81.refs_0_, f32[19,128,128]{2,1,0:T(8,128)} %collective-permute-done.4.refs_1_, f32[19,128,128]{2,1,0:T(8,128)S(1)} %collective-permute-done.5.refs_2_, ...), custom_call_target="tpu_custom_call", output_to_operand_aliasing={{}: (11, {})} | custom-call | tf_op jit(solution)/shard_map/pallas_call | solution.py:76
  178.9 4.1 %shard_map.31.refs_4_ = f32[3,128,512]{2,1,0:T(8,128)S(1)} custom-call(s32[1]{0:T(128)} %bitcast.offset_ref, f32[13,128,128]{2,1,0:T(8,128)} %slice.80.refs_0_, f32[13,128,128]{2,1,0:T(8,128)} %collective-permute-done.1.refs_1_, f32[13,128,128]{2,1,0:T(8,128)S(1)} %copy-done.3, f32[200,128,512]{2,1,0:T(8,128)} %bitcast.76, ...), custom_call_target="tpu_custom_call", output_to_operand_aliasing={{}: (10, {})} | custom-call | tf_op jit(solution)/shard_map/pallas_call | solution.py:76
  185.7 1.8 slice.101.refs_0_
  194.3 1.8 bitcast_add_fusion.1
  196.2 1.8 shard_map.33.refs_3_
  198.0 2.5 %shard_map.34.refs_8_ = f32[1,128,512]{2,1,0:T(8,128)S(1)} custom-call(s32[1]{0:T(128)} %bitcast.7.offset_ref, f32[9,128,128]{2,1,0:T(8,128)S(1)} %copy-done.7, f32[9,128,128]{2,1,0:T(8,128)S(1)} %copy-done.11, f32[200,128,512]{2,1,0:T(8,128)} %bitcast.89, f32[1,128,512]{2,1,0:T(8,128)S(1)} %shard_map.33.refs_3_), custom_call_target="tpu_custom_call", output_to_operand_aliasing={{}: (4, {})} | custom-call | tf_op jit(solution)/shard_map/pallas_call | solution.py:76
  200.5 2.1 shard_map.35.refs_3_
  202.7 2.7 %shard_map.36.refs_7_ = f32[1,128,512]{2,1,0:T(8,128)S(1)} custom-call(s32[1]{0:T(128)} %bitcast.12.offset_ref, f32[9,128,128]{2,1,0:T(8,128)} %get-tuple-element.30.refs_0_, f32[9,128,128]{2,1,0:T(8,128)} %collective-permute-done.11.refs_1_, f32[200,128,512]{2,1,0:T(8,128)} %bitcast.96, ...), custom_call_target="tpu_custom_call", output_to_operand_aliasing={{}: (4, {})} | custom-call | tf_op jit(solution)/shard_map/pallas_call | solution.py:76
  205.4 2.6 %shard_map.37.refs_2_ = f32[1,128,512]{2,1,0:T(8,128)S(1)} custom-call(s32[1]{0:T(128)} %bitcast.offset_ref, f32[13,128,128]{2,1,0:T(8,128)S(1)} %copy-done.5, f32[200,128,512]{2,1,0:T(8,128)} %bitcast.100, f32[200,128,512]{2,1,0:T(8,128)} %bitcast.98, f32[200,128,512]{2,1,0:T(8,128)} %bitcast.99, ...), custom_call_target="tpu_custom_call", output_to_operand_aliasing={{}: (8, {})} | custom-call | tf_op jit(solution)/shard_map/pallas_call | solution.py:76
  209.2 3.0 %shard_map.39.refs_3_ = f32[1,128,512]{2,1,0:T(8,128)S(1)} custom-call(s32[1]{0:T(128)} %bitcast.6.offset_ref, f32[13,128,128]{2,1,0:T(8,128)} %slice.103.refs_0_, f32[13,128,128]{2,1,0:T(8,128)} %collective-permute-done.14.refs_1_, f32[200,128,512]{2,1,0:T(8,128)} %bitcast.104, f32[200,128,512]{2,1,0:T(8,128)} %bitcast.105, ...), custom_call_target="tpu_custom_call", output_to_operand_aliasing={{}: (9, {})} | custom-call | tf_op jit(solution)/shard_map/pallas_call | solution.py:76
  213.5 2.2 shard_map.41
  221.9 4.3 %collective-permute-done.29 = f32[64,512]{1,0:T(8,128)S(1)} collective-permute-done((f32[64,512]{1,0:T(8,128)S(1)}, f32[64,512]{1,0:T(8,128)S(1)}, u32[]{:S(2)}, u32[]{:S(2)}) %collective-permute-start.29) | collective-permute-done | bytes 131104 | tf_op jit(solution)/shard_map/ppermute | solution.py:111
  226.2 2.1 collective-permute-done.18
  (103 shorter events, 43.9 us)
Async XLA Ops:
  3.8 38.7 %collective-permute-start.5 = (f32[19,128,128]{2,1,0:T(8,128)S(1)}, f32[19,128,128]{2,1,0:T(8,128)S(1)}, u32[]{:S(2)}, u32[]{:S(2)}) collective-permute-start(f32[19,128,128]{2,1,0:T(8,128)S(1)} %slice.81.refs_0_), channel_id=1, source_target_pairs={{2,4},{4,2},{3,5},{5,3},{10,12},{12,10},{11,13},{13,11},{18,20},{2... | collective-permute-start | bytes 3735560 | tf_op jit(solution)/shard_map/ppermute | solution.py:111
  4.5 33.0 %collective-permute-start = (f32[18,128,128]{2,1,0:T(8,128)}, f32[18,128,128]{2,1,0:T(8,128)}, u32[]{:S(2)}, u32[]{:S(2)}) collective-permute-start(f32[18,128,128]{2,1,0:T(8,128)} %bitcast.2.refs_0_), channel_id=1, source_target_pairs={{0,2},{2,0},{4,6},{6,4},{1,3},{3,1},{5,7},{7,5},{8,10},{10,8},{12,... | collective-permute-start | bytes 3538952 | tf_op jit(solution)/shard_map/ppermute | solution.py:111
  10.4 53.3 %collective-permute-start.4 = (f32[19,128,128]{2,1,0:T(8,128)S(1)}, f32[19,128,128]{2,1,0:T(8,128)}, u32[]{:S(2)}, u32[]{:S(2)}) collective-permute-start(f32[19,128,128]{2,1,0:T(8,128)S(1)} %slice.81.refs_0_), channel_id=1, source_target_pairs={{0,2},{2,0},{4,6},{6,4},{1,3},{3,1},{5,7},{7,5},{8,10},{10,8},{12,... | collective-permute-start | bytes 3735560 | tf_op jit(solution)/shard_map/ppermute | solution.py:111
  10.5 58.6 %collective-permute-start.2 = (f32[18,128,128]{2,1,0:T(8,128)}, f32[18,128,128]{2,1,0:T(8,128)}, u32[]{:S(2)}, u32[]{:S(2)}) collective-permute-start(f32[18,128,128]{2,1,0:T(8,128)} %bitcast.2.refs_0_), channel_id=1, source_target_pairs={{2,4},{4,2},{3,5},{5,3},{10,12},{12,10},{11,13},{13,11},{18,20},{2... | collective-permute-start | bytes 3538952 | tf_op jit(solution)/shard_map/ppermute | solution.py:111
  37.5 61.2 %collective-permute-start.1 = (f32[13,128,128]{2,1,0:T(8,128)}, f32[13,128,128]{2,1,0:T(8,128)}, u32[]{:S(2)}, u32[]{:S(2)}) collective-permute-start(f32[13,128,128]{2,1,0:T(8,128)} %slice.80.refs_0_), channel_id=1, source_target_pairs={{0,2},{6,4},{1,3},{7,5},{8,10},{14,12},{9,11},{15,13},{16,18},{22,... | collective-permute-start | bytes 2555912 | tf_op jit(solution)/shard_map/ppermute | solution.py:111
  42.5 62.1 %collective-permute-start.10 = (f32[18,128,128]{2,1,0:T(8,128)}, f32[18,128,128]{2,1,0:T(8,128)}, u32[]{:S(2)}, u32[]{:S(2)}) collective-permute-start(f32[18,128,128]{2,1,0:T(8,128)} %collective-permute-done.refs_1_), channel_id=1, source_target_pairs={{2,4},{4,2},{3,5},{5,3},{10,12},{12,10},{11,13},{13,11},{18,20},{2... | collective-permute-start | bytes 3538952 | tf_op jit(solution)/shard_map/ppermute | solution.py:111
  63.7 33.8 %collective-permute-start.20 = (f32[3,128,512]{2,1,0:T(8,128)}, f32[3,128,512]{2,1,0:T(8,128)}, u32[]{:S(2)}, u32[]{:S(2)}) collective-permute-start(f32[3,128,512]{2,1,0:T(8,128)} %get-tuple-element.36), channel_id=1, source_target_pairs={{0,2},{6,4},{1,3},{7,5},{8,10},{14,12},{9,11},{15,13},{16,18},{22,... | collective-permute-start | bytes 2359304 | tf_op jit(solution)/shard_map/ppermute | solution.py:111
  69.1 37.8 %collective-permute-start.3 = (f32[13,128,128]{2,1,0:T(8,128)}, f32[13,128,128]{2,1,0:T(8,128)S(1)}, u32[]{:S(2)}, u32[]{:S(2)}) collective-permute-start(f32[13,128,128]{2,1,0:T(8,128)} %slice.80.refs_0_), channel_id=1, source_target_pairs={{2,4},{4,2},{3,5},{5,3},{10,12},{12,10},{11,13},{13,11},{18,20},{2... | collective-permute-start | bytes 2555912 | tf_op jit(solution)/shard_map/ppermute | solution.py:111
  69.8 70.5 %collective-permute-start.7 = (f32[18,128,128]{2,1,0:T(8,128)}, f32[18,128,128]{2,1,0:T(8,128)}, u32[]{:S(2)}, u32[]{:S(2)}) collective-permute-start(f32[18,128,128]{2,1,0:T(8,128)} %collective-permute-done.2.refs_2_), channel_id=1, source_target_pairs={{2,0},{4,6},{3,1},{5,7},{10,8},{12,14},{11,9},{13,15},{18,16},{20,... | collective-permute-start | bytes 3538952 | tf_op jit(solution)/shard_map/ppermute | solution.py:111
  97.4 46.4 %collective-permute-start.6 = (f32[19,128,128]{2,1,0:T(8,128)S(1)}, f32[19,128,128]{2,1,0:T(8,128)S(1)}, u32[]{:S(2)}, u32[]{:S(2)}) collective-permute-start(f32[19,128,128]{2,1,0:T(8,128)S(1)} %collective-permute-done.5.refs_2_), channel_id=1, source_target_pairs={{2,0},{4,6},{3,1},{5,7},{10,8},{12,14},{11,9},{13,15},{18,16},{20,... | collective-permute-start | bytes 3735560 | tf_op jit(solution)/shard_map/ppermute | solution.py:111
  98.7 22.9 %collective-permute-start.21 = (f32[3,128,512]{2,1,0:T(8,128)}, f32[3,128,512]{2,1,0:T(8,128)S(1)}, u32[]{:S(2)}, u32[]{:S(2)}) collective-permute-start(f32[3,128,512]{2,1,0:T(8,128)} %get-tuple-element.37), channel_id=1, source_target_pairs={{0,2},{6,4},{1,3},{7,5},{8,10},{14,12},{9,11},{15,13},{16,18},{22,... | collective-permute-start | bytes 2359304 | tf_op jit(solution)/shard_map/ppermute | solution.py:111
  104.6 31.4 %collective-permute-start.23 = (f32[3,128,512]{2,1,0:T(8,128)}, f32[3,128,512]{2,1,0:T(8,128)S(1)}, u32[]{:S(2)}, u32[]{:S(2)}) collective-permute-start(f32[3,128,512]{2,1,0:T(8,128)} %get-tuple-element.39), channel_id=1, source_target_pairs={{0,2},{6,4},{1,3},{7,5},{8,10},{14,12},{9,11},{15,13},{16,18},{22,... | collective-permute-start | bytes 2359304 | tf_op jit(solution)/shard_map/ppermute | solution.py:111
  106.9 15.5 %copy-start.2 = (f32[13,128,128]{2,1,0:T(8,128)}, f32[13,128,128]{2,1,0:T(8,128)S(1)}, u32[]{:S(2)}) copy-start(f32[13,128,128]{2,1,0:T(8,128)S(1)} %collective-permute-done.3.refs_2_) | copy-start | bytes 2555908
  106.9 39.2 %collective-permute-start.15 = (f32[13,128,128]{2,1,0:T(8,128)}, f32[13,128,128]{2,1,0:T(8,128)S(1)}, u32[]{:S(2)}, u32[]{:S(2)}) collective-permute-start(f32[13,128,128]{2,1,0:T(8,128)} %collective-permute-done.1.refs_1_), channel_id=1, source_target_pairs={{2,4},{4,2},{3,5},{5,3},{10,12},{12,10},{11,13},{13,11},{18,20},{2... | collective-permute-start | bytes 2555912 | tf_op jit(solution)/shard_map/ppermute | solution.py:111
  121.7 40.6 %collective-permute-start.9 = (f32[19,128,128]{2,1,0:T(8,128)}, f32[19,128,128]{2,1,0:T(8,128)S(1)}, u32[]{:S(2)}, u32[]{:S(2)}) collective-permute-start(f32[19,128,128]{2,1,0:T(8,128)} %collective-permute-done.4.refs_1_), channel_id=1, source_target_pairs={{2,4},{4,2},{3,5},{5,3},{10,12},{12,10},{11,13},{13,11},{18,20},{2... | collective-permute-start | bytes 3735560 | tf_op jit(solution)/shard_map/ppermute | solution.py:111
  136.0 24.9 %collective-permute-start.22 = (f32[2,128,512]{2,1,0:T(8,128)S(1)}, f32[2,128,512]{2,1,0:T(8,128)S(1)}, u32[]{:S(2)}, u32[]{:S(2)}) collective-permute-start(f32[2,128,512]{2,1,0:T(8,128)S(1)} %get-tuple-element.38), channel_id=1, source_target_pairs={{0,2},{6,4},{1,3},{7,5},{8,10},{14,12},{9,11},{15,13},{16,18},{22,... | collective-permute-start | bytes 1572872 | tf_op jit(solution)/shard_map/ppermute | solution.py:111
  140.3 20.1 %collective-permute-start.24 = (f32[2,128,512]{2,1,0:T(8,128)S(1)}, f32[2,128,512]{2,1,0:T(8,128)S(1)}, u32[]{:S(2)}, u32[]{:S(2)}) collective-permute-start(f32[2,128,512]{2,1,0:T(8,128)S(1)} %get-tuple-element.40), channel_id=1, source_target_pairs={{0,2},{6,4},{1,3},{7,5},{8,10},{14,12},{9,11},{15,13},{16,18},{22,... | collective-permute-start | bytes 1572872 | tf_op jit(solution)/shard_map/ppermute | solution.py:111
  144.9 18.5 %collective-permute-start.13 = (f32[9,128,128]{2,1,0:T(8,128)S(1)}, f32[9,128,128]{2,1,0:T(8,128)S(1)}, u32[]{:S(2)}, u32[]{:S(2)}) collective-permute-start(f32[9,128,128]{2,1,0:T(8,128)S(1)} %get-tuple-element.32.refs_0_), channel_id=1, source_target_pairs={{2,0},{4,6},{3,1},{5,7},{10,8},{12,14},{11,9},{13,15},{18,16},{20,... | collective-permute-start | bytes 1769480 | tf_op jit(solution)/shard_map/ppermute | solution.py:111
  146.2 41.3 %collective-permute-start.11 = (f32[9,128,128]{2,1,0:T(8,128)}, f32[9,128,128]{2,1,0:T(8,128)}, u32[]{:S(2)}, u32[]{:S(2)}) collective-permute-start(f32[9,128,128]{2,1,0:T(8,128)} %get-tuple-element.30.refs_0_), channel_id=1, source_target_pairs={{2,0},{4,6},{3,1},{5,7},{10,8},{12,14},{11,9},{13,15},{18,16},{20,... | collective-permute-start | bytes 1769480 | tf_op jit(solution)/shard_map/ppermute | solution.py:111
  162.3 26.7 %collective-permute-start.25 = (f32[3,64,512]{2,1,0:T(8,128)}, f32[3,64,512]{2,1,0:T(8,128)}, u32[]{:S(2)}, u32[]{:S(2)}) collective-permute-start(f32[3,64,512]{2,1,0:T(8,128)} %dynamic-slice_bitcast_fusion), channel_id=1, source_target_pairs={{0,1},{1,0},{2,3},{3,2},{4,5},{5,4},{6,7},{7,6},{8,9},{9,8},{10,11... | collective-permute-start | bytes 1179656 | tf_op jit(solution)/shard_map/ppermute | solution.py:184
  164.5 44.8 %collective-permute-start.14 = (f32[13,128,128]{2,1,0:T(8,128)}, f32[13,128,128]{2,1,0:T(8,128)}, u32[]{:S(2)}, u32[]{:S(2)}) collective-permute-start(f32[13,128,128]{2,1,0:T(8,128)} %slice.103.refs_0_), channel_id=1, source_target_pairs={{2,0},{4,6},{3,1},{5,7},{10,8},{12,14},{11,9},{13,15},{18,16},{20,... | collective-permute-start | bytes 2555912 | tf_op jit(solution)/shard_map/ppermute | solution.py:111
  185.2 8.7 %collective-permute-start.8 = (f32[3,64,512]{2,1,0:T(8,128)}, f32[3,64,512]{2,1,0:T(8,128)}, u32[]{:S(2)}, u32[]{:S(2)}) collective-permute-start(f32[3,64,512]{2,1,0:T(8,128)} %dynamic-slice_bitcast_fusion.1), channel_id=1, source_target_pairs={{0,1},{1,0},{2,3},{3,2},{4,5},{5,4},{6,7},{7,6},{8,9},{9,8},{10,11... | collective-permute-start | bytes 1179656 | tf_op jit(solution)/shard_map/ppermute | solution.py:184
  187.5 26.0 %collective-permute-start.12 = (f32[6,128,128]{2,1,0:T(8,128)}, f32[6,128,128]{2,1,0:T(8,128)}, u32[]{:S(2)}, u32[]{:S(2)}) collective-permute-start(f32[6,128,128]{2,1,0:T(8,128)} %slice.101.refs_0_), channel_id=1, source_target_pairs={{2,0},{4,6},{3,1},{5,7},{10,8},{12,14},{11,9},{13,15},{18,16},{20,... | collective-permute-start | bytes 1179656 | tf_op jit(solution)/shard_map/ppermute | solution.py:111
  190.1 8.0 %copy-start.12 = (f32[3,64,512]{2,1,0:T(8,128)}, f32[3,64,512]{2,1,0:T(8,128)S(1)}, u32[]{:S(2)}) copy-start(f32[3,64,512]{2,1,0:T(8,128)S(1)} %bitcast_add_fusion) | copy-start | bytes 1179652
  190.8 24.9 %collective-permute-start.26 = (f32[64,512]{1,0:T(8,128)}, f32[64,512]{1,0:T(8,128)}, u32[]{:S(2)}, u32[]{:S(2)}) collective-permute-start(f32[64,512]{1,0:T(8,128)} %get-tuple-element.66), channel_id=1, source_target_pairs={{0,8},{8,0},{16,24},{24,16},{1,9},{9,1},{17,25},{25,17},{2,10},{10... | collective-permute-start | bytes 393224 | tf_op jit(solution)/shard_map/ppermute | solution.py:196
  192.3 23.5 %collective-permute-start.27 = (f32[64,512]{1,0:T(8,128)}, f32[64,512]{1,0:T(8,128)}, u32[]{:S(2)}, u32[]{:S(2)}) collective-permute-start(f32[64,512]{1,0:T(8,128)} %get-tuple-element.67), channel_id=1, source_target_pairs={{0,16},{8,24},{16,0},{24,8},{1,17},{9,25},{17,1},{25,9},{2,18},{10... | collective-permute-start | bytes 393224 | tf_op jit(solution)/shard_map/ppermute | solution.py:196
  193.9 21.9 %collective-permute-start.28 = (f32[64,512]{1,0:T(8,128)}, f32[64,512]{1,0:T(8,128)}, u32[]{:S(2)}, u32[]{:S(2)}) collective-permute-start(f32[64,512]{1,0:T(8,128)} %get-tuple-element.68), channel_id=1, source_target_pairs={{0,24},{8,16},{16,8},{24,0},{1,25},{9,17},{17,9},{25,1},{2,26},{10... | collective-permute-start | bytes 393224 | tf_op jit(solution)/shard_map/ppermute | solution.py:196
  215.7 2.5 %collective-permute-start.16 = (f32[1,64,512]{2,1,0:T(8,128)S(1)}, f32[1,64,512]{2,1,0:T(8,128)S(1)}, u32[]{:S(2)}, u32[]{:S(2)}) collective-permute-start(f32[1,64,512]{2,1,0:T(8,128)S(1)} %dynamic-slice_bitcast_fusion.2), channel_id=1, source_target_pairs={{0,1},{1,0},{2,3},{3,2},{4,5},{5,4},{6,7},{7,6},{8,9},{9,8},{10,11... | collective-permute-start | bytes 393224 | tf_op jit(solution)/shard_map/ppermute | solution.py:184
  216.9 9.3 %collective-permute-start.29 = (f32[64,512]{1,0:T(8,128)S(1)}, f32[64,512]{1,0:T(8,128)S(1)}, u32[]{:S(2)}, u32[]{:S(2)}) collective-permute-start(f32[64,512]{1,0:T(8,128)S(1)} %fusion.3), channel_id=1, source_target_pairs={{2,0},{4,6},{3,1},{5,7},{10,8},{12,14},{11,9},{13,15},{18,16},{20,... | collective-permute-start | bytes 393224 | tf_op jit(solution)/shard_map/ppermute | solution.py:111
  218.4 7.9 %collective-permute-start.17 = (f32[64,512]{1,0:T(8,128)S(1)}, f32[64,512]{1,0:T(8,128)S(1)}, u32[]{:S(2)}, u32[]{:S(2)}) collective-permute-start(f32[64,512]{1,0:T(8,128)S(1)} %get-tuple-element.63), channel_id=1, source_target_pairs={{0,8},{8,0},{16,24},{24,16},{1,9},{9,1},{17,25},{25,17},{2,10},{10... | collective-permute-start | bytes 393224 | tf_op jit(solution)/shard_map/ppermute | solution.py:196
  219.9 8.4 %collective-permute-start.18 = (f32[64,512]{1,0:T(8,128)S(1)}, f32[64,512]{1,0:T(8,128)S(1)}, u32[]{:S(2)}, u32[]{:S(2)}) collective-permute-start(f32[64,512]{1,0:T(8,128)S(1)} %get-tuple-element.64), channel_id=1, source_target_pairs={{0,16},{8,24},{16,0},{24,8},{1,17},{9,25},{17,1},{25,9},{2,18},{10... | collective-permute-start | bytes 393224 | tf_op jit(solution)/shard_map/ppermute | solution.py:196
  221.5 6.9 %collective-permute-start.19 = (f32[64,512]{1,0:T(8,128)S(1)}, f32[64,512]{1,0:T(8,128)S(1)}, u32[]{:S(2)}, u32[]{:S(2)}) collective-permute-start(f32[64,512]{1,0:T(8,128)S(1)} %get-tuple-element.65), channel_id=1, source_target_pairs={{0,24},{8,16},{16,8},{24,0},{1,25},{9,17},{17,9},{25,1},{2,26},{10... | collective-permute-start | bytes 393224 | tf_op jit(solution)/shard_map/ppermute | solution.py:196
  (14 other events, 44.2 us)

commit v7 on v6

--- a/solution.py
+++ b/solution.py
@@ -86,7 +86,9 @@
 
 def contract(slots, weights, offset, total):
     count = slots[0][0].shape[0]
-    per = min(6, count)
+    per = max(n for n in range(1, 7) if count % n == 0)
+    if per < 3:
+        per = min(6, count)
     total = contract_run(slots, weights, offset, total, 0, per, count // per)
     left = count % per
     if left:
@@ -118,62 +120,117 @@
     main = bounds(0, base // 2, base - base // 2)
     extra = (base, ko)
     pieces = bounds(base, *[lent // 5 + (i < lent % 5) for i in range(5)])
-    ends = []
-    for start, stop in main:
-        cut = (stop - start) // 2 if not ends else (stop - start) // 3
-        ends += bounds(start, stop - start - cut, cut)
-
-    own = {main[0]: amplitude[: main[0][1]]}
-    later = after(amplitude, own[main[0]])
-    shift = after(row, own[main[0]]) * ko
-    for c in main[1:] + [extra]:
+    first, second = main
+    half = (first[1] - first[0]) // 2
+    third = (second[1] - second[0]) // 3
+    heads = bounds(first[0], first[1] - first[0] - half, half)
+    tails = bounds(second[0], second[1] - second[0] - third, third)
+
+    own = {first: amplitude[: first[1]]}
+    later = after(amplitude, own[first])
+    shift = after(row, own[first]) * ko
+    for c in [second, extra]:
         own[c] = later[c[0] : c[1]]
     same, far_inner, far_end, out_inner, out_end, lent_weights = {}, {}, {}, {}, {}, {}
+    tables = {
+        "own": own,
+        "same": same,
+        "far_inner": far_inner,
+        "far_end": far_end,
+        "out_inner": out_inner,
+        "out_end": out_end,
+        "lent": lent_weights,
+    }
+
+    def cover(table, c):
+        return next(k for k in table if k[0] <= c[0] and c[1] <= k[1])
 
     def find(table, c):
-        for (k0, k1), value in table.items():
-            if k0 <= c[0] and c[1] <= k1:
-                return value if (k0, k1) == c else value[c[0] - k0 : c[1] - k0]
-        return None
-
-    done = {"out": [], "across": [], "in": []}
-
-    def send(name, into, c, source, move):
+        k = cover(table, c)
+        return table[k] if k == c else table[k][c[0] - k[0] : c[1] - k[0]]
+
+    queues = {"out": [], "across": [], "in": []}
+    queues["out"] += [("out_inner", c, "far_inner", outward) for c in main]
+    queues["out"] += [("out_end", c, "far_end", outward) for c in heads + tails]
+    queues["across"] += [("far_inner", c, "own", across) for c in main]
+    queues["across"] += [("far_end", first, "same", across), ("far_inner", extra, "own", across)]
+    queues["across"] += [("far_end", c, "same", across) for c in [extra] + tails]
+    queues["in"] += [("same", extra, "own", inward)]
+    queues["in"] += [("lent", c, None, inward) for c in pieces]
+
+    arrival = {("own", c): 0 for c in own}
+    plan, free, begins = [], dict.fromkeys(queues, 0), {name: [] for name in queues}
+    for c in main:
+        begin = free["out"]
+        arrival["same", c] = free["out"] = free["in"] = begin + c[1] - c[0]
+        begins["out"].append(begin)
+        begins["in"].append(begin)
+        plan.append((("out", "in"), "same", c, "own", swap, begin, free["out"]))
+    while any(queues.values()):
+        options = []
+        for name, queue in queues.items():
+            if queue:
+                into, c, source, move = queue[0]
+                ends = [t for (kind, k), t in arrival.items() if kind == source and k[0] <= c[0] and c[1] <= k[1]]
+                if source is None or ends:
+                    options.append((max([free[name]] + ends[:1]), name))
+        begin, name = min(options)
+        into, c, source, move = queues[name].pop(0)
+        units = (c[1] - c[0]) * (width // block if source is None else 1)
+        free[name] = arrival[into, c] = begin + units
+        plan.append(((name,), into, c, source, move, begin, free[name]))
+
+    work = []
+
+    def step(name, c, *needs):
+        ready = max(t for need in needs for (kind, k), t in arrival.items() if kind == need and k[0] <= c[0] and c[1] <= k[1])
+        work.append((ready, len(work), name, c))
+
+    for c in main:
+        step("near", c, "same", "far_inner", "out_inner")
+    step("near", extra, "same", "far_inner")
+    for c in heads + tails:
+        step("far", c, "far_end", "out_end")
+    step("far", extra, "far_end")
+    for c in pieces:
+        step("loan", c, "far_end", "lent")
+    work.sort()
+
+    totals = dict.fromkeys(("near", "far", "loan"))
+
+    def run(name, c):
+        if name == "near":
+            slots = [[own[c]], [same[c]], [far_inner[c]] + ([out_inner[c]] if c in out_inner else [])]
+        elif name == "far":
+            slots = [[find(far_end, c)] + ([out_end[c]] if c in out_end else [])]
+        else:
+            slots = [[find(held, c)] for held in (own, far_inner, far_end)]
+        weights, offset = (lent_weights[c], jnp.int32(0)) if name == "loan" else (integral, row * ko + c[0])
+        totals[name] = contract(slots, weights, offset, totals[name])
+
+    sent = {name: [] for name in queues}
+    recent = {name: None for name in totals}
+    margin = 2 * (ko // 50 or 1)
+    for names, into, c, source, move, begin, end in plan:
+        issue = max((sent[n][-1][0] for n in names if sent[n]), default=0)
+        while work and work[0][0] + margin <= issue:
+            _, _, name, k = work.pop(0)
+            run(name, k)
+            recent[name] = totals[name]
         if source is None:
             value = lax.dynamic_slice_in_dim(integral, shift + c[0], c[1] - c[0], axis=0)
         else:
-            value = find(source, c)
-        if len(done[name]) >= 2:
-            value = after(value, done[name][-2])
-        into[c] = move(value)
-        done[name].append(into[c])
-
-    for c in main:
-        send("out", same, c, own, swap)
-        done["in"].append(same[c])
-    for c in main + [extra]:
-        send("across", far_inner, c, own, across)
-    for c in main:
-        send("out", out_inner, c, far_inner, outward)
-    send("in", same, extra, own, inward)
-    for c in main + [extra]:
-        send("across", far_end, c, same, across)
-    for c in ends:
-        send("out", out_end, c, far_end, outward)
-    for c in pieces:
-        send("in", lent_weights, c, None, inward)
-
-    near, far, loan = None, None, None
-    for c in main:
-        slots = [[own[c]], [same[c]], [far_inner[c], out_inner[c]]]
-        near = contract(slots, integral, row * ko + c[0], near)
-    near = contract([[own[extra]], [same[extra]], [far_inner[extra]]], integral, row * ko + base, near)
-    for c in ends[:2] + [extra] + ends[2:]:
-        slots = [[find(far_end, c)] + ([out_end[c]] if c in out_end else [])]
-        far = contract(slots, integral, row * ko + c[0], far)
-    for c in pieces:
-        slots = [[find(held, c)] for held in (own, far_inner, far_end)]
-        loan = contract(slots, lent_weights[c], jnp.int32(0), loan)
+            value = find(tables[source], c)
+        earlier = [entry[2] for n in queues for entry in [e for e in sent[n] if e[1] <= issue][-1:]]
+        earlier += [v for v in recent.values() if v is not None]
+        if earlier:
+            value = after(value, *earlier)
+        tables[into][c] = move(value)
+        for n in names:
+            sent[n].append((begin, end, tables[into][c]))
+    for _, _, name, k in work:
+        run(name, k)
+    near, far, loan = (totals[name] for name in ("near", "far", "loan"))
 
     def layer_sum(blocks):
         halves = blocks.reshape(blocks.shape[0], layers, block // layers, width)

time: 231 us -> 206 us (0.89)
  waiting for transfers between devices: 108 us -> 65.8 us
  starting transfers between devices: 50.9 us -> 68.5 us
  local copies, waits for them, and re-layouts: 22.2 us -> 24.6 us
    ppermute x21 -> x22, waiting for transfers between devices: 106 us -> 60.2 us  [hop(): return lambda value: lax.ppermute(value, 'col', lanes)]
    ppermute x21 -> x22, starting transfers between devices: 43.3 us -> 59.7 us  [hop(): return lambda value: lax.ppermute(value, 'col', lanes)]
    ppermute x6, waiting for transfers between devices: 2.11 us -> 5.61 us  [row_sum(): lax.ppermute(part(row ^ t), 'row', [(r, r ^ t) for r in range(4)])]
    pallas_call x19 -> x17, Pallas kernels: 42.2 us -> 42.8 us  [contract_run(): pl.pallas_call(functools.partial(contract_kernel, terms, per, total is No...]
  transfers between devices with their start and end apart: 30 -> 31, of which waited for: 8 -> 12; matrix products, arithmetic and copies ran while one was open for 9% -> 11% of each run, Pallas kernels for 18% -> 21%
where the time goes in v7:
time: 206 us; the launch traced here: 205 us
  starting transfers between devices  68.5 us (33%)
  waiting for transfers between devices  65.8 us (32%)
  Pallas kernels  42.8 us (21%)
  local copies, waits for them, and re-layouts  24.6 us (12%)
  other arithmetic  2.76 us (1%)
    ppermute x22, waiting for transfers between devices, hop(): return lambda value: lax.ppermute(value, 'col', lanes)  60.2 us
    ppermute x22, starting transfers between devices, hop(): return lambda value: lax.ppermute(value, 'col', lanes)  59.7 us
    pallas_call x17, Pallas kernels, contract_run(): pl.pallas_call(functools.partial(contract_kernel, terms, per, total is No...  42.8 us
    slice x9, local copies, waits for them, and re-layouts, find(): return table[k] if k == c else table[k][c[0] - k[0]:c[1] - k[0]]  9.51 us
    ppermute x6, starting transfers between devices, row_sum(): lax.ppermute(part(row ^ t), 'row', [(r, r ^ t) for r in range(4)])  8.25 us
    ppermute x6, waiting for transfers between devices, row_sum(): lax.ppermute(part(row ^ t), 'row', [(r, r ^ t) for r in range(4)])  5.61 us
    dynamic_slice x2, local copies, waits for them, and re-layouts, shards(): lax.dynamic_slice_in_dim(integral, shift + c[0], c[1] - c[0], axis=0)  5.31 us
  transfers between devices with their start and end apart: 31, of which 12 were waited for; matrix products, arithmetic and copies ran while one was open for 11% of the time, Pallas kernels for 21%

profile of v7, /device:TPU:0, one launch (start us, length us, event | category | flops | bytes accessed | tf_op | source)
XLA Modules:
  0.0 205.0 jit_solution(17494898495422686684)
XLA Ops:
  1.4 3.1 %collective-permute-start.3 = (f32[18,128,128]{2,1,0:T(8,128)S(1)}, f32[18,128,128]{2,1,0:T(8,128)}, u32[]{:S(2)}, u32[]{:S(2)}) collective-permute-start(f32[18,128,128]{2,1,0:T(8,128)S(1)} %bitcast.61), channel_id=1, source_target_pairs={{0,2},{2,0},{4,6},{6,4},{1,3},{3,1},{5,7},{7,5},{8,10},{10,8},{12,... | collective-permute-start | bytes 3538952 | tf_op jit(solution)/shard_map/ppermute | solution.py:113
  7.5 3.5 %collective-permute-start = (f32[19,128,128]{2,1,0:T(8,128)S(1)}, f32[19,128,128]{2,1,0:T(8,128)S(1)}, u32[]{:S(2)}, u32[]{:S(2)}) collective-permute-start(f32[19,128,128]{2,1,0:T(8,128)S(1)} %slice.78.refs_0_), channel_id=1, source_target_pairs={{0,2},{2,0},{4,6},{6,4},{1,3},{3,1},{5,7},{7,5},{8,10},{10,8},{12,... | collective-permute-start | bytes 3735560 | tf_op jit(solution)/shard_map/ppermute | solution.py:113
  13.8 17.6 %collective-permute-done.3.refs_1_ = f32[18,128,128]{2,1,0:T(8,128)} collective-permute-done((f32[18,128,128]{2,1,0:T(8,128)S(1)}, f32[18,128,128]{2,1,0:T(8,128)}, u32[]{:S(2)}, u32[]{:S(2)}) %collective-permute-start.3) | collective-permute-done | bytes 1179680 | tf_op jit(solution)/shard_map/ppermute | solution.py:113
  32.6 2.1 %slice.79.refs_0_ = f32[13,128,128]{2,1,0:T(8,128)} slice(f32[50,128,128]{2,1,0:T(8,128)} %bitcast.113), slice={[37:50], [0:128], [0:128]} | slice | bytes 1703936 | tf_op jit(solution)/shard_map/slice | solution.py:133
  34.8 8.9 %collective-permute-start.5 = (f32[13,128,128]{2,1,0:T(8,128)}, f32[13,128,128]{2,1,0:T(8,128)}, u32[]{:S(2)}, u32[]{:S(2)}) collective-permute-start(f32[13,128,128]{2,1,0:T(8,128)} %slice.79.refs_0_), channel_id=1, source_target_pairs={{0,2},{6,4},{1,3},{7,5},{8,10},{14,12},{9,11},{15,13},{16,18},{22,... | collective-permute-start | bytes 2555912 | tf_op jit(solution)/shard_map/ppermute | solution.py:113
  45.4 12.5 %collective-permute-done.refs_1_ = f32[19,128,128]{2,1,0:T(8,128)S(1)} collective-permute-done((f32[19,128,128]{2,1,0:T(8,128)S(1)}, f32[19,128,128]{2,1,0:T(8,128)S(1)}, u32[]{:S(2)}, u32[]{:S(2)}) %collective-permute-start) | collective-permute-done | bytes 1245216 | tf_op jit(solution)/shard_map/ppermute | solution.py:113
  60.0 3.1 %constant_dynamic-slice_fusion.4 = (f32[3,128,512]{2,1,0:T(8,128)}, f32[3,128,512]{2,1,0:T(8,128)}, f32[3,128,512]{2,1,0:T(8,128)}) fusion(f32[200,128,512]{2,1,0:T(8,128)} %bitcast.64, s32[]{:T(128)S(6)} %select_n.73, s32[]{:T(128)S(6)} %select_n.76, s32[]{:T(128)S(6)} %select_n.74), kind=kLoop, calls=%fused_computation.41 | loop fusion | bytes 4718604 | tf_op jit(solution)/shard_map/dynamic_slice | solution.py:221
  63.0 11.7 %collective-permute-done.5.refs_1_ = f32[13,128,128]{2,1,0:T(8,128)} collective-permute-done((f32[13,128,128]{2,1,0:T(8,128)}, f32[13,128,128]{2,1,0:T(8,128)}, u32[]{:S(2)}, u32[]{:S(2)}) %collective-permute-start.5) | collective-permute-done | bytes 852000 | tf_op jit(solution)/shard_map/ppermute | solution.py:113
  74.7 5.3 %collective-permute-start.14 = (f32[3,128,512]{2,1,0:T(8,128)}, f32[3,128,512]{2,1,0:T(8,128)}, u32[]{:S(2)}, u32[]{:S(2)}) collective-permute-start(f32[3,128,512]{2,1,0:T(8,128)} %get-tuple-element.35), channel_id=1, source_target_pairs={{0,2},{6,4},{1,3},{7,5},{8,10},{14,12},{9,11},{15,13},{16,18},{22,... | collective-permute-start | bytes 2359304 | tf_op jit(solution)/shard_map/ppermute | solution.py:113
  80.0 3.3 %collective-permute-done.7.refs_3_ = f32[18,128,128]{2,1,0:T(8,128)} collective-permute-done((f32[18,128,128]{2,1,0:T(8,128)}, f32[18,128,128]{2,1,0:T(8,128)}, u32[]{:S(2)}, u32[]{:S(2)}) %collective-permute-start.7) | collective-permute-done | bytes 1179680 | tf_op jit(solution)/shard_map/ppermute | solution.py:113
  83.3 2.3 %collective-permute-start.11 = (f32[3,128,512]{2,1,0:T(8,128)}, f32[3,128,512]{2,1,0:T(8,128)}, u32[]{:S(2)}, u32[]{:S(2)}) collective-permute-start(f32[3,128,512]{2,1,0:T(8,128)} %get-tuple-element.32), channel_id=1, source_target_pairs={{0,2},{6,4},{1,3},{7,5},{8,10},{14,12},{9,11},{15,13},{16,18},{22,... | collective-permute-start | bytes 2359304 | tf_op jit(solution)/shard_map/ppermute | solution.py:113
  89.5 5.8 %shard_map.28.refs_9_ = f32[3,128,512]{2,1,0:T(8,128)S(1)} custom-call(s32[1]{0:T(128)} %bitcast.7.offset_ref, f32[18,128,128]{2,1,0:T(8,128)S(1)} %bitcast.63, f32[18,128,128]{2,1,0:T(8,128)} %collective-permute-done.3.refs_1_, f32[18,128,128]{2,1,0:T(8,128)} %collective-permute-done.4.refs_2_, f32[18,128,128]{2,1,0:T(8,128)} %collective-permute-done.7.refs_3_, ...), custom_call_target="tpu_custom_call" | custom-call | tf_op jit(solution)/shard_map/pallas_call | solution.py:76
  95.3 2.5 %fusion.21 = (f32[9,128,128]{2,1,0:T(8,128)}, f32[9,128,128]{2,1,0:T(8,128)}) fusion(f32[18,128,128]{2,1,0:T(8,128)} %collective-permute-done.9), kind=kLoop, calls=%fused_computation.44 | loop fusion | bytes 2359296 | tf_op jit(solution)/shard_map/slice | solution.py:150
  99.1 10.2 %collective-permute-start.18 = (f32[3,128,512]{2,1,0:T(8,128)}, f32[3,128,512]{2,1,0:T(8,128)}, u32[]{:S(2)}, u32[]{:S(2)}) collective-permute-start(f32[3,128,512]{2,1,0:T(8,128)} %get-tuple-element.39), channel_id=1, source_target_pairs={{0,2},{6,4},{1,3},{7,5},{8,10},{14,12},{9,11},{15,13},{16,18},{22,... | collective-permute-start | bytes 2359304 | tf_op jit(solution)/shard_map/ppermute | solution.py:113
  109.3 2.3 %constant_dynamic-slice_fusion.2 = (f32[2,128,512]{2,1,0:T(8,128)}, f32[2,128,512]{2,1,0:T(8,128)}) fusion(f32[200,128,512]{2,1,0:T(8,128)} %bitcast.71, s32[]{:T(128)S(6)} %select_n.75, s32[]{:T(128)S(6)} %select_n.85), kind=kLoop, calls=%fused_computation.39 | loop fusion | bytes 2097160 | tf_op jit(solution)/shard_map/dynamic_slice | solution.py:221
  116.0 4.1 %shard_map.29.refs_4_ = f32[3,128,512]{2,1,0:T(8,128)S(1)} custom-call(s32[1]{0:T(128)} %bitcast.6.offset_ref, f32[13,128,128]{2,1,0:T(8,128)} %slice.79.refs_0_, f32[13,128,128]{2,1,0:T(8,128)} %collective-permute-done.5.refs_1_, f32[13,128,128]{2,1,0:T(8,128)S(1)} %collective-permute-done.6.refs_2_, ...), custom_call_target="tpu_custom_call", output_to_operand_aliasing={{}: (10, {})} | custom-call | tf_op jit(solution)/shard_map/pallas_call | solution.py:76
  123.0 5.7 %shard_map.31.refs_5_ = f32[3,128,512]{2,1,0:T(8,128)S(1)} custom-call(s32[1]{0:T(128)} %bitcast.offset_ref, f32[19,128,128]{2,1,0:T(8,128)S(1)} %copy-done.3, f32[19,128,128]{2,1,0:T(8,128)S(1)} %collective-permute-done.refs_1_, f32[19,128,128]{2,1,0:T(8,128)} %collective-permute-done.1.refs_2_, ...), custom_call_target="tpu_custom_call", output_to_operand_aliasing={{}: (11, {})} | custom-call | tf_op jit(solution)/shard_map/pallas_call | solution.py:76
  130.1 6.2 %collective-permute-start.16 = (f32[2,128,512]{2,1,0:T(8,128)}, f32[2,128,512]{2,1,0:T(8,128)}, u32[]{:S(2)}, u32[]{:S(2)}) collective-permute-start(f32[2,128,512]{2,1,0:T(8,128)} %get-tuple-element.37), channel_id=1, source_target_pairs={{0,2},{6,4},{1,3},{7,5},{8,10},{14,12},{9,11},{15,13},{16,18},{22,... | collective-permute-start | bytes 1572872 | tf_op jit(solution)/shard_map/ppermute | solution.py:113
  136.3 2.7 %shard_map.33.refs_2_ = f32[1,128,512]{2,1,0:T(8,128)S(1)} custom-call(s32[1]{0:T(128)} %bitcast.6.offset_ref, f32[13,128,128]{2,1,0:T(8,128)} %collective-permute-done.10.refs_0_, f32[200,128,512]{2,1,0:T(8,128)} %bitcast.87, f32[200,128,512]{2,1,0:T(8,128)} %bitcast.86, f32[200,128,512]{2,1,0:T(8,128)} %bitcast.88, f32[200,128,512]{2,1,0:T(8,128)} %bitcast.89, ...), custom_call_target="tpu_custom_call" | custom-call | tf_op jit(solution)/shard_map/pallas_call | solution.py:76
  140.3 3.5 %shard_map.35.refs_5_ = f32[1,128,512]{2,1,0:T(8,128)S(1)} custom-call(s32[1]{0:T(128)} %bitcast.7.offset_ref, f32[9,128,128]{2,1,0:T(8,128)} %get-tuple-element.38.refs_0_, f32[9,128,128]{2,1,0:T(8,128)} %collective-permute-done.17.refs_1_, f32[200,128,512]{2,1,0:T(8,128)} %bitcast.93, f32[200,128,512]{2,1,0:T(8,128)} %bitcast.94, ...), custom_call_target="tpu_custom_call", output_to_operand_aliasing={{}: (6, {})} | custom-call | tf_op jit(solution)/shard_map/pallas_call | solution.py:76
  144.9 1.8 shard_map.37.refs_6_
  146.7 1.9 shard_map.38.refs_6_
  153.8 1.8 shard_map.39.refs_5_
  156.6 3.5 %shard_map.36.refs_8_ = f32[1,128,512]{2,1,0:T(8,128)S(1)} custom-call(s32[1]{0:T(128)} %bitcast.12.offset_ref, f32[9,128,128]{2,1,0:T(8,128)} %get-tuple-element.34.refs_0_, f32[9,128,128]{2,1,0:T(8,128)} %collective-permute-done.13.refs_1_, f32[200,128,512]{2,1,0:T(8,128)} %bitcast.96, f32[200,128,512]{2,1,0:T(8,128)} %bitcast.97, ...), custom_call_target="tpu_custom_call", output_to_operand_aliasing={{}: (6, {})} | custom-call | tf_op jit(solution)/shard_map/pallas_call | solution.py:76
  166.7 8.6 %collective-permute-done.20.refs_1_ = f32[13,128,128]{2,1,0:T(8,128)S(1)} collective-permute-done((f32[13,128,128]{2,1,0:T(8,128)}, f32[13,128,128]{2,1,0:T(8,128)S(1)}, u32[]{:S(2)}, u32[]{:S(2)}) %collective-permute-start.20) | collective-permute-done | bytes 852000 | tf_op jit(solution)/shard_map/ppermute | solution.py:113
  175.3 2.7 %shard_map.40.refs_3_ = f32[1,128,512]{2,1,0:T(8,128)S(1)} custom-call(s32[1]{0:T(128)} %bitcast.offset_ref, f32[13,128,128]{2,1,0:T(8,128)} %collective-permute-done.15.refs_0_, f32[13,128,128]{2,1,0:T(8,128)S(1)} %collective-permute-done.20.refs_1_, f32[200,128,512]{2,1,0:T(8,128)} %bitcast.99, ...), custom_call_target="tpu_custom_call", output_to_operand_aliasing={{}: (9, {})} | custom-call | tf_op jit(solution)/shard_map/pallas_call | solution.py:76
  179.3 4.1 %collective-permute-done.19.refs_1_ = f32[6,128,128]{2,1,0:T(8,128)S(1)} collective-permute-done((f32[6,128,128]{2,1,0:T(8,128)S(1)}, f32[6,128,128]{2,1,0:T(8,128)S(1)}, u32[]{:S(2)}, u32[]{:S(2)}) %collective-permute-start.19) | collective-permute-done | bytes 393248 | tf_op jit(solution)/shard_map/ppermute | solution.py:113
  183.4 1.9 shard_map.42
  186.6 2.5 %collective-permute-start.29 = (f32[64,512]{1,0:T(8,128)S(1)}, f32[64,512]{1,0:T(8,128)S(1)}, u32[]{:S(2)}, u32[]{:S(2)}) collective-permute-start(f32[64,512]{1,0:T(8,128)S(1)} %get-tuple-element.70), channel_id=1, source_target_pairs={{0,24},{8,16},{16,8},{24,0},{1,25},{9,17},{17,9},{25,1},{2,26},{10... | collective-permute-start | bytes 393224 | tf_op jit(solution)/shard_map/ppermute | solution.py:253
  190.3 2.5 %collective-permute-start.24 = (f32[64,512]{1,0:T(8,128)S(1)}, f32[64,512]{1,0:T(8,128)S(1)}, u32[]{:S(2)}, u32[]{:S(2)}) collective-permute-start(f32[64,512]{1,0:T(8,128)S(1)} %get-tuple-element.67), channel_id=1, source_target_pairs={{0,24},{8,16},{16,8},{24,0},{1,25},{9,17},{17,9},{25,1},{2,26},{10... | collective-permute-start | bytes 393224 | tf_op jit(solution)/shard_map/ppermute | solution.py:253
  199.8 2.0 collective-permute-done.23
  202.0 2.3 %collective-permute-done.30 = f32[64,512]{1,0:T(8,128)S(1)} collective-permute-done((f32[64,512]{1,0:T(8,128)S(1)}, f32[64,512]{1,0:T(8,128)S(1)}, u32[]{:S(2)}, u32[]{:S(2)}) %collective-permute-start.30) | collective-permute-done | bytes 131104 | tf_op jit(solution)/shard_map/ppermute | solution.py:113
  (91 shorter events, 52.5 us)
Async XLA Ops:
  1.4 30.0 %collective-permute-start.3 = (f32[18,128,128]{2,1,0:T(8,128)S(1)}, f32[18,128,128]{2,1,0:T(8,128)}, u32[]{:S(2)}, u32[]{:S(2)}) collective-permute-start(f32[18,128,128]{2,1,0:T(8,128)S(1)} %bitcast.61), channel_id=1, source_target_pairs={{0,2},{2,0},{4,6},{6,4},{1,3},{3,1},{5,7},{7,5},{8,10},{10,8},{12,... | collective-permute-start | bytes 3538952 | tf_op jit(solution)/shard_map/ppermute | solution.py:113
  4.4 26.9 %collective-permute-start.4 = (f32[18,128,128]{2,1,0:T(8,128)S(1)}, f32[18,128,128]{2,1,0:T(8,128)}, u32[]{:S(2)}, u32[]{:S(2)}) collective-permute-start(f32[18,128,128]{2,1,0:T(8,128)S(1)} %bitcast.62), channel_id=1, source_target_pairs={{2,4},{4,2},{3,5},{5,3},{10,12},{12,10},{11,13},{13,11},{18,20},{2... | collective-permute-start | bytes 3538952 | tf_op jit(solution)/shard_map/ppermute | solution.py:113
  7.5 50.4 %collective-permute-start = (f32[19,128,128]{2,1,0:T(8,128)S(1)}, f32[19,128,128]{2,1,0:T(8,128)S(1)}, u32[]{:S(2)}, u32[]{:S(2)}) collective-permute-start(f32[19,128,128]{2,1,0:T(8,128)S(1)} %slice.78.refs_0_), channel_id=1, source_target_pairs={{0,2},{2,0},{4,6},{6,4},{1,3},{3,1},{5,7},{7,5},{8,10},{10,8},{12,... | collective-permute-start | bytes 3735560 | tf_op jit(solution)/shard_map/ppermute | solution.py:113
  11.0 47.0 %collective-permute-start.1 = (f32[19,128,128]{2,1,0:T(8,128)S(1)}, f32[19,128,128]{2,1,0:T(8,128)}, u32[]{:S(2)}, u32[]{:S(2)}) collective-permute-start(f32[19,128,128]{2,1,0:T(8,128)S(1)} %slice.78.refs_0_), channel_id=1, source_target_pairs={{2,4},{4,2},{3,5},{5,3},{10,12},{12,10},{11,13},{13,11},{18,20},{2... | collective-permute-start | bytes 3735560 | tf_op jit(solution)/shard_map/ppermute | solution.py:113
  31.4 52.0 %collective-permute-start.7 = (f32[18,128,128]{2,1,0:T(8,128)}, f32[18,128,128]{2,1,0:T(8,128)}, u32[]{:S(2)}, u32[]{:S(2)}) collective-permute-start(f32[18,128,128]{2,1,0:T(8,128)} %collective-permute-done.4.refs_2_), channel_id=1, source_target_pairs={{2,0},{4,6},{3,1},{5,7},{10,8},{12,14},{11,9},{13,15},{18,16},{20,... | collective-permute-start | bytes 3538952 | tf_op jit(solution)/shard_map/ppermute | solution.py:113
  34.8 39.9 %collective-permute-start.5 = (f32[13,128,128]{2,1,0:T(8,128)}, f32[13,128,128]{2,1,0:T(8,128)}, u32[]{:S(2)}, u32[]{:S(2)}) collective-permute-start(f32[13,128,128]{2,1,0:T(8,128)} %slice.79.refs_0_), channel_id=1, source_target_pairs={{0,2},{6,4},{1,3},{7,5},{8,10},{14,12},{9,11},{15,13},{16,18},{22,... | collective-permute-start | bytes 2555912 | tf_op jit(solution)/shard_map/ppermute | solution.py:113
  43.7 42.9 %collective-permute-start.9 = (f32[18,128,128]{2,1,0:T(8,128)}, f32[18,128,128]{2,1,0:T(8,128)}, u32[]{:S(2)}, u32[]{:S(2)}) collective-permute-start(f32[18,128,128]{2,1,0:T(8,128)} %collective-permute-done.3.refs_1_), channel_id=1, source_target_pairs={{2,4},{4,2},{3,5},{5,3},{10,12},{12,10},{11,13},{13,11},{18,20},{2... | collective-permute-start | bytes 3538952 | tf_op jit(solution)/shard_map/ppermute | solution.py:113
  57.9 54.6 %collective-permute-start.2 = (f32[19,128,128]{2,1,0:T(8,128)}, f32[19,128,128]{2,1,0:T(8,128)}, u32[]{:S(2)}, u32[]{:S(2)}) collective-permute-start(f32[19,128,128]{2,1,0:T(8,128)} %collective-permute-done.1.refs_2_), channel_id=1, source_target_pairs={{2,0},{4,6},{3,1},{5,7},{10,8},{12,14},{11,9},{13,15},{18,16},{20,... | collective-permute-start | bytes 3735560 | tf_op jit(solution)/shard_map/ppermute | solution.py:113
  59.2 39.8 %collective-permute-start.6 = (f32[13,128,128]{2,1,0:T(8,128)}, f32[13,128,128]{2,1,0:T(8,128)S(1)}, u32[]{:S(2)}, u32[]{:S(2)}) collective-permute-start(f32[13,128,128]{2,1,0:T(8,128)} %slice.79.refs_0_), channel_id=1, source_target_pairs={{2,4},{4,2},{3,5},{5,3},{10,12},{12,10},{11,13},{13,11},{18,20},{2... | collective-permute-start | bytes 2555912 | tf_op jit(solution)/shard_map/ppermute | solution.py:113
  74.7 23.0 %collective-permute-start.14 = (f32[3,128,512]{2,1,0:T(8,128)}, f32[3,128,512]{2,1,0:T(8,128)}, u32[]{:S(2)}, u32[]{:S(2)}) collective-permute-start(f32[3,128,512]{2,1,0:T(8,128)} %get-tuple-element.35), channel_id=1, source_target_pairs={{0,2},{6,4},{1,3},{7,5},{8,10},{14,12},{9,11},{15,13},{16,18},{22,... | collective-permute-start | bytes 2359304 | tf_op jit(solution)/shard_map/ppermute | solution.py:113
  83.3 38.3 %collective-permute-start.11 = (f32[3,128,512]{2,1,0:T(8,128)}, f32[3,128,512]{2,1,0:T(8,128)}, u32[]{:S(2)}, u32[]{:S(2)}) collective-permute-start(f32[3,128,512]{2,1,0:T(8,128)} %get-tuple-element.32), channel_id=1, source_target_pairs={{0,2},{6,4},{1,3},{7,5},{8,10},{14,12},{9,11},{15,13},{16,18},{22,... | collective-permute-start | bytes 2359304 | tf_op jit(solution)/shard_map/ppermute | solution.py:113
  86.7 43.5 %collective-permute-start.10 = (f32[13,128,128]{2,1,0:T(8,128)}, f32[13,128,128]{2,1,0:T(8,128)}, u32[]{:S(2)}, u32[]{:S(2)}) collective-permute-start(f32[13,128,128]{2,1,0:T(8,128)} %collective-permute-done.5.refs_1_), channel_id=1, source_target_pairs={{2,4},{4,2},{3,5},{5,3},{10,12},{12,10},{11,13},{13,11},{18,20},{2... | collective-permute-start | bytes 2555912 | tf_op jit(solution)/shard_map/ppermute | solution.py:113
  97.8 42.5 %collective-permute-start.17 = (f32[9,128,128]{2,1,0:T(8,128)}, f32[9,128,128]{2,1,0:T(8,128)}, u32[]{:S(2)}, u32[]{:S(2)}) collective-permute-start(f32[9,128,128]{2,1,0:T(8,128)} %get-tuple-element.38.refs_0_), channel_id=1, source_target_pairs={{2,0},{4,6},{3,1},{5,7},{10,8},{12,14},{11,9},{13,15},{18,16},{20,... | collective-permute-start | bytes 1769480 | tf_op jit(solution)/shard_map/ppermute | solution.py:113
  99.1 23.9 %copy-start.4 = (f32[13,128,128]{2,1,0:T(8,128)}, f32[13,128,128]{2,1,0:T(8,128)S(1)}, u32[]{:S(2)}) copy-start(f32[13,128,128]{2,1,0:T(8,128)S(1)} %collective-permute-done.6.refs_2_) | copy-start | bytes 2555908
  99.1 49.6 %collective-permute-start.18 = (f32[3,128,512]{2,1,0:T(8,128)}, f32[3,128,512]{2,1,0:T(8,128)}, u32[]{:S(2)}, u32[]{:S(2)}) collective-permute-start(f32[3,128,512]{2,1,0:T(8,128)} %get-tuple-element.39), channel_id=1, source_target_pairs={{0,2},{6,4},{1,3},{7,5},{8,10},{14,12},{9,11},{15,13},{16,18},{22,... | collective-permute-start | bytes 2359304 | tf_op jit(solution)/shard_map/ppermute | solution.py:113
  112.5 38.3 %collective-permute-start.15 = (f32[13,128,128]{2,1,0:T(8,128)}, f32[13,128,128]{2,1,0:T(8,128)}, u32[]{:S(2)}, u32[]{:S(2)}) collective-permute-start(f32[13,128,128]{2,1,0:T(8,128)} %slice.101), channel_id=1, source_target_pairs={{2,4},{4,2},{3,5},{5,3},{10,12},{12,10},{11,13},{13,11},{18,20},{2... | collective-permute-start | bytes 2555912 | tf_op jit(solution)/shard_map/ppermute | solution.py:113
  121.6 29.9 %collective-permute-start.13 = (f32[9,128,128]{2,1,0:T(8,128)}, f32[9,128,128]{2,1,0:T(8,128)}, u32[]{:S(2)}, u32[]{:S(2)}) collective-permute-start(f32[9,128,128]{2,1,0:T(8,128)} %get-tuple-element.34.refs_0_), channel_id=1, source_target_pairs={{2,0},{4,6},{3,1},{5,7},{10,8},{12,14},{11,9},{13,15},{18,16},{20,... | collective-permute-start | bytes 1769480 | tf_op jit(solution)/shard_map/ppermute | solution.py:113
  130.1 30.0 %collective-permute-start.16 = (f32[2,128,512]{2,1,0:T(8,128)}, f32[2,128,512]{2,1,0:T(8,128)}, u32[]{:S(2)}, u32[]{:S(2)}) collective-permute-start(f32[2,128,512]{2,1,0:T(8,128)} %get-tuple-element.37), channel_id=1, source_target_pairs={{0,2},{6,4},{1,3},{7,5},{8,10},{14,12},{9,11},{15,13},{16,18},{22,... | collective-permute-start | bytes 1572872 | tf_op jit(solution)/shard_map/ppermute | solution.py:113
  148.7 14.5 %collective-permute-start.25 = (f32[2,128,512]{2,1,0:T(8,128)S(1)}, f32[2,128,512]{2,1,0:T(8,128)S(1)}, u32[]{:S(2)}, u32[]{:S(2)}) collective-permute-start(f32[2,128,512]{2,1,0:T(8,128)S(1)} %copy-done.8), channel_id=1, source_target_pairs={{0,2},{6,4},{1,3},{7,5},{8,10},{14,12},{9,11},{15,13},{16,18},{22,... | collective-permute-start | bytes 1572872 | tf_op jit(solution)/shard_map/ppermute | solution.py:113
  150.8 15.1 %collective-permute-start.8 = (f32[3,64,512]{2,1,0:T(8,128)}, f32[3,64,512]{2,1,0:T(8,128)S(1)}, u32[]{:S(2)}, u32[]{:S(2)}) collective-permute-start(f32[3,64,512]{2,1,0:T(8,128)} %dynamic-slice_bitcast_fusion.1), channel_id=1, source_target_pairs={{0,1},{1,0},{2,3},{3,2},{4,5},{5,4},{6,7},{7,6},{8,9},{9,8},{10,11... | collective-permute-start | bytes 1179656 | tf_op jit(solution)/shard_map/ppermute | solution.py:241
  150.8 9.3 %collective-permute-start.12 = (f32[6,128,128]{2,1,0:T(8,128)S(1)}, f32[6,128,128]{2,1,0:T(8,128)S(1)}, u32[]{:S(2)}, u32[]{:S(2)}) collective-permute-start(f32[6,128,128]{2,1,0:T(8,128)S(1)} %copy-done.9), channel_id=1, source_target_pairs={{2,4},{4,2},{3,5},{5,3},{10,12},{12,10},{11,13},{13,11},{18,20},{2... | collective-permute-start | bytes 1179656 | tf_op jit(solution)/shard_map/ppermute | solution.py:113
  151.5 23.8 %collective-permute-start.20 = (f32[13,128,128]{2,1,0:T(8,128)}, f32[13,128,128]{2,1,0:T(8,128)S(1)}, u32[]{:S(2)}, u32[]{:S(2)}) collective-permute-start(f32[13,128,128]{2,1,0:T(8,128)} %collective-permute-done.15.refs_0_), channel_id=1, source_target_pairs={{2,0},{4,6},{3,1},{5,7},{10,8},{12,14},{11,9},{13,15},{18,16},{20,... | collective-permute-start | bytes 2555912 | tf_op jit(solution)/shard_map/ppermute | solution.py:113
  160.1 23.2 %collective-permute-start.19 = (f32[6,128,128]{2,1,0:T(8,128)S(1)}, f32[6,128,128]{2,1,0:T(8,128)S(1)}, u32[]{:S(2)}, u32[]{:S(2)}) collective-permute-start(f32[6,128,128]{2,1,0:T(8,128)S(1)} %collective-permute-done.12.refs_0_), channel_id=1, source_target_pairs={{2,0},{4,6},{3,1},{5,7},{10,8},{12,14},{11,9},{13,15},{18,16},{20,... | collective-permute-start | bytes 1179656 | tf_op jit(solution)/shard_map/ppermute | solution.py:113
  165.4 20.0 %collective-permute-start.26 = (f32[3,64,512]{2,1,0:T(8,128)}, f32[3,64,512]{2,1,0:T(8,128)}, u32[]{:S(2)}, u32[]{:S(2)}) collective-permute-start(f32[3,64,512]{2,1,0:T(8,128)} %dynamic-slice_bitcast_fusion), channel_id=1, source_target_pairs={{0,1},{1,0},{2,3},{3,2},{4,5},{5,4},{6,7},{7,6},{8,9},{9,8},{10,11... | collective-permute-start | bytes 1179656 | tf_op jit(solution)/shard_map/ppermute | solution.py:241
  185.4 4.8 %collective-permute-start.21 = (f32[1,64,512]{2,1,0:T(8,128)S(1)}, f32[1,64,512]{2,1,0:T(8,128)S(1)}, u32[]{:S(2)}, u32[]{:S(2)}) collective-permute-start(f32[1,64,512]{2,1,0:T(8,128)S(1)} %dynamic-slice_bitcast_fusion.2), channel_id=1, source_target_pairs={{0,1},{1,0},{2,3},{3,2},{4,5},{5,4},{6,7},{7,6},{8,9},{9,8},{10,11... | collective-permute-start | bytes 393224 | tf_op jit(solution)/shard_map/ppermute | solution.py:241
  186.6 7.1 %collective-permute-start.29 = (f32[64,512]{1,0:T(8,128)S(1)}, f32[64,512]{1,0:T(8,128)S(1)}, u32[]{:S(2)}, u32[]{:S(2)}) collective-permute-start(f32[64,512]{1,0:T(8,128)S(1)} %get-tuple-element.70), channel_id=1, source_target_pairs={{0,24},{8,16},{16,8},{24,0},{1,25},{9,17},{17,9},{25,1},{2,26},{10... | collective-permute-start | bytes 393224 | tf_op jit(solution)/shard_map/ppermute | solution.py:253
  189.1 7.9 %collective-permute-start.28 = (f32[64,512]{1,0:T(8,128)S(1)}, f32[64,512]{1,0:T(8,128)S(1)}, u32[]{:S(2)}, u32[]{:S(2)}) collective-permute-start(f32[64,512]{1,0:T(8,128)S(1)} %get-tuple-element.69), channel_id=1, source_target_pairs={{0,16},{8,24},{16,0},{24,8},{1,17},{9,25},{17,1},{25,9},{2,18},{10... | collective-permute-start | bytes 393224 | tf_op jit(solution)/shard_map/ppermute | solution.py:253
  189.6 7.4 %collective-permute-start.27 = (f32[64,512]{1,0:T(8,128)S(1)}, f32[64,512]{1,0:T(8,128)S(1)}, u32[]{:S(2)}, u32[]{:S(2)}) collective-permute-start(f32[64,512]{1,0:T(8,128)S(1)} %get-tuple-element.68), channel_id=1, source_target_pairs={{0,8},{8,0},{16,24},{24,16},{1,9},{9,1},{17,25},{25,17},{2,10},{10... | collective-permute-start | bytes 393224 | tf_op jit(solution)/shard_map/ppermute | solution.py:253
  190.3 9.5 %collective-permute-start.24 = (f32[64,512]{1,0:T(8,128)S(1)}, f32[64,512]{1,0:T(8,128)S(1)}, u32[]{:S(2)}, u32[]{:S(2)}) collective-permute-start(f32[64,512]{1,0:T(8,128)S(1)} %get-tuple-element.67), channel_id=1, source_target_pairs={{0,24},{8,16},{16,8},{24,0},{1,25},{9,17},{17,9},{25,1},{2,26},{10... | collective-permute-start | bytes 393224 | tf_op jit(solution)/shard_map/ppermute | solution.py:253
  192.8 9.0 %collective-permute-start.23 = (f32[64,512]{1,0:T(8,128)S(1)}, f32[64,512]{1,0:T(8,128)S(1)}, u32[]{:S(2)}, u32[]{:S(2)}) collective-permute-start(f32[64,512]{1,0:T(8,128)S(1)} %get-tuple-element.66), channel_id=1, source_target_pairs={{0,16},{8,24},{16,0},{24,8},{1,17},{9,25},{17,1},{25,9},{2,18},{10... | collective-permute-start | bytes 393224 | tf_op jit(solution)/shard_map/ppermute | solution.py:253
  193.7 8.3 %collective-permute-start.22 = (f32[64,512]{1,0:T(8,128)S(1)}, f32[64,512]{1,0:T(8,128)S(1)}, u32[]{:S(2)}, u32[]{:S(2)}) collective-permute-start(f32[64,512]{1,0:T(8,128)S(1)} %get-tuple-element.65), channel_id=1, source_target_pairs={{0,8},{8,0},{16,24},{24,16},{1,9},{9,1},{17,25},{25,17},{2,10},{10... | collective-permute-start | bytes 393224 | tf_op jit(solution)/shard_map/ppermute | solution.py:253
  197.1 7.2 %collective-permute-start.30 = (f32[64,512]{1,0:T(8,128)S(1)}, f32[64,512]{1,0:T(8,128)S(1)}, u32[]{:S(2)}, u32[]{:S(2)}) collective-permute-start(f32[64,512]{1,0:T(8,128)S(1)} %fusion.3), channel_id=1, source_target_pairs={{2,0},{4,6},{3,1},{5,7},{10,8},{12,14},{11,9},{13,15},{18,16},{20,... | collective-permute-start | bytes 393224 | tf_op jit(solution)/shard_map/ppermute | solution.py:113
  (9 other events, 25.2 us)

commit v8 on v7

--- a/solution.py
+++ b/solution.py
@@ -115,7 +115,7 @@
     inward, across, outward = hop([(0, 1), (3, 2)]), hop([(1, 2), (2, 1)]), hop([(1, 0), (2, 3)])
     swap = hop([(0, 1), (1, 0), (2, 3), (3, 2)])
 
-    lent = round(ko * 2 * block / (3 * block + width)) - 1
+    lent = round(ko * 2 * block / (3 * block + width))
     base = ko - lent
     main = bounds(0, base // 2, base - base // 2)
     extra = (base, ko)
@@ -154,7 +154,7 @@
     queues["out"] += [("out_end", c, "far_end", outward) for c in heads + tails]
     queues["across"] += [("far_inner", c, "own", across) for c in main]
     queues["across"] += [("far_end", first, "same", across), ("far_inner", extra, "own", across)]
-    queues["across"] += [("far_end", c, "same", across) for c in [extra] + tails]
+    queues["across"] += [("far_end", c, "same", across) for c in [tails[0], extra, tails[1]]]
     queues["in"] += [("same", extra, "own", inward)]
     queues["in"] += [("lent", c, None, inward) for c in pieces]
 
@@ -228,10 +228,6 @@
         tables[into][c] = move(value)
         for n in names:
             sent[n].append((begin, end, tables[into][c]))
-    for _, _, name, k in work:
-        run(name, k)
-    near, far, loan = (totals[name] for name in ("near", "far", "loan"))
-
     def layer_sum(blocks):
         halves = blocks.reshape(blocks.shape[0], layers, block // layers, width)
         if layers != 2:
@@ -253,10 +249,15 @@
             total = total + lax.ppermute(part(row ^ t), "row", [(r, r ^ t) for r in range(4)])
         return total
 
-    near = layer_sum(near)
-    loan = layer_sum(loan)
+    last = ("far", tails[1])
+    for _, _, name, k in work:
+        if (name, k) != last:
+            run(name, k)
+    near = layer_sum(totals["near"])
+    loan = layer_sum(totals["loan"])
+    run(*last)
     returned = outward(row_sum(jnp.concatenate([jnp.zeros_like(loan[:1]), loan]), 0))
-    return row_sum(jnp.concatenate([near, layer_sum(far)]), inner) + returned
+    return row_sum(jnp.concatenate([near, layer_sum(totals["far"])]), inner) + returned
 
 
 def solution(mesh):

time: 206 us -> 203 us (0.985)
  waiting for transfers between devices: 65.8 us -> 53.5 us
  starting transfers between devices: 68.5 us -> 79.4 us
  Pallas kernels: 42.8 us -> 40.6 us
    ppermute x22, waiting for transfers between devices: 60.2 us -> 48.1 us  [hop(): return lambda value: lax.ppermute(value, 'col', lanes)]
    ppermute x22, starting transfers between devices: 59.7 us -> 70.1 us  [hop(): return lambda value: lax.ppermute(value, 'col', lanes)]
    pallas_call x17 -> x15, Pallas kernels: 42.8 us -> 40.6 us  [contract_run(): pl.pallas_call(functools.partial(contract_kernel, terms, per, total is No...]
  transfers between devices with their start and end apart: 31 -> 31, of which waited for: 12 -> 9; matrix products, arithmetic and copies ran while one was open for 11% -> 11% of each run, Pallas kernels for 21% -> 20%
where the time goes in v8:
time: 203 us; the launch traced here: 202 us
  starting transfers between devices  79.4 us (39%)
  waiting for transfers between devices  53.5 us (26%)
  Pallas kernels  40.6 us (20%)
  local copies, waits for them, and re-layouts  23.8 us (12%)
  other arithmetic  3.76 us (2%)
    ppermute x22, starting transfers between devices, hop(): return lambda value: lax.ppermute(value, 'col', lanes)  70.1 us
    ppermute x22, waiting for transfers between devices, hop(): return lambda value: lax.ppermute(value, 'col', lanes)  48.1 us
    pallas_call x15, Pallas kernels, contract_run(): pl.pallas_call(functools.partial(contract_kernel, terms, per, total is No...  40.6 us
    slice x9, local copies, waits for them, and re-layouts, find(): return table[k] if k == c else table[k][c[0] - k[0]:c[1] - k[0]]  11.4 us
    ppermute x6, starting transfers between devices, row_sum(): lax.ppermute(part(row ^ t), 'row', [(r, r ^ t) for r in range(4)])  8.66 us
    ppermute x6, waiting for transfers between devices, row_sum(): lax.ppermute(part(row ^ t), 'row', [(r, r ^ t) for r in range(4)])  5.39 us
    dynamic_slice x2, local copies, waits for them, and re-layouts, shards(): lax.dynamic_slice_in_dim(integral, shift + c[0], c[1] - c[0], axis=0)  4.43 us
  transfers between devices with their start and end apart: 31, of which 9 were waited for; matrix products, arithmetic and copies ran while one was open for 11% of the time, Pallas kernels for 20%

profile of v8, /device:TPU:0, one launch (start us, length us, event | category | flops | bytes accessed | tf_op | source)
XLA Modules:
  0.0 201.6 jit_solution(17223761261953667935)
XLA Ops:
  1.4 3.1 %collective-permute-start.3 = (f32[18,128,128]{2,1,0:T(8,128)S(1)}, f32[18,128,128]{2,1,0:T(8,128)}, u32[]{:S(2)}, u32[]{:S(2)}) collective-permute-start(f32[18,128,128]{2,1,0:T(8,128)S(1)} %bitcast.61), channel_id=1, source_target_pairs={{0,2},{2,0},{4,6},{6,4},{1,3},{3,1},{5,7},{7,5},{8,10},{10,8},{12,... | collective-permute-start | bytes 3538952 | tf_op jit(solution)/shard_map/ppermute | solution.py:113
  4.4 1.8 collective-permute-start.4
  7.6 3.3 %collective-permute-start = (f32[18,128,128]{2,1,0:T(8,128)S(1)}, f32[18,128,128]{2,1,0:T(8,128)}, u32[]{:S(2)}, u32[]{:S(2)}) collective-permute-start(f32[18,128,128]{2,1,0:T(8,128)S(1)} %slice.78.refs_0_), channel_id=1, source_target_pairs={{0,2},{2,0},{4,6},{6,4},{1,3},{3,1},{5,7},{7,5},{8,10},{10,8},{12,... | collective-permute-start | bytes 3538952 | tf_op jit(solution)/shard_map/ppermute | solution.py:113
  13.9 17.4 %collective-permute-done.3.refs_1_ = f32[18,128,128]{2,1,0:T(8,128)} collective-permute-done((f32[18,128,128]{2,1,0:T(8,128)S(1)}, f32[18,128,128]{2,1,0:T(8,128)}, u32[]{:S(2)}, u32[]{:S(2)}) %collective-permute-start.3) | collective-permute-done | bytes 1179680 | tf_op jit(solution)/shard_map/ppermute | solution.py:113
  31.4 7.9 %collective-permute-start.5 = (f32[14,128,128]{2,1,0:T(8,128)S(1)}, f32[14,128,128]{2,1,0:T(8,128)}, u32[]{:S(2)}, u32[]{:S(2)}) collective-permute-start(f32[14,128,128]{2,1,0:T(8,128)S(1)} %slice.79.refs_0_), channel_id=1, source_target_pairs={{0,2},{6,4},{1,3},{7,5},{8,10},{14,12},{9,11},{15,13},{16,18},{22,... | collective-permute-start | bytes 2752520 | tf_op jit(solution)/shard_map/ppermute | solution.py:113
  42.2 14.4 %collective-permute-done.refs_1_ = f32[18,128,128]{2,1,0:T(8,128)} collective-permute-done((f32[18,128,128]{2,1,0:T(8,128)S(1)}, f32[18,128,128]{2,1,0:T(8,128)}, u32[]{:S(2)}, u32[]{:S(2)}) %collective-permute-start) | collective-permute-done | bytes 1179680 | tf_op jit(solution)/shard_map/ppermute | solution.py:113
  58.7 3.4 %constant_dynamic-slice_fusion.4 = (f32[3,128,512]{2,1,0:T(8,128)}, f32[3,128,512]{2,1,0:T(8,128)}, f32[3,128,512]{2,1,0:T(8,128)}, f32[3,128,512]{2,1,0:T(8,128)S(1)}) fusion(f32[200,128,512]{2,1,0:T(8,128)} %bitcast.64, s32[]{:T(128)S(6)} %select_n.73, s32[]{:T(128)S(6)} %select_n.85, s32[]{:T(128)S(6)} %select_n.75, s32[]{:T(128)S(6)} %select_n.74), kind=kLoop, calls=%fused_computation.41 | loop fusion | bytes 6291472 | tf_op jit(solution)/shard_map/dynamic_slice | solution.py:221
  62.0 12.6 %collective-permute-done.5.refs_1_ = f32[14,128,128]{2,1,0:T(8,128)} collective-permute-done((f32[14,128,128]{2,1,0:T(8,128)S(1)}, f32[14,128,128]{2,1,0:T(8,128)}, u32[]{:S(2)}, u32[]{:S(2)}) %collective-permute-start.5) | collective-permute-done | bytes 917536 | tf_op jit(solution)/shard_map/ppermute | solution.py:113
  74.6 5.4 %collective-permute-start.13 = (f32[3,128,512]{2,1,0:T(8,128)S(1)}, f32[3,128,512]{2,1,0:T(8,128)}, u32[]{:S(2)}, u32[]{:S(2)}) collective-permute-start(f32[3,128,512]{2,1,0:T(8,128)S(1)} %get-tuple-element.34), channel_id=1, source_target_pairs={{0,2},{6,4},{1,3},{7,5},{8,10},{14,12},{9,11},{15,13},{16,18},{22,... | collective-permute-start | bytes 2359304 | tf_op jit(solution)/shard_map/ppermute | solution.py:113
  80.0 9.8 %collective-permute-start.11 = (f32[3,128,512]{2,1,0:T(8,128)}, f32[3,128,512]{2,1,0:T(8,128)}, u32[]{:S(2)}, u32[]{:S(2)}) collective-permute-start(f32[3,128,512]{2,1,0:T(8,128)} %get-tuple-element.32), channel_id=1, source_target_pairs={{0,2},{6,4},{1,3},{7,5},{8,10},{14,12},{9,11},{15,13},{16,18},{22,... | collective-permute-start | bytes 2359304 | tf_op jit(solution)/shard_map/ppermute | solution.py:113
  89.8 2.4 %fusion.20 = (f32[9,128,128]{2,1,0:T(8,128)}, f32[9,128,128]{2,1,0:T(8,128)}) fusion(f32[18,128,128]{2,1,0:T(8,128)} %collective-permute-done.9), kind=kLoop, calls=%fused_computation.43 | loop fusion | bytes 2359296 | tf_op jit(solution)/shard_map/slice | solution.py:150
  94.7 5.8 %shard_map.28.refs_9_ = f32[3,128,512]{2,1,0:T(8,128)S(1)} custom-call(s32[1]{0:T(128)} %bitcast.7.offset_ref, f32[18,128,128]{2,1,0:T(8,128)S(1)} %bitcast.63, f32[18,128,128]{2,1,0:T(8,128)} %collective-permute-done.3.refs_1_, f32[18,128,128]{2,1,0:T(8,128)} %collective-permute-done.4.refs_2_, f32[18,128,128]{2,1,0:T(8,128)} %collective-permute-done.7.refs_3_, ...), custom_call_target="tpu_custom_call" | custom-call | tf_op jit(solution)/shard_map/pallas_call | solution.py:76
  102.2 2.2 %slice.100 = f32[12,128,128]{2,1,0:T(8,128)} slice(f32[18,128,128]{2,1,0:T(8,128)} %collective-permute-done.refs_1_), slice={[0:12], [0:128], [0:128]} | slice | bytes 1572864 | tf_op jit(solution)/shard_map/slice | solution.py:150
  107.2 9.0 %collective-permute-start.15 = (f32[3,128,512]{2,1,0:T(8,128)}, f32[3,128,512]{2,1,0:T(8,128)}, u32[]{:S(2)}, u32[]{:S(2)}) collective-permute-start(f32[3,128,512]{2,1,0:T(8,128)} %get-tuple-element.36), channel_id=1, source_target_pairs={{0,2},{6,4},{1,3},{7,5},{8,10},{14,12},{9,11},{15,13},{16,18},{22,... | collective-permute-start | bytes 2359304 | tf_op jit(solution)/shard_map/ppermute | solution.py:113
  116.2 3.9 %shard_map.29.refs_4_ = f32[3,128,512]{2,1,0:T(8,128)S(1)} custom-call(s32[1]{0:T(128)} %bitcast.5.offset_ref, f32[14,128,128]{2,1,0:T(8,128)S(1)} %slice.79.refs_0_, f32[14,128,128]{2,1,0:T(8,128)} %collective-permute-done.5.refs_1_, f32[14,128,128]{2,1,0:T(8,128)S(1)} %collective-permute-done.6.refs_2_, ...), custom_call_target="tpu_custom_call", output_to_operand_aliasing={{}: (10, {})} | custom-call | tf_op jit(solution)/shard_map/pallas_call | solution.py:76
  120.2 2.0 %shard_map.30.refs_10_ = f32[3,128,512]{2,1,0:T(8,128)S(1)} custom-call(s32[1]{0:T(128)} %bitcast.5.offset_ref, f32[14,128,128]{2,1,0:T(8,128)S(1)} %slice.79.refs_0_, f32[14,128,128]{2,1,0:T(8,128)} %collective-permute-done.5.refs_1_, f32[14,128,128]{2,1,0:T(8,128)S(1)} %collective-permute-done.6.refs_2_, ...), custom_call_target="tpu_custom_call", output_to_operand_aliasing={{}: (5, {})} | custom-call | tf_op jit(solution)/shard_map/pallas_call | solution.py:76
  122.2 5.9 %shard_map.31 = f32[3,128,512]{2,1,0:T(8,128)S(1)} custom-call(s32[1]{0:T(128)} %bitcast.offset_ref, f32[18,128,128]{2,1,0:T(8,128)S(1)} %copy-done.3, f32[18,128,128]{2,1,0:T(8,128)} %collective-permute-done.refs_1_, f32[18,128,128]{2,1,0:T(8,128)} %collective-permute-done.1.refs_2_, ...), custom_call_target="tpu_custom_call", output_to_operand_aliasing={{}: (11, {})} | custom-call | tf_op jit(solution)/shard_map/pallas_call | solution.py:76
  129.5 5.5 %collective-permute-start.25 = (f32[3,128,512]{2,1,0:T(8,128)}, f32[3,128,512]{2,1,0:T(8,128)S(1)}, u32[]{:S(2)}, u32[]{:S(2)}) collective-permute-start(f32[3,128,512]{2,1,0:T(8,128)} %get-tuple-element.42), channel_id=1, source_target_pairs={{0,2},{6,4},{1,3},{7,5},{8,10},{14,12},{9,11},{15,13},{16,18},{22,... | collective-permute-start | bytes 2359304 | tf_op jit(solution)/shard_map/ppermute | solution.py:113
  135.0 2.1 %fusion.19 = (f32[3,128,128]{2,1,0:T(8,128)}, f32[3,128,128]{2,1,0:T(8,128)}, f32[3,128,128]{2,1,0:T(8,128)}, f32[3,128,128]{2,1,0:T(8,128)S(1)}) fusion(f32[50,128,128]{2,1,0:T(8,128)} %bitcast.112), kind=kLoop, calls=%fused_computation.42 | loop fusion | bytes 1572864 | tf_op jit(solution)/shard_map/slice | solution.py:150
  140.7 3.5 %shard_map.32.refs_5_ = f32[1,128,512]{2,1,0:T(8,128)S(1)} custom-call(s32[1]{0:T(128)} %bitcast.7.offset_ref, f32[9,128,128]{2,1,0:T(8,128)} %get-tuple-element.37.refs_0_, f32[9,128,128]{2,1,0:T(8,128)} %collective-permute-done.16.refs_1_, f32[200,128,512]{2,1,0:T(8,128)} %bitcast.86, f32[200,128,512]{2,1,0:T(8,128)} %bitcast.85, f32[200,128,512]{2,1,0:T(8,128)} %bitcast.87), custom_call_target="tpu_custom_call" | custom-call | tf_op jit(solution)/shard_map/pallas_call | solution.py:76
  146.9 6.4 %collective-permute-start.24 = (f32[2,128,512]{2,1,0:T(8,128)S(1)}, f32[2,128,512]{2,1,0:T(8,128)S(1)}, u32[]{:S(2)}, u32[]{:S(2)}) collective-permute-start(f32[2,128,512]{2,1,0:T(8,128)S(1)} %constant_dynamic-slice_fusion.1), channel_id=1, source_target_pairs={{0,2},{6,4},{1,3},{7,5},{8,10},{14,12},{9,11},{15,13},{16,18},{22,... | collective-permute-start | bytes 1572872 | tf_op jit(solution)/shard_map/ppermute | solution.py:113
  156.5 1.8 shard_map.38.refs_6_
  158.4 1.9 shard_map.39.refs_6_
  160.3 1.8 shard_map.40.refs_6_
  167.2 1.8 bitcast_add_fusion.1
  169.0 3.2 %shard_map.33.refs_7_ = f32[1,128,512]{2,1,0:T(8,128)S(1)} custom-call(s32[1]{0:T(128)} %bitcast.12.offset_ref, f32[9,128,128]{2,1,0:T(8,128)S(1)} %copy-done.6, f32[9,128,128]{2,1,0:T(8,128)} %collective-permute-done.14.refs_1_, f32[200,128,512]{2,1,0:T(8,128)} %bitcast.88, f32[200,128,512]{2,1,0:T(8,128)} %bitcast.89, ...), custom_call_target="tpu_custom_call", output_to_operand_aliasing={{}: (6, {})} | custom-call | tf_op jit(solution)/shard_map/pallas_call | solution.py:76
  172.3 2.7 %shard_map.34.refs_2_ = f32[1,128,512]{2,1,0:T(8,128)S(1)} custom-call(s32[1]{0:T(128)} %bitcast.5.offset_ref, f32[14,128,128]{2,1,0:T(8,128)} %collective-permute-done.19.refs_0_, f32[200,128,512]{2,1,0:T(8,128)} %bitcast.91, f32[200,128,512]{2,1,0:T(8,128)} %bitcast.92, f32[200,128,512]{2,1,0:T(8,128)} %bitcast.93, ...), custom_call_target="tpu_custom_call", output_to_operand_aliasing={{}: (8, {})} | custom-call | tf_op jit(solution)/shard_map/pallas_call | solution.py:76
  176.6 2.9 %shard_map.36.refs_8_ = f32[1,128,512]{2,1,0:T(8,128)S(1)} custom-call(s32[1]{0:T(128)} %bitcast.offset_ref, f32[12,128,128]{2,1,0:T(8,128)} %collective-permute-done.10.refs_0_, f32[12,128,128]{2,1,0:T(8,128)} %collective-permute-done.18.refs_1_, f32[200,128,512]{2,1,0:T(8,128)} %bitcast.98, ...), custom_call_target="tpu_custom_call", output_to_operand_aliasing={{}: (9, {})} | custom-call | tf_op jit(solution)/shard_map/pallas_call | solution.py:76
  179.6 2.2 %shard_map.37 = f32[1,128,512]{2,1,0:T(8,128)S(1)} custom-call(s32[1]{0:T(128)} %bitcast.11.offset_ref, f32[6,128,128]{2,1,0:T(8,128)} %collective-permute-done.12.refs_0_, f32[6,128,128]{2,1,0:T(8,128)} %collective-permute-done.17.refs_1_, f32[200,128,512]{2,1,0:T(8,128)} %bitcast.104, f32[200,128,512]{2,1,0:T(8,128)} %bitcast.105, ...), custom_call_target="tpu_custom_call", output_to_operand_aliasing={{}: (9, {})} | custom-call | tf_op jit(solution)/shard_map/pallas_call | solution.py:76
  189.8 2.0 %collective-permute-start.23 = (f32[64,512]{1,0:T(8,128)S(1)}, f32[64,512]{1,0:T(8,128)S(1)}, u32[]{:S(2)}, u32[]{:S(2)}) collective-permute-start(f32[64,512]{1,0:T(8,128)S(1)} %get-tuple-element.63), channel_id=1, source_target_pairs={{0,24},{8,16},{16,8},{24,0},{1,25},{9,17},{17,9},{25,1},{2,26},{10... | collective-permute-start | bytes 393224 | tf_op jit(solution)/shard_map/ppermute | solution.py:249
  195.3 3.3 %collective-permute-done.22 = f32[64,512]{1,0:T(8,128)S(1)} collective-permute-done((f32[64,512]{1,0:T(8,128)S(1)}, f32[64,512]{1,0:T(8,128)S(1)}, u32[]{:S(2)}, u32[]{:S(2)}) %collective-permute-start.22) | collective-permute-done | bytes 131104 | tf_op jit(solution)/shard_map/ppermute | solution.py:249
  198.6 2.3 %collective-permute-done.30 = f32[64,512]{1,0:T(8,128)S(1)} collective-permute-done((f32[64,512]{1,0:T(8,128)S(1)}, f32[64,512]{1,0:T(8,128)S(1)}, u32[]{:S(2)}, u32[]{:S(2)}) %collective-permute-start.30) | collective-permute-done | bytes 131104 | tf_op jit(solution)/shard_map/ppermute | solution.py:113
  (93 shorter events, 47.2 us)
Async XLA Ops:
  1.4 30.0 %collective-permute-start.3 = (f32[18,128,128]{2,1,0:T(8,128)S(1)}, f32[18,128,128]{2,1,0:T(8,128)}, u32[]{:S(2)}, u32[]{:S(2)}) collective-permute-start(f32[18,128,128]{2,1,0:T(8,128)S(1)} %bitcast.61), channel_id=1, source_target_pairs={{0,2},{2,0},{4,6},{6,4},{1,3},{3,1},{5,7},{7,5},{8,10},{10,8},{12,... | collective-permute-start | bytes 3538952 | tf_op jit(solution)/shard_map/ppermute | solution.py:113
  4.4 26.9 %collective-permute-start.4 = (f32[18,128,128]{2,1,0:T(8,128)S(1)}, f32[18,128,128]{2,1,0:T(8,128)}, u32[]{:S(2)}, u32[]{:S(2)}) collective-permute-start(f32[18,128,128]{2,1,0:T(8,128)S(1)} %bitcast.62), channel_id=1, source_target_pairs={{2,4},{4,2},{3,5},{5,3},{10,12},{12,10},{11,13},{13,11},{18,20},{2... | collective-permute-start | bytes 3538952 | tf_op jit(solution)/shard_map/ppermute | solution.py:113
  7.6 23.7 %copy-start.2 = (f32[18,128,128]{2,1,0:T(8,128)}, f32[18,128,128]{2,1,0:T(8,128)S(1)}, u32[]{:S(2)}) copy-start(f32[18,128,128]{2,1,0:T(8,128)S(1)} %slice.78.refs_0_) | copy-start | bytes 3538948
  7.6 49.0 %collective-permute-start = (f32[18,128,128]{2,1,0:T(8,128)S(1)}, f32[18,128,128]{2,1,0:T(8,128)}, u32[]{:S(2)}, u32[]{:S(2)}) collective-permute-start(f32[18,128,128]{2,1,0:T(8,128)S(1)} %slice.78.refs_0_), channel_id=1, source_target_pairs={{0,2},{2,0},{4,6},{6,4},{1,3},{3,1},{5,7},{7,5},{8,10},{10,8},{12,... | collective-permute-start | bytes 3538952 | tf_op jit(solution)/shard_map/ppermute | solution.py:113
  11.0 45.7 %collective-permute-start.1 = (f32[18,128,128]{2,1,0:T(8,128)S(1)}, f32[18,128,128]{2,1,0:T(8,128)}, u32[]{:S(2)}, u32[]{:S(2)}) collective-permute-start(f32[18,128,128]{2,1,0:T(8,128)S(1)} %slice.78.refs_0_), channel_id=1, source_target_pairs={{2,4},{4,2},{3,5},{5,3},{10,12},{12,10},{11,13},{13,11},{18,20},{2... | collective-permute-start | bytes 3538952 | tf_op jit(solution)/shard_map/ppermute | solution.py:113
  31.4 43.3 %collective-permute-start.5 = (f32[14,128,128]{2,1,0:T(8,128)S(1)}, f32[14,128,128]{2,1,0:T(8,128)}, u32[]{:S(2)}, u32[]{:S(2)}) collective-permute-start(f32[14,128,128]{2,1,0:T(8,128)S(1)} %slice.79.refs_0_), channel_id=1, source_target_pairs={{0,2},{6,4},{1,3},{7,5},{8,10},{14,12},{9,11},{15,13},{16,18},{22,... | collective-permute-start | bytes 2752520 | tf_op jit(solution)/shard_map/ppermute | solution.py:113
  39.3 40.7 %collective-permute-start.9 = (f32[18,128,128]{2,1,0:T(8,128)}, f32[18,128,128]{2,1,0:T(8,128)}, u32[]{:S(2)}, u32[]{:S(2)}) collective-permute-start(f32[18,128,128]{2,1,0:T(8,128)} %collective-permute-done.3.refs_1_), channel_id=1, source_target_pairs={{2,4},{4,2},{3,5},{5,3},{10,12},{12,10},{11,13},{13,11},{18,20},{2... | collective-permute-start | bytes 3538952 | tf_op jit(solution)/shard_map/ppermute | solution.py:113
  40.9 51.3 %collective-permute-start.7 = (f32[18,128,128]{2,1,0:T(8,128)}, f32[18,128,128]{2,1,0:T(8,128)}, u32[]{:S(2)}, u32[]{:S(2)}) collective-permute-start(f32[18,128,128]{2,1,0:T(8,128)} %collective-permute-done.4.refs_2_), channel_id=1, source_target_pairs={{2,0},{4,6},{3,1},{5,7},{10,8},{12,14},{11,9},{13,15},{18,16},{20,... | collective-permute-start | bytes 3538952 | tf_op jit(solution)/shard_map/ppermute | solution.py:113
  56.6 50.6 %collective-permute-start.2 = (f32[18,128,128]{2,1,0:T(8,128)}, f32[18,128,128]{2,1,0:T(8,128)}, u32[]{:S(2)}, u32[]{:S(2)}) collective-permute-start(f32[18,128,128]{2,1,0:T(8,128)} %collective-permute-done.1.refs_2_), channel_id=1, source_target_pairs={{2,0},{4,6},{3,1},{5,7},{10,8},{12,14},{11,9},{13,15},{18,16},{20,... | collective-permute-start | bytes 3538952 | tf_op jit(solution)/shard_map/ppermute | solution.py:113
  57.9 42.6 %collective-permute-start.6 = (f32[14,128,128]{2,1,0:T(8,128)S(1)}, f32[14,128,128]{2,1,0:T(8,128)S(1)}, u32[]{:S(2)}, u32[]{:S(2)}) collective-permute-start(f32[14,128,128]{2,1,0:T(8,128)S(1)} %slice.79.refs_0_), channel_id=1, source_target_pairs={{2,4},{4,2},{3,5},{5,3},{10,12},{12,10},{11,13},{13,11},{18,20},{2... | collective-permute-start | bytes 2752520 | tf_op jit(solution)/shard_map/ppermute | solution.py:113
  74.6 25.9 %collective-permute-start.13 = (f32[3,128,512]{2,1,0:T(8,128)S(1)}, f32[3,128,512]{2,1,0:T(8,128)}, u32[]{:S(2)}, u32[]{:S(2)}) collective-permute-start(f32[3,128,512]{2,1,0:T(8,128)S(1)} %get-tuple-element.34), channel_id=1, source_target_pairs={{0,2},{6,4},{1,3},{7,5},{8,10},{14,12},{9,11},{15,13},{16,18},{22,... | collective-permute-start | bytes 2359304 | tf_op jit(solution)/shard_map/ppermute | solution.py:113
  80.0 48.2 %collective-permute-start.11 = (f32[3,128,512]{2,1,0:T(8,128)}, f32[3,128,512]{2,1,0:T(8,128)}, u32[]{:S(2)}, u32[]{:S(2)}) collective-permute-start(f32[3,128,512]{2,1,0:T(8,128)} %get-tuple-element.32), channel_id=1, source_target_pairs={{0,2},{6,4},{1,3},{7,5},{8,10},{14,12},{9,11},{15,13},{16,18},{22,... | collective-permute-start | bytes 2359304 | tf_op jit(solution)/shard_map/ppermute | solution.py:113
  92.2 37.3 %collective-permute-start.16 = (f32[9,128,128]{2,1,0:T(8,128)}, f32[9,128,128]{2,1,0:T(8,128)}, u32[]{:S(2)}, u32[]{:S(2)}) collective-permute-start(f32[9,128,128]{2,1,0:T(8,128)} %get-tuple-element.37.refs_0_), channel_id=1, source_target_pairs={{2,0},{4,6},{3,1},{5,7},{10,8},{12,14},{11,9},{13,15},{18,16},{20,... | collective-permute-start | bytes 1769480 | tf_op jit(solution)/shard_map/ppermute | solution.py:113
  100.6 46.3 %collective-permute-start.19 = (f32[14,128,128]{2,1,0:T(8,128)}, f32[14,128,128]{2,1,0:T(8,128)}, u32[]{:S(2)}, u32[]{:S(2)}) collective-permute-start(f32[14,128,128]{2,1,0:T(8,128)} %collective-permute-done.5.refs_1_), channel_id=1, source_target_pairs={{2,4},{4,2},{3,5},{5,3},{10,12},{12,10},{11,13},{13,11},{18,20},{2... | collective-permute-start | bytes 2752520 | tf_op jit(solution)/shard_map/ppermute | solution.py:113
  104.3 39.8 %collective-permute-start.10 = (f32[12,128,128]{2,1,0:T(8,128)}, f32[12,128,128]{2,1,0:T(8,128)}, u32[]{:S(2)}, u32[]{:S(2)}) collective-permute-start(f32[12,128,128]{2,1,0:T(8,128)} %slice.100), channel_id=1, source_target_pairs={{2,4},{4,2},{3,5},{5,3},{10,12},{12,10},{11,13},{13,11},{18,20},{2... | collective-permute-start | bytes 2359304 | tf_op jit(solution)/shard_map/ppermute | solution.py:113
  107.2 38.4 %collective-permute-start.15 = (f32[3,128,512]{2,1,0:T(8,128)}, f32[3,128,512]{2,1,0:T(8,128)}, u32[]{:S(2)}, u32[]{:S(2)}) collective-permute-start(f32[3,128,512]{2,1,0:T(8,128)} %get-tuple-element.36), channel_id=1, source_target_pairs={{0,2},{6,4},{1,3},{7,5},{8,10},{14,12},{9,11},{15,13},{16,18},{22,... | collective-permute-start | bytes 2359304 | tf_op jit(solution)/shard_map/ppermute | solution.py:113
  128.2 27.0 %collective-permute-start.14 = (f32[9,128,128]{2,1,0:T(8,128)S(1)}, f32[9,128,128]{2,1,0:T(8,128)}, u32[]{:S(2)}, u32[]{:S(2)}) collective-permute-start(f32[9,128,128]{2,1,0:T(8,128)S(1)} %copy-done.6), channel_id=1, source_target_pairs={{2,0},{4,6},{3,1},{5,7},{10,8},{12,14},{11,9},{13,15},{18,16},{20,... | collective-permute-start | bytes 1769480 | tf_op jit(solution)/shard_map/ppermute | solution.py:113
  129.5 34.1 %collective-permute-start.25 = (f32[3,128,512]{2,1,0:T(8,128)}, f32[3,128,512]{2,1,0:T(8,128)S(1)}, u32[]{:S(2)}, u32[]{:S(2)}) collective-permute-start(f32[3,128,512]{2,1,0:T(8,128)} %get-tuple-element.42), channel_id=1, source_target_pairs={{0,2},{6,4},{1,3},{7,5},{8,10},{14,12},{9,11},{15,13},{16,18},{22,... | collective-permute-start | bytes 2359304 | tf_op jit(solution)/shard_map/ppermute | solution.py:113
  144.2 17.9 %collective-permute-start.12 = (f32[6,128,128]{2,1,0:T(8,128)S(1)}, f32[6,128,128]{2,1,0:T(8,128)}, u32[]{:S(2)}, u32[]{:S(2)}) collective-permute-start(f32[6,128,128]{2,1,0:T(8,128)S(1)} %slice.99), channel_id=1, source_target_pairs={{2,4},{4,2},{3,5},{5,3},{10,12},{12,10},{11,13},{13,11},{18,20},{2... | collective-permute-start | bytes 1179656 | tf_op jit(solution)/shard_map/ppermute | solution.py:113
  145.6 31.0 %collective-permute-start.18 = (f32[12,128,128]{2,1,0:T(8,128)}, f32[12,128,128]{2,1,0:T(8,128)}, u32[]{:S(2)}, u32[]{:S(2)}) collective-permute-start(f32[12,128,128]{2,1,0:T(8,128)} %collective-permute-done.10.refs_0_), channel_id=1, source_target_pairs={{2,0},{4,6},{3,1},{5,7},{10,8},{12,14},{11,9},{13,15},{18,16},{20,... | collective-permute-start | bytes 2359304 | tf_op jit(solution)/shard_map/ppermute | solution.py:113
  146.9 17.4 %collective-permute-start.24 = (f32[2,128,512]{2,1,0:T(8,128)S(1)}, f32[2,128,512]{2,1,0:T(8,128)S(1)}, u32[]{:S(2)}, u32[]{:S(2)}) collective-permute-start(f32[2,128,512]{2,1,0:T(8,128)S(1)} %constant_dynamic-slice_fusion.1), channel_id=1, source_target_pairs={{0,2},{6,4},{1,3},{7,5},{8,10},{14,12},{9,11},{15,13},{16,18},{22,... | collective-permute-start | bytes 1572872 | tf_op jit(solution)/shard_map/ppermute | solution.py:113
  155.1 12.1 %collective-permute-start.8 = (f32[3,64,512]{2,1,0:T(8,128)}, f32[3,64,512]{2,1,0:T(8,128)}, u32[]{:S(2)}, u32[]{:S(2)}) collective-permute-start(f32[3,64,512]{2,1,0:T(8,128)} %dynamic-slice_bitcast_fusion.1), channel_id=1, source_target_pairs={{0,1},{1,0},{2,3},{3,2},{4,5},{5,4},{6,7},{7,6},{8,9},{9,8},{10,11... | collective-permute-start | bytes 1179656 | tf_op jit(solution)/shard_map/ppermute | solution.py:237
  162.1 17.4 %collective-permute-start.17 = (f32[6,128,128]{2,1,0:T(8,128)}, f32[6,128,128]{2,1,0:T(8,128)}, u32[]{:S(2)}, u32[]{:S(2)}) collective-permute-start(f32[6,128,128]{2,1,0:T(8,128)} %collective-permute-done.12.refs_0_), channel_id=1, source_target_pairs={{2,0},{4,6},{3,1},{5,7},{10,8},{12,14},{11,9},{13,15},{18,16},{20,... | collective-permute-start | bytes 1179656 | tf_op jit(solution)/shard_map/ppermute | solution.py:113
  166.7 15.2 %collective-permute-start.26 = (f32[3,64,512]{2,1,0:T(8,128)}, f32[3,64,512]{2,1,0:T(8,128)}, u32[]{:S(2)}, u32[]{:S(2)}) collective-permute-start(f32[3,64,512]{2,1,0:T(8,128)} %dynamic-slice_bitcast_fusion), channel_id=1, source_target_pairs={{0,1},{1,0},{2,3},{3,2},{4,5},{5,4},{6,7},{7,6},{8,9},{9,8},{10,11... | collective-permute-start | bytes 1179656 | tf_op jit(solution)/shard_map/ppermute | solution.py:237
  181.8 4.8 %collective-permute-start.20 = (f32[1,64,512]{2,1,0:T(8,128)S(1)}, f32[1,64,512]{2,1,0:T(8,128)S(1)}, u32[]{:S(2)}, u32[]{:S(2)}) collective-permute-start(f32[1,64,512]{2,1,0:T(8,128)S(1)} %dynamic-slice_bitcast_fusion.2), channel_id=1, source_target_pairs={{0,1},{1,0},{2,3},{3,2},{4,5},{5,4},{6,7},{7,6},{8,9},{9,8},{10,11... | collective-permute-start | bytes 393224 | tf_op jit(solution)/shard_map/ppermute | solution.py:237
  183.1 6.8 %collective-permute-start.27 = (f32[64,512]{1,0:T(8,128)S(1)}, f32[64,512]{1,0:T(8,128)S(1)}, u32[]{:S(2)}, u32[]{:S(2)}) collective-permute-start(f32[64,512]{1,0:T(8,128)S(1)} %get-tuple-element.64), channel_id=1, source_target_pairs={{0,8},{8,0},{16,24},{24,16},{1,9},{9,1},{17,25},{25,17},{2,10},{10... | collective-permute-start | bytes 393224 | tf_op jit(solution)/shard_map/ppermute | solution.py:249
  184.6 8.3 %collective-permute-start.28 = (f32[64,512]{1,0:T(8,128)S(1)}, f32[64,512]{1,0:T(8,128)S(1)}, u32[]{:S(2)}, u32[]{:S(2)}) collective-permute-start(f32[64,512]{1,0:T(8,128)S(1)} %get-tuple-element.65), channel_id=1, source_target_pairs={{0,16},{8,24},{16,0},{24,8},{1,17},{9,25},{17,1},{25,9},{2,18},{10... | collective-permute-start | bytes 393224 | tf_op jit(solution)/shard_map/ppermute | solution.py:249
  186.1 7.3 %collective-permute-start.29 = (f32[64,512]{1,0:T(8,128)S(1)}, f32[64,512]{1,0:T(8,128)S(1)}, u32[]{:S(2)}, u32[]{:S(2)}) collective-permute-start(f32[64,512]{1,0:T(8,128)S(1)} %get-tuple-element.66), channel_id=1, source_target_pairs={{0,24},{8,16},{16,8},{24,0},{1,25},{9,17},{17,9},{25,1},{2,26},{10... | collective-permute-start | bytes 393224 | tf_op jit(solution)/shard_map/ppermute | solution.py:249
  186.8 8.6 %collective-permute-start.21 = (f32[64,512]{1,0:T(8,128)S(1)}, f32[64,512]{1,0:T(8,128)S(1)}, u32[]{:S(2)}, u32[]{:S(2)}) collective-permute-start(f32[64,512]{1,0:T(8,128)S(1)} %get-tuple-element.61), channel_id=1, source_target_pairs={{0,8},{8,0},{16,24},{24,16},{1,9},{9,1},{17,25},{25,17},{2,10},{10... | collective-permute-start | bytes 393224 | tf_op jit(solution)/shard_map/ppermute | solution.py:249
  188.3 10.3 %collective-permute-start.22 = (f32[64,512]{1,0:T(8,128)S(1)}, f32[64,512]{1,0:T(8,128)S(1)}, u32[]{:S(2)}, u32[]{:S(2)}) collective-permute-start(f32[64,512]{1,0:T(8,128)S(1)} %get-tuple-element.62), channel_id=1, source_target_pairs={{0,16},{8,24},{16,0},{24,8},{1,17},{9,25},{17,1},{25,9},{2,18},{10... | collective-permute-start | bytes 393224 | tf_op jit(solution)/shard_map/ppermute | solution.py:249
  189.8 8.8 %collective-permute-start.23 = (f32[64,512]{1,0:T(8,128)S(1)}, f32[64,512]{1,0:T(8,128)S(1)}, u32[]{:S(2)}, u32[]{:S(2)}) collective-permute-start(f32[64,512]{1,0:T(8,128)S(1)} %get-tuple-element.63), channel_id=1, source_target_pairs={{0,24},{8,16},{16,8},{24,0},{1,25},{9,17},{17,9},{25,1},{2,26},{10... | collective-permute-start | bytes 393224 | tf_op jit(solution)/shard_map/ppermute | solution.py:249
  193.5 7.4 %collective-permute-start.30 = (f32[64,512]{1,0:T(8,128)S(1)}, f32[64,512]{1,0:T(8,128)S(1)}, u32[]{:S(2)}, u32[]{:S(2)}) collective-permute-start(f32[64,512]{1,0:T(8,128)S(1)} %fusion.3), channel_id=1, source_target_pairs={{2,0},{4,6},{3,1},{5,7},{10,8},{12,14},{11,9},{13,15},{18,16},{20,... | collective-permute-start | bytes 393224 | tf_op jit(solution)/shard_map/ppermute | solution.py:113
  (11 other events, 31.4 us)

commit v9 on v8

--- a/solution.py
+++ b/solution.py
@@ -223,6 +223,8 @@
             value = find(tables[source], c)
         earlier = [entry[2] for n in queues for entry in [e for e in sent[n] if e[1] <= issue][-1:]]
         earlier += [v for v in recent.values() if v is not None]
+        if (into, c) == ("far_end", extra):
+            earlier.append(far_end[tails[0]])
         if earlier:
             value = after(value, *earlier)
         tables[into][c] = move(value)

time: 203 us -> 211 us (1.039)
  starting transfers between devices: 79.4 us -> 92 us
  waiting for transfers between devices: 53.5 us -> 49.2 us
    ppermute x22, starting transfers between devices: 70.1 us -> 82.6 us  [hop(): return lambda value: lax.ppermute(value, 'col', lanes)]
    ppermute x22, waiting for transfers between devices: 48.1 us -> 44.3 us  [hop(): return lambda value: lax.ppermute(value, 'col', lanes)]
  transfers between devices with their start and end apart: 31 -> 31, of which waited for: 9 -> 10; matrix products, arithmetic and copies ran while one was open for 11% -> 11% of each run, Pallas kernels for 20% -> 19%
where the time goes in v9:
time: 211 us; the launch traced here: 210 us
  starting transfers between devices  92 us (44%)
  waiting for transfers between devices  49.2 us (23%)
  Pallas kernels  39.5 us (19%)
  local copies, waits for them, and re-layouts  24.6 us (12%)
  other arithmetic  3.72 us (2%)
    ppermute x22, starting transfers between devices, hop(): return lambda value: lax.ppermute(value, 'col', lanes)  82.6 us
    ppermute x22, waiting for transfers between devices, hop(): return lambda value: lax.ppermute(value, 'col', lanes)  44.3 us
    pallas_call x15, Pallas kernels, contract_run(): pl.pallas_call(functools.partial(contract_kernel, terms, per, total is No...  39.5 us
    slice x9, local copies, waits for them, and re-layouts, find(): return table[k] if k == c else table[k][c[0] - k[0]:c[1] - k[0]]  11.3 us
    ppermute x6, starting transfers between devices, row_sum(): lax.ppermute(part(row ^ t), 'row', [(r, r ^ t) for r in range(4)])  8.75 us
    ppermute x6, waiting for transfers between devices, row_sum(): lax.ppermute(part(row ^ t), 'row', [(r, r ^ t) for r in range(4)])  4.91 us
    dynamic_slice x2, local copies, waits for them, and re-layouts, shards(): lax.dynamic_slice_in_dim(integral, shift + c[0], c[1] - c[0], axis=0)  4.39 us
  transfers between devices with their start and end apart: 31, of which 10 were waited for; matrix products, arithmetic and copies ran while one was open for 11% of the time, Pallas kernels for 19%

profile of v9, /device:TPU:0, one launch (start us, length us, event | category | flops | bytes accessed | tf_op | source)
XLA Modules:
  0.0 209.5 jit_solution(4898279952888125351)
XLA Ops:
  1.4 3.1 %collective-permute-start.3 = (f32[18,128,128]{2,1,0:T(8,128)S(1)}, f32[18,128,128]{2,1,0:T(8,128)}, u32[]{:S(2)}, u32[]{:S(2)}) collective-permute-start(f32[18,128,128]{2,1,0:T(8,128)S(1)} %bitcast.61), channel_id=1, source_target_pairs={{0,2},{2,0},{4,6},{6,4},{1,3},{3,1},{5,7},{7,5},{8,10},{10,8},{12,... | collective-permute-start | bytes 3538952 | tf_op jit(solution)/shard_map/ppermute | solution.py:113
  4.4 1.8 collective-permute-start.4
  7.6 3.3 %collective-permute-start = (f32[18,128,128]{2,1,0:T(8,128)S(1)}, f32[18,128,128]{2,1,0:T(8,128)}, u32[]{:S(2)}, u32[]{:S(2)}) collective-permute-start(f32[18,128,128]{2,1,0:T(8,128)S(1)} %slice.78.refs_0_), channel_id=1, source_target_pairs={{0,2},{2,0},{4,6},{6,4},{1,3},{3,1},{5,7},{7,5},{8,10},{10,8},{12,... | collective-permute-start | bytes 3538952 | tf_op jit(solution)/shard_map/ppermute | solution.py:113
  12.6 18.7 %collective-permute-done.3.refs_1_ = f32[18,128,128]{2,1,0:T(8,128)} collective-permute-done((f32[18,128,128]{2,1,0:T(8,128)S(1)}, f32[18,128,128]{2,1,0:T(8,128)}, u32[]{:S(2)}, u32[]{:S(2)}) %collective-permute-start.3) | collective-permute-done | bytes 1179680 | tf_op jit(solution)/shard_map/ppermute | solution.py:113
  35.6 11.2 %collective-permute-start.5 = (f32[14,128,128]{2,1,0:T(8,128)S(1)}, f32[14,128,128]{2,1,0:T(8,128)}, u32[]{:S(2)}, u32[]{:S(2)}) collective-permute-start(f32[14,128,128]{2,1,0:T(8,128)S(1)} %slice.79.refs_0_), channel_id=1, source_target_pairs={{0,2},{6,4},{1,3},{7,5},{8,10},{14,12},{9,11},{15,13},{16,18},{22,... | collective-permute-start | bytes 2752520 | tf_op jit(solution)/shard_map/ppermute | solution.py:113
  46.8 3.3 %constant_dynamic-slice_fusion.4 = (f32[3,128,512]{2,1,0:T(8,128)}, f32[3,128,512]{2,1,0:T(8,128)}, f32[3,128,512]{2,1,0:T(8,128)}, f32[3,128,512]{2,1,0:T(8,128)S(1)}) fusion(f32[200,128,512]{2,1,0:T(8,128)} %bitcast.64, s32[]{:T(128)S(6)} %select_n.73, s32[]{:T(128)S(6)} %select_n.85, s32[]{:T(128)S(6)} %select_n.75, s32[]{:T(128)S(6)} %select_n.74), kind=kLoop, calls=%fused_computation.41 | loop fusion | bytes 6291472 | tf_op jit(solution)/shard_map/dynamic_slice | solution.py:221
  50.1 6.5 %collective-permute-done.refs_1_ = f32[18,128,128]{2,1,0:T(8,128)} collective-permute-done((f32[18,128,128]{2,1,0:T(8,128)S(1)}, f32[18,128,128]{2,1,0:T(8,128)}, u32[]{:S(2)}, u32[]{:S(2)}) %collective-permute-start) | collective-permute-done | bytes 1179680 | tf_op jit(solution)/shard_map/ppermute | solution.py:113
  56.6 7.0 %collective-permute-start.13 = (f32[3,128,512]{2,1,0:T(8,128)S(1)}, f32[3,128,512]{2,1,0:T(8,128)S(1)}, u32[]{:S(2)}, u32[]{:S(2)}) collective-permute-start(f32[3,128,512]{2,1,0:T(8,128)S(1)} %get-tuple-element.34), channel_id=1, source_target_pairs={{0,2},{6,4},{1,3},{7,5},{8,10},{14,12},{9,11},{15,13},{16,18},{22,... | collective-permute-start | bytes 2359304 | tf_op jit(solution)/shard_map/ppermute | solution.py:113
  64.4 11.4 %collective-permute-done.5.refs_1_ = f32[14,128,128]{2,1,0:T(8,128)} collective-permute-done((f32[14,128,128]{2,1,0:T(8,128)S(1)}, f32[14,128,128]{2,1,0:T(8,128)}, u32[]{:S(2)}, u32[]{:S(2)}) %collective-permute-start.5) | collective-permute-done | bytes 917536 | tf_op jit(solution)/shard_map/ppermute | solution.py:113
  78.2 3.7 %collective-permute-done.7.refs_3_ = f32[18,128,128]{2,1,0:T(8,128)} collective-permute-done((f32[18,128,128]{2,1,0:T(8,128)}, f32[18,128,128]{2,1,0:T(8,128)}, u32[]{:S(2)}, u32[]{:S(2)}) %collective-permute-start.7) | collective-permute-done | bytes 1179680 | tf_op jit(solution)/shard_map/ppermute | solution.py:113
  83.5 10.3 %collective-permute-start.11 = (f32[3,128,512]{2,1,0:T(8,128)}, f32[3,128,512]{2,1,0:T(8,128)}, u32[]{:S(2)}, u32[]{:S(2)}) collective-permute-start(f32[3,128,512]{2,1,0:T(8,128)} %get-tuple-element.32), channel_id=1, source_target_pairs={{0,2},{6,4},{1,3},{7,5},{8,10},{14,12},{9,11},{15,13},{16,18},{22,... | collective-permute-start | bytes 2359304 | tf_op jit(solution)/shard_map/ppermute | solution.py:113
  93.8 2.4 %fusion.20 = (f32[9,128,128]{2,1,0:T(8,128)}, f32[9,128,128]{2,1,0:T(8,128)}) fusion(f32[18,128,128]{2,1,0:T(8,128)} %collective-permute-done.9), kind=kLoop, calls=%fused_computation.43 | loop fusion | bytes 2359296 | tf_op jit(solution)/shard_map/slice | solution.py:150
  99.6 5.8 %shard_map.28.refs_9_ = f32[3,128,512]{2,1,0:T(8,128)S(1)} custom-call(s32[1]{0:T(128)} %bitcast.7.offset_ref, f32[18,128,128]{2,1,0:T(8,128)S(1)} %bitcast.63, f32[18,128,128]{2,1,0:T(8,128)} %collective-permute-done.3.refs_1_, f32[18,128,128]{2,1,0:T(8,128)} %collective-permute-done.4.refs_2_, f32[18,128,128]{2,1,0:T(8,128)} %collective-permute-done.7.refs_3_, ...), custom_call_target="tpu_custom_call" | custom-call | tf_op jit(solution)/shard_map/pallas_call | solution.py:76
  105.4 6.3 %collective-permute-start.15 = (f32[3,128,512]{2,1,0:T(8,128)}, f32[3,128,512]{2,1,0:T(8,128)}, u32[]{:S(2)}, u32[]{:S(2)}) collective-permute-start(f32[3,128,512]{2,1,0:T(8,128)} %get-tuple-element.36), channel_id=1, source_target_pairs={{0,2},{6,4},{1,3},{7,5},{8,10},{14,12},{9,11},{15,13},{16,18},{22,... | collective-permute-start | bytes 2359304 | tf_op jit(solution)/shard_map/ppermute | solution.py:113
  115.0 3.9 %shard_map.29.refs_4_ = f32[3,128,512]{2,1,0:T(8,128)S(1)} custom-call(s32[1]{0:T(128)} %bitcast.5.offset_ref, f32[14,128,128]{2,1,0:T(8,128)S(1)} %slice.79.refs_0_, f32[14,128,128]{2,1,0:T(8,128)} %collective-permute-done.5.refs_1_, f32[14,128,128]{2,1,0:T(8,128)S(1)} %collective-permute-done.6.refs_2_, ...), custom_call_target="tpu_custom_call", output_to_operand_aliasing={{}: (10, {})} | custom-call | tf_op jit(solution)/shard_map/pallas_call | solution.py:76
  119.0 2.0 shard_map.30.refs_10_
  121.1 5.9 %shard_map.31 = f32[3,128,512]{2,1,0:T(8,128)S(1)} custom-call(s32[1]{0:T(128)} %bitcast.offset_ref, f32[18,128,128]{2,1,0:T(8,128)S(1)} %copy-done.5, f32[18,128,128]{2,1,0:T(8,128)} %collective-permute-done.refs_1_, f32[18,128,128]{2,1,0:T(8,128)} %collective-permute-done.1.refs_2_, ...), custom_call_target="tpu_custom_call", output_to_operand_aliasing={{}: (11, {})} | custom-call | tf_op jit(solution)/shard_map/pallas_call | solution.py:76
  129.7 16.3 %collective-permute-start.25 = (f32[3,128,512]{2,1,0:T(8,128)}, f32[3,128,512]{2,1,0:T(8,128)S(1)}, u32[]{:S(2)}, u32[]{:S(2)}) collective-permute-start(f32[3,128,512]{2,1,0:T(8,128)} %get-tuple-element.42), channel_id=1, source_target_pairs={{0,2},{6,4},{1,3},{7,5},{8,10},{14,12},{9,11},{15,13},{16,18},{22,... | collective-permute-start | bytes 2359304 | tf_op jit(solution)/shard_map/ppermute | solution.py:113
  146.1 2.1 %fusion.19 = (f32[3,128,128]{2,1,0:T(8,128)}, f32[3,128,128]{2,1,0:T(8,128)}, f32[3,128,128]{2,1,0:T(8,128)}, f32[3,128,128]{2,1,0:T(8,128)S(1)}) fusion(f32[50,128,128]{2,1,0:T(8,128)} %bitcast.112), kind=kLoop, calls=%fused_computation.42 | loop fusion | bytes 1572864 | tf_op jit(solution)/shard_map/slice | solution.py:150
  150.9 3.5 %shard_map.32.refs_5_ = f32[1,128,512]{2,1,0:T(8,128)S(1)} custom-call(s32[1]{0:T(128)} %bitcast.7.offset_ref, f32[9,128,128]{2,1,0:T(8,128)} %get-tuple-element.37.refs_0_, f32[9,128,128]{2,1,0:T(8,128)} %collective-permute-done.16.refs_1_, f32[200,128,512]{2,1,0:T(8,128)} %bitcast.86, f32[200,128,512]{2,1,0:T(8,128)} %bitcast.85, f32[200,128,512]{2,1,0:T(8,128)} %bitcast.87), custom_call_target="tpu_custom_call" | custom-call | tf_op jit(solution)/shard_map/pallas_call | solution.py:76
  155.6 5.4 %collective-permute-start.24 = (f32[2,128,512]{2,1,0:T(8,128)S(1)}, f32[2,128,512]{2,1,0:T(8,128)S(1)}, u32[]{:S(2)}, u32[]{:S(2)}) collective-permute-start(f32[2,128,512]{2,1,0:T(8,128)S(1)} %constant_dynamic-slice_fusion.1), channel_id=1, source_target_pairs={{0,2},{6,4},{1,3},{7,5},{8,10},{14,12},{9,11},{15,13},{16,18},{22,... | collective-permute-start | bytes 1572872 | tf_op jit(solution)/shard_map/ppermute | solution.py:113
  166.6 1.9 shard_map.39.refs_6_
  168.5 1.8 shard_map.40.refs_6_
  171.1 1.8 collective-permute-done.24.refs_3_.refs_4_
  175.1 1.8 bitcast_add_fusion.1
  176.9 3.2 %shard_map.33.refs_7_ = f32[1,128,512]{2,1,0:T(8,128)S(1)} custom-call(s32[1]{0:T(128)} %bitcast.12.offset_ref, f32[9,128,128]{2,1,0:T(8,128)S(1)} %copy-done.8, f32[9,128,128]{2,1,0:T(8,128)} %collective-permute-done.14.refs_1_, f32[200,128,512]{2,1,0:T(8,128)} %bitcast.88, f32[200,128,512]{2,1,0:T(8,128)} %bitcast.89, ...), custom_call_target="tpu_custom_call", output_to_operand_aliasing={{}: (6, {})} | custom-call | tf_op jit(solution)/shard_map/pallas_call | solution.py:76
  180.1 2.7 %shard_map.34.refs_2_ = f32[1,128,512]{2,1,0:T(8,128)S(1)} custom-call(s32[1]{0:T(128)} %bitcast.5.offset_ref, f32[14,128,128]{2,1,0:T(8,128)} %collective-permute-done.19.refs_0_, f32[200,128,512]{2,1,0:T(8,128)} %bitcast.91, f32[200,128,512]{2,1,0:T(8,128)} %bitcast.92, f32[200,128,512]{2,1,0:T(8,128)} %bitcast.93, ...), custom_call_target="tpu_custom_call", output_to_operand_aliasing={{}: (8, {})} | custom-call | tf_op jit(solution)/shard_map/pallas_call | solution.py:76
  184.5 2.9 %shard_map.36.refs_8_ = f32[1,128,512]{2,1,0:T(8,128)S(1)} custom-call(s32[1]{0:T(128)} %bitcast.offset_ref, f32[12,128,128]{2,1,0:T(8,128)} %collective-permute-done.10.refs_0_, f32[12,128,128]{2,1,0:T(8,128)} %collective-permute-done.18.refs_1_, f32[200,128,512]{2,1,0:T(8,128)} %bitcast.98, ...), custom_call_target="tpu_custom_call", output_to_operand_aliasing={{}: (9, {})} | custom-call | tf_op jit(solution)/shard_map/pallas_call | solution.py:76
  187.5 2.2 %shard_map.37 = f32[1,128,512]{2,1,0:T(8,128)S(1)} custom-call(s32[1]{0:T(128)} %bitcast.11.offset_ref, f32[6,128,128]{2,1,0:T(8,128)} %collective-permute-done.12.refs_0_, f32[6,128,128]{2,1,0:T(8,128)} %collective-permute-done.17.refs_1_, f32[200,128,512]{2,1,0:T(8,128)} %bitcast.104, f32[200,128,512]{2,1,0:T(8,128)} %bitcast.105, ...), custom_call_target="tpu_custom_call", output_to_operand_aliasing={{}: (9, {})} | custom-call | tf_op jit(solution)/shard_map/pallas_call | solution.py:76
  198.2 2.1 collective-permute-start.23
  203.7 2.9 %collective-permute-done.22 = f32[64,512]{1,0:T(8,128)S(1)} collective-permute-done((f32[64,512]{1,0:T(8,128)S(1)}, f32[64,512]{1,0:T(8,128)S(1)}, u32[]{:S(2)}, u32[]{:S(2)}) %collective-permute-start.22) | collective-permute-done | bytes 131104 | tf_op jit(solution)/shard_map/ppermute | solution.py:251
  206.6 2.2 %collective-permute-done.30 = f32[64,512]{1,0:T(8,128)S(1)} collective-permute-done((f32[64,512]{1,0:T(8,128)S(1)}, f32[64,512]{1,0:T(8,128)S(1)}, u32[]{:S(2)}, u32[]{:S(2)}) %collective-permute-start.30) | collective-permute-done | bytes 131104 | tf_op jit(solution)/shard_map/ppermute | solution.py:113
  (97 shorter events, 49.5 us)
Async XLA Ops:
  1.4 30.0 %collective-permute-start.3 = (f32[18,128,128]{2,1,0:T(8,128)S(1)}, f32[18,128,128]{2,1,0:T(8,128)}, u32[]{:S(2)}, u32[]{:S(2)}) collective-permute-start(f32[18,128,128]{2,1,0:T(8,128)S(1)} %bitcast.61), channel_id=1, source_target_pairs={{0,2},{2,0},{4,6},{6,4},{1,3},{3,1},{5,7},{7,5},{8,10},{10,8},{12,... | collective-permute-start | bytes 3538952 | tf_op jit(solution)/shard_map/ppermute | solution.py:113
  4.4 26.9 %collective-permute-start.4 = (f32[18,128,128]{2,1,0:T(8,128)S(1)}, f32[18,128,128]{2,1,0:T(8,128)}, u32[]{:S(2)}, u32[]{:S(2)}) collective-permute-start(f32[18,128,128]{2,1,0:T(8,128)S(1)} %bitcast.62), channel_id=1, source_target_pairs={{2,4},{4,2},{3,5},{5,3},{10,12},{12,10},{11,13},{13,11},{18,20},{2... | collective-permute-start | bytes 3538952 | tf_op jit(solution)/shard_map/ppermute | solution.py:113
  7.6 42.5 %copy-start.4 = (f32[18,128,128]{2,1,0:T(8,128)}, f32[18,128,128]{2,1,0:T(8,128)S(1)}, u32[]{:S(2)}) copy-start(f32[18,128,128]{2,1,0:T(8,128)S(1)} %slice.78.refs_0_) | copy-start | bytes 3538948
  7.6 49.0 %collective-permute-start = (f32[18,128,128]{2,1,0:T(8,128)S(1)}, f32[18,128,128]{2,1,0:T(8,128)}, u32[]{:S(2)}, u32[]{:S(2)}) collective-permute-start(f32[18,128,128]{2,1,0:T(8,128)S(1)} %slice.78.refs_0_), channel_id=1, source_target_pairs={{0,2},{2,0},{4,6},{6,4},{1,3},{3,1},{5,7},{7,5},{8,10},{10,8},{12,... | collective-permute-start | bytes 3538952 | tf_op jit(solution)/shard_map/ppermute | solution.py:113
  10.9 45.7 %collective-permute-start.1 = (f32[18,128,128]{2,1,0:T(8,128)S(1)}, f32[18,128,128]{2,1,0:T(8,128)}, u32[]{:S(2)}, u32[]{:S(2)}) collective-permute-start(f32[18,128,128]{2,1,0:T(8,128)S(1)} %slice.78.refs_0_), channel_id=1, source_target_pairs={{2,4},{4,2},{3,5},{5,3},{10,12},{12,10},{11,13},{13,11},{18,20},{2... | collective-permute-start | bytes 3538952 | tf_op jit(solution)/shard_map/ppermute | solution.py:113
  31.4 50.6 %collective-permute-start.7 = (f32[18,128,128]{2,1,0:T(8,128)}, f32[18,128,128]{2,1,0:T(8,128)}, u32[]{:S(2)}, u32[]{:S(2)}) collective-permute-start(f32[18,128,128]{2,1,0:T(8,128)} %collective-permute-done.4.refs_2_), channel_id=1, source_target_pairs={{2,0},{4,6},{3,1},{5,7},{10,8},{12,14},{11,9},{13,15},{18,16},{20,... | collective-permute-start | bytes 3538952 | tf_op jit(solution)/shard_map/ppermute | solution.py:113
  32.6 49.3 %collective-permute-start.9 = (f32[18,128,128]{2,1,0:T(8,128)}, f32[18,128,128]{2,1,0:T(8,128)}, u32[]{:S(2)}, u32[]{:S(2)}) collective-permute-start(f32[18,128,128]{2,1,0:T(8,128)} %collective-permute-done.3.refs_1_), channel_id=1, source_target_pairs={{2,4},{4,2},{3,5},{5,3},{10,12},{12,10},{11,13},{13,11},{18,20},{2... | collective-permute-start | bytes 3538952 | tf_op jit(solution)/shard_map/ppermute | solution.py:113
  35.6 40.2 %collective-permute-start.5 = (f32[14,128,128]{2,1,0:T(8,128)S(1)}, f32[14,128,128]{2,1,0:T(8,128)}, u32[]{:S(2)}, u32[]{:S(2)}) collective-permute-start(f32[14,128,128]{2,1,0:T(8,128)S(1)} %slice.79.refs_0_), channel_id=1, source_target_pairs={{0,2},{6,4},{1,3},{7,5},{8,10},{14,12},{9,11},{15,13},{16,18},{22,... | collective-permute-start | bytes 2752520 | tf_op jit(solution)/shard_map/ppermute | solution.py:113
  56.6 39.5 %collective-permute-start.13 = (f32[3,128,512]{2,1,0:T(8,128)S(1)}, f32[3,128,512]{2,1,0:T(8,128)S(1)}, u32[]{:S(2)}, u32[]{:S(2)}) collective-permute-start(f32[3,128,512]{2,1,0:T(8,128)S(1)} %get-tuple-element.34), channel_id=1, source_target_pairs={{0,2},{6,4},{1,3},{7,5},{8,10},{14,12},{9,11},{15,13},{16,18},{22,... | collective-permute-start | bytes 2359304 | tf_op jit(solution)/shard_map/ppermute | solution.py:113
  63.7 41.7 %collective-permute-start.6 = (f32[14,128,128]{2,1,0:T(8,128)S(1)}, f32[14,128,128]{2,1,0:T(8,128)S(1)}, u32[]{:S(2)}, u32[]{:S(2)}) collective-permute-start(f32[14,128,128]{2,1,0:T(8,128)S(1)} %slice.79.refs_0_), channel_id=1, source_target_pairs={{2,4},{4,2},{3,5},{5,3},{10,12},{12,10},{11,13},{13,11},{18,20},{2... | collective-permute-start | bytes 2752520 | tf_op jit(solution)/shard_map/ppermute | solution.py:113
  75.8 45.3 %collective-permute-start.2 = (f32[18,128,128]{2,1,0:T(8,128)}, f32[18,128,128]{2,1,0:T(8,128)}, u32[]{:S(2)}, u32[]{:S(2)}) collective-permute-start(f32[18,128,128]{2,1,0:T(8,128)} %collective-permute-done.1.refs_2_), channel_id=1, source_target_pairs={{2,0},{4,6},{3,1},{5,7},{10,8},{12,14},{11,9},{13,15},{18,16},{20,... | collective-permute-start | bytes 3538952 | tf_op jit(solution)/shard_map/ppermute | solution.py:113
  81.9 29.7 %collective-permute-start.10 = (f32[12,128,128]{2,1,0:T(8,128)S(1)}, f32[12,128,128]{2,1,0:T(8,128)}, u32[]{:S(2)}, u32[]{:S(2)}) collective-permute-start(f32[12,128,128]{2,1,0:T(8,128)S(1)} %slice.100), channel_id=1, source_target_pairs={{2,4},{4,2},{3,5},{5,3},{10,12},{12,10},{11,13},{13,11},{18,20},{2... | collective-permute-start | bytes 2359304 | tf_op jit(solution)/shard_map/ppermute | solution.py:113
  83.5 43.5 %collective-permute-start.11 = (f32[3,128,512]{2,1,0:T(8,128)}, f32[3,128,512]{2,1,0:T(8,128)}, u32[]{:S(2)}, u32[]{:S(2)}) collective-permute-start(f32[3,128,512]{2,1,0:T(8,128)} %get-tuple-element.32), channel_id=1, source_target_pairs={{0,2},{6,4},{1,3},{7,5},{8,10},{14,12},{9,11},{15,13},{16,18},{22,... | collective-permute-start | bytes 2359304 | tf_op jit(solution)/shard_map/ppermute | solution.py:113
  97.0 32.7 %collective-permute-start.16 = (f32[9,128,128]{2,1,0:T(8,128)}, f32[9,128,128]{2,1,0:T(8,128)}, u32[]{:S(2)}, u32[]{:S(2)}) collective-permute-start(f32[9,128,128]{2,1,0:T(8,128)} %get-tuple-element.37.refs_0_), channel_id=1, source_target_pairs={{2,0},{4,6},{3,1},{5,7},{10,8},{12,14},{11,9},{13,15},{18,16},{20,... | collective-permute-start | bytes 1769480 | tf_op jit(solution)/shard_map/ppermute | solution.py:113
  105.4 48.9 %collective-permute-start.15 = (f32[3,128,512]{2,1,0:T(8,128)}, f32[3,128,512]{2,1,0:T(8,128)}, u32[]{:S(2)}, u32[]{:S(2)}) collective-permute-start(f32[3,128,512]{2,1,0:T(8,128)} %get-tuple-element.36), channel_id=1, source_target_pairs={{0,2},{6,4},{1,3},{7,5},{8,10},{14,12},{9,11},{15,13},{16,18},{22,... | collective-permute-start | bytes 2359304 | tf_op jit(solution)/shard_map/ppermute | solution.py:113
  111.7 50.3 %collective-permute-start.19 = (f32[14,128,128]{2,1,0:T(8,128)}, f32[14,128,128]{2,1,0:T(8,128)}, u32[]{:S(2)}, u32[]{:S(2)}) collective-permute-start(f32[14,128,128]{2,1,0:T(8,128)} %collective-permute-done.5.refs_1_), channel_id=1, source_target_pairs={{2,4},{4,2},{3,5},{5,3},{10,12},{12,10},{11,13},{13,11},{18,20},{2... | collective-permute-start | bytes 2752520 | tf_op jit(solution)/shard_map/ppermute | solution.py:113
  127.0 28.6 %collective-permute-start.12 = (f32[6,128,128]{2,1,0:T(8,128)}, f32[6,128,128]{2,1,0:T(8,128)}, u32[]{:S(2)}, u32[]{:S(2)}) collective-permute-start(f32[6,128,128]{2,1,0:T(8,128)} %slice.99), channel_id=1, source_target_pairs={{2,4},{4,2},{3,5},{5,3},{10,12},{12,10},{11,13},{13,11},{18,20},{2... | collective-permute-start | bytes 1179656 | tf_op jit(solution)/shard_map/ppermute | solution.py:113
  128.4 33.5 %collective-permute-start.14 = (f32[9,128,128]{2,1,0:T(8,128)S(1)}, f32[9,128,128]{2,1,0:T(8,128)}, u32[]{:S(2)}, u32[]{:S(2)}) collective-permute-start(f32[9,128,128]{2,1,0:T(8,128)S(1)} %copy-done.8), channel_id=1, source_target_pairs={{2,0},{4,6},{3,1},{5,7},{10,8},{12,14},{11,9},{13,15},{18,16},{20,... | collective-permute-start | bytes 1769480 | tf_op jit(solution)/shard_map/ppermute | solution.py:113
  129.7 40.6 %collective-permute-start.25 = (f32[3,128,512]{2,1,0:T(8,128)}, f32[3,128,512]{2,1,0:T(8,128)S(1)}, u32[]{:S(2)}, u32[]{:S(2)}) collective-permute-start(f32[3,128,512]{2,1,0:T(8,128)} %get-tuple-element.42), channel_id=1, source_target_pairs={{0,2},{6,4},{1,3},{7,5},{8,10},{14,12},{9,11},{15,13},{16,18},{22,... | collective-permute-start | bytes 2359304 | tf_op jit(solution)/shard_map/ppermute | solution.py:113
  154.3 30.2 %collective-permute-start.18 = (f32[12,128,128]{2,1,0:T(8,128)}, f32[12,128,128]{2,1,0:T(8,128)}, u32[]{:S(2)}, u32[]{:S(2)}) collective-permute-start(f32[12,128,128]{2,1,0:T(8,128)} %collective-permute-done.10.refs_0_), channel_id=1, source_target_pairs={{2,0},{4,6},{3,1},{5,7},{10,8},{12,14},{11,9},{13,15},{18,16},{20,... | collective-permute-start | bytes 2359304 | tf_op jit(solution)/shard_map/ppermute | solution.py:113
  155.6 17.2 %collective-permute-start.24 = (f32[2,128,512]{2,1,0:T(8,128)S(1)}, f32[2,128,512]{2,1,0:T(8,128)S(1)}, u32[]{:S(2)}, u32[]{:S(2)}) collective-permute-start(f32[2,128,512]{2,1,0:T(8,128)S(1)} %constant_dynamic-slice_fusion.1), channel_id=1, source_target_pairs={{0,2},{6,4},{1,3},{7,5},{8,10},{14,12},{9,11},{15,13},{16,18},{22,... | collective-permute-start | bytes 1572872 | tf_op jit(solution)/shard_map/ppermute | solution.py:113
  162.0 13.1 %collective-permute-start.8 = (f32[3,64,512]{2,1,0:T(8,128)}, f32[3,64,512]{2,1,0:T(8,128)}, u32[]{:S(2)}, u32[]{:S(2)}) collective-permute-start(f32[3,64,512]{2,1,0:T(8,128)} %dynamic-slice_bitcast_fusion.1), channel_id=1, source_target_pairs={{0,1},{1,0},{2,3},{3,2},{4,5},{5,4},{6,7},{7,6},{8,9},{9,8},{10,11... | collective-permute-start | bytes 1179656 | tf_op jit(solution)/shard_map/ppermute | solution.py:239
  162.0 25.5 %collective-permute-start.17 = (f32[6,128,128]{2,1,0:T(8,128)}, f32[6,128,128]{2,1,0:T(8,128)}, u32[]{:S(2)}, u32[]{:S(2)}) collective-permute-start(f32[6,128,128]{2,1,0:T(8,128)} %collective-permute-done.12.refs_0_), channel_id=1, source_target_pairs={{2,0},{4,6},{3,1},{5,7},{10,8},{12,14},{11,9},{13,15},{18,16},{20,... | collective-permute-start | bytes 1179656 | tf_op jit(solution)/shard_map/ppermute | solution.py:113
  175.1 15.2 %collective-permute-start.26 = (f32[3,64,512]{2,1,0:T(8,128)}, f32[3,64,512]{2,1,0:T(8,128)}, u32[]{:S(2)}, u32[]{:S(2)}) collective-permute-start(f32[3,64,512]{2,1,0:T(8,128)} %dynamic-slice_bitcast_fusion), channel_id=1, source_target_pairs={{0,1},{1,0},{2,3},{3,2},{4,5},{5,4},{6,7},{7,6},{8,9},{9,8},{10,11... | collective-permute-start | bytes 1179656 | tf_op jit(solution)/shard_map/ppermute | solution.py:239
  189.7 5.3 %collective-permute-start.20 = (f32[1,64,512]{2,1,0:T(8,128)S(1)}, f32[1,64,512]{2,1,0:T(8,128)S(1)}, u32[]{:S(2)}, u32[]{:S(2)}) collective-permute-start(f32[1,64,512]{2,1,0:T(8,128)S(1)} %dynamic-slice_bitcast_fusion.2), channel_id=1, source_target_pairs={{0,1},{1,0},{2,3},{3,2},{4,5},{5,4},{6,7},{7,6},{8,9},{9,8},{10,11... | collective-permute-start | bytes 393224 | tf_op jit(solution)/shard_map/ppermute | solution.py:239
  191.4 6.8 %collective-permute-start.27 = (f32[64,512]{1,0:T(8,128)S(1)}, f32[64,512]{1,0:T(8,128)S(1)}, u32[]{:S(2)}, u32[]{:S(2)}) collective-permute-start(f32[64,512]{1,0:T(8,128)S(1)} %get-tuple-element.64), channel_id=1, source_target_pairs={{0,8},{8,0},{16,24},{24,16},{1,9},{9,1},{17,25},{25,17},{2,10},{10... | collective-permute-start | bytes 393224 | tf_op jit(solution)/shard_map/ppermute | solution.py:251
  193.0 8.5 %collective-permute-start.28 = (f32[64,512]{1,0:T(8,128)S(1)}, f32[64,512]{1,0:T(8,128)S(1)}, u32[]{:S(2)}, u32[]{:S(2)}) collective-permute-start(f32[64,512]{1,0:T(8,128)S(1)} %get-tuple-element.65), channel_id=1, source_target_pairs={{0,16},{8,24},{16,0},{24,8},{1,17},{9,25},{17,1},{25,9},{2,18},{10... | collective-permute-start | bytes 393224 | tf_op jit(solution)/shard_map/ppermute | solution.py:251
  194.5 7.4 %collective-permute-start.29 = (f32[64,512]{1,0:T(8,128)S(1)}, f32[64,512]{1,0:T(8,128)S(1)}, u32[]{:S(2)}, u32[]{:S(2)}) collective-permute-start(f32[64,512]{1,0:T(8,128)S(1)} %get-tuple-element.66), channel_id=1, source_target_pairs={{0,24},{8,16},{16,8},{24,0},{1,25},{9,17},{17,9},{25,1},{2,26},{10... | collective-permute-start | bytes 393224 | tf_op jit(solution)/shard_map/ppermute | solution.py:251
  195.1 8.6 %collective-permute-start.21 = (f32[64,512]{1,0:T(8,128)S(1)}, f32[64,512]{1,0:T(8,128)S(1)}, u32[]{:S(2)}, u32[]{:S(2)}) collective-permute-start(f32[64,512]{1,0:T(8,128)S(1)} %get-tuple-element.61), channel_id=1, source_target_pairs={{0,8},{8,0},{16,24},{24,16},{1,9},{9,1},{17,25},{25,17},{2,10},{10... | collective-permute-start | bytes 393224 | tf_op jit(solution)/shard_map/ppermute | solution.py:251
  196.7 9.9 %collective-permute-start.22 = (f32[64,512]{1,0:T(8,128)S(1)}, f32[64,512]{1,0:T(8,128)S(1)}, u32[]{:S(2)}, u32[]{:S(2)}) collective-permute-start(f32[64,512]{1,0:T(8,128)S(1)} %get-tuple-element.62), channel_id=1, source_target_pairs={{0,16},{8,24},{16,0},{24,8},{1,17},{9,25},{17,1},{25,9},{2,18},{10... | collective-permute-start | bytes 393224 | tf_op jit(solution)/shard_map/ppermute | solution.py:251
  198.2 8.3 %collective-permute-start.23 = (f32[64,512]{1,0:T(8,128)S(1)}, f32[64,512]{1,0:T(8,128)S(1)}, u32[]{:S(2)}, u32[]{:S(2)}) collective-permute-start(f32[64,512]{1,0:T(8,128)S(1)} %get-tuple-element.63), channel_id=1, source_target_pairs={{0,24},{8,16},{16,8},{24,0},{1,25},{9,17},{17,9},{25,1},{2,26},{10... | collective-permute-start | bytes 393224 | tf_op jit(solution)/shard_map/ppermute | solution.py:251
  201.9 6.9 %collective-permute-start.30 = (f32[64,512]{1,0:T(8,128)S(1)}, f32[64,512]{1,0:T(8,128)S(1)}, u32[]{:S(2)}, u32[]{:S(2)}) collective-permute-start(f32[64,512]{1,0:T(8,128)S(1)} %fusion.3), channel_id=1, source_target_pairs={{2,0},{4,6},{3,1},{5,7},{10,8},{12,14},{11,9},{13,15},{18,16},{20,... | collective-permute-start | bytes 393224 | tf_op jit(solution)/shard_map/ppermute | solution.py:113
  (13 other events, 41.2 us)
